TPU v7x, 256 devices: a whole 4x4x8 slice. The times are simulated.
256 devices in a mesh: rep: 4 (over z_hi), section: 4 (over z_lo, core), tp: 16 (over y, x).
Axes of the slice: x: 4, y: 4, z: 8 (z_hi: 4, z_lo: 2; z = z_hi * 2 + z_lo), core: 2. Of those that a mesh axis runs over, the one named last changes fastest.
Arguments:
- layer_section: int32 [4, 6], replicated, may hold values from 0 to 3, as said below
- token_count: int32 [4], replicated, may hold values from 1 to 1536, 3840 in all
- window_size: int32 [6], replicated, may hold values from 192 to 768, as said below
- normed_input: bfloat16 [4, 4, 2, 1536, 6144], P('rep', 'section', None, None, 'tp'), may hold values from -6 to 6
- queries: bfloat16 [4, 4, 2, 1536, 4096], P('rep', 'section', None, None, 'tp'), may hold values from -6 to 6
- key_rows: bfloat16 [4, 4, 2, 1536, 512], P('rep', 'section'), may hold values from -6 to 6
- out_grad: bfloat16 [4, 4, 2, 1536, 4096], P('rep', 'section', None, None, 'tp'), may hold values from -6 to 6
- master: float32 [6, 16, 384, 512], P(None, 'tp', ('rep', 'section')), may hold values from -6 to 6
- moment_one: float32 [6, 16, 384, 512], P(None, 'tp', ('rep', 'section')), may hold values from -12 to 12
- moment_two: float32 [6, 16, 384, 512], P(None, 'tp', ('rep', 'section')), may hold values from 1 to 20
Outputs:
- new_master: float32 [6, 16, 384, 512], P(None, 'tp', ('rep', 'section'))
- new_moment_one: float32 [6, 16, 384, 512], P(None, 'tp', ('rep', 'section'))
- new_moment_two: float32 [6, 16, 384, 512], P(None, 'tp', ('rep', 'section'))
- compute_weights: bfloat16 [4, 4, 2, 6144, 512], P('rep', 'section', None, 'tp')
Inputs may be any that keep to these rules, and one draw needn't show every extreme that they name: layer_section[r, l] never falls as l grows, and every section of every replica holds 1 or 2 layers. Rows from token_count[r] on are padding; the largest count is exactly 1536. `window_size`: query i sees keys i - w + 1 to i; one layer has exactly 768 and one exactly 192.
All inputs are finite; a program needn't handle non-finite values.
Results may differ from a plain program's by a relative error of at most 0.02.
Values may be sent and summed in bfloat16 or wider, within the bound.
No kernel may reach another device: no remote copies, remote signals or barrier semaphores. Data moves between devices by JAX's collectives and lax.ppermute only.
A program may use at most 128 MiB of HBM per device.

v0:
```python
import functools

import jax
import jax.numpy as jnp
from jax import lax
from jax.experimental import pallas as pl
from jax.experimental.pallas import tpu as pltpu
from jax.sharding import Mesh, PartitionSpec as P

HQ = 32
KVH = 4
HD = 128
BETA_ONE = 0.9
BETA_TWO = 0.95
LEARN_RATE = 0.03
DECAY_RATE = 0.1
EPSILON = 1e-08
CORRECT_ONE = 0.9999734386011124
CORRECT_TWO = 0.994079470779667
LOG2E = 1.4426950408889634
TQ = 256
SECTIONS = 4
BF = jnp.bfloat16
F32 = jnp.float32


def first_and_count(map_ref, replica, section, layers):
    first = jnp.int32(0)
    count = jnp.int32(0)
    for l in range(layers):
        at = map_ref[replica, l]
        first += (at < section).astype(jnp.int32)
        count += (at == section).astype(jnp.int32)
    return first, count


def attention_kernel(slot, layers, tokens, per_dev, ids, lmap, counts, windows,
                     q_ref, k_ref, g_ref, *rest):
    outs = rest[:4]
    acc, p_scr, g_scr = rest[4:]
    step = pl.program_id(0)
    steps = pl.num_programs(0)
    replica, section, x_id = ids[0], ids[1], ids[3]
    first, held = first_and_count(lmap, replica, section, layers)
    layer = jnp.minimum(first + slot, layers - 1)
    window = windows[layer]
    length = jnp.where(slot < held, counts[replica], 0)
    reach = tokens // 2 // TQ
    row0 = step * TQ

    @pl.when(step == 0)
    def _():
        acc[...] = jnp.zeros_like(acc)

    def work(chunks):
        base = pl.multiple_of((step - (chunks - 1)) * TQ, TQ)
        keys = k_ref[pl.ds(base, chunks * TQ), :]
        q_col = lax.broadcasted_iota(jnp.int32, (TQ, TQ), 1)
        k_row = lax.broadcasted_iota(jnp.int32, (TQ, TQ), 0)
        diff = q_col - k_row
        live = (row0 + lax.broadcasted_iota(jnp.int32, (TQ, HD), 0)) < length
        scale = HD ** (-0.5) * LOG2E
        for h in range(per_dev):
            query = q_ref[:, h * HD:(h + 1) * HD]
            parts = []
            peak = None
            for c in range(chunks):
                s = lax.dot_general(
                    keys[c * TQ:(c + 1) * TQ], query, (((1,), (1,)), ((), ())),
                    preferred_element_type=F32)
                off = (chunks - 1 - c) * TQ
                ok = diff < (window - off)
                if c == chunks - 1:
                    ok = ok & (diff >= 0)
                s = jnp.where(ok, s, -1e30)
                parts.append(s)
                m = jnp.max(s, axis=0, keepdims=True)
                peak = m if peak is None else jnp.maximum(peak, m)
            shift = peak * scale
            total = None
            for c in range(chunks):
                e = jnp.exp2(parts[c] * scale - shift)
                t = jnp.sum(e, axis=0, keepdims=True)
                total = t if total is None else total + t
                p_scr[c * TQ:(c + 1) * TQ, h * TQ:(h + 1) * TQ] = e.astype(BF)
            inverse = jnp.broadcast_to(1.0 / total, (HD, TQ)).T
            grad = g_ref[:, h * HD:(h + 1) * HD].astype(F32) * inverse
            g_scr[h * TQ:(h + 1) * TQ, :] = jnp.where(live, grad, 0.0).astype(BF)
        for c in range(chunks):
            rows = pl.ds(base + c * TQ, TQ)
            acc[rows, :] += jnp.dot(
                p_scr[c * TQ:(c + 1) * TQ, :], g_scr[...], preferred_element_type=F32)

    wanted = jnp.minimum(step, (window + TQ - 2) // TQ) + 1
    for chunks in range(1, reach + 2):
        @pl.when((row0 < length) & (wanted == chunks))
        def _(chunks=chunks):
            work(chunks)

    @pl.when(step == steps - 1)
    def _():
        part = tokens // 4
        for k in range(4):
            at = pl.multiple_of(lax.rem(x_id + k, 4) * part, part)
            outs[k][...] = acc[pl.ds(at, part), :].astype(BF)


def attention(slot, scalars, queries, key_rows, out_grad, layers):
    tokens = queries.shape[3]
    per_dev = queries.shape[4] // HD
    steps = tokens // TQ
    part = tokens // 4
    wide = per_dev * HD
    row_block = pl.BlockSpec((None, None, None, TQ, wide), lambda i, *_: (0, 0, slot, i, 0))
    key_block = pl.BlockSpec(
        (None, None, None, tokens, HD), lambda i, ids, *_: (0, 0, slot, 0, ids[2]))
    out_block = pl.BlockSpec((part, HD), lambda i, *_: (0, 0))
    return pl.pallas_call(
        functools.partial(attention_kernel, slot, layers, tokens, per_dev),
        grid_spec=pltpu.PrefetchScalarGridSpec(
            num_scalar_prefetch=4,
            grid=(steps,),
            in_specs=[row_block, key_block, row_block],
            out_specs=[out_block] * 4,
            scratch_shapes=[
                pltpu.VMEM((tokens, HD), F32),
                pltpu.VMEM((tokens // 2 + TQ, per_dev * TQ), BF),
                pltpu.VMEM((per_dev * TQ, HD), BF),
            ],
        ),
        out_shape=[jax.ShapeDtypeStruct((part, HD), BF)] * 4,
        compiler_params=pltpu.CompilerParams(vmem_limit_bytes=40 << 20),
        cost_estimate=pl.CostEstimate(
            flops=18 * per_dev * 4 * TQ * TQ * HD, bytes_accessed=2 << 20,
            transcendentals=18 * per_dev * TQ * TQ),
        name="attn%d" % slot,
    )(*scalars, queries, key_rows, out_grad)


def grad_kernel(tokens, ids, x_ref, *refs):
    own_p, px, own_q, qy, py, qx = refs[0], refs[1:4], refs[4], refs[5:8], refs[8:11], refs[11:14]
    out_ref, value = refs[14], refs[15]
    y_id, x_id = ids[2], ids[3]
    part = tokens // 4
    half = part // 2

    def put(block, y, x, second):
        y = lax.rem(y_id + 4 - y, 4)
        x = lax.rem(x_id + 4 - x, 4)
        at = pl.multiple_of(x * part + second * half, half)
        col = pl.multiple_of(y * HD, HD)
        value[pl.ds(at, half), pl.ds(col, HD)] = block

    put(own_p[...], 0, 0, 0)
    put(own_q[...], 0, 0, 1)
    for k in range(1, 4):
        put(px[k - 1][...], 0, k, 0)
        put(qy[k - 1][...], k, 0, 1)
        for i in range(4):
            put(py[k - 1][i], k, i, 0)
            put(qx[k - 1][i], i, k, 1)
    out_ref[...] = lax.dot_general(
        x_ref[...], value[...], (((0,), (0,)), ((), ())),
        preferred_element_type=F32).astype(BF)


def layer_grad(slot, scalars, normed, pieces):
    tokens, width = normed.shape[3], normed.shape[4]
    whole = pl.BlockSpec(memory_space=pltpu.VMEM)
    return pl.pallas_call(
        functools.partial(grad_kernel, tokens),
        grid_spec=pltpu.PrefetchScalarGridSpec(
            num_scalar_prefetch=1,
            grid=(1,),
            in_specs=[pl.BlockSpec((None, None, None, tokens, width),
                                   lambda i, *_: (0, 0, slot, 0, 0))] + [
                pl.BlockSpec(p.shape, lambda i, *_, n=p.ndim: (0,) * n) for p in pieces],
            out_specs=pl.BlockSpec((width, KVH * HD), lambda i, *_: (0, 0)),
            scratch_shapes=[pltpu.VMEM((tokens, KVH * HD), BF)],
        ),
        out_shape=jax.ShapeDtypeStruct((width, KVH * HD), BF),
        compiler_params=pltpu.CompilerParams(vmem_limit_bytes=40 << 20),
        cost_estimate=pl.CostEstimate(
            flops=2 * tokens * width * KVH * HD, bytes_accessed=3 << 20, transcendentals=0),
        name="grad%d" % slot,
    )(scalars[0], normed, *pieces)


def adam_kernel(reps, layers, lmap, first_ref, second_ref, master, one, two,
                new_master, new_one, new_two, send):
    layer = pl.program_id(0)

    @pl.when(layer == 0)
    def _():
        send[...] = jnp.zeros_like(send)

    total = None
    places = []
    for r in range(reps):
        section = lmap[r, layer]
        first, _ = first_and_count(lmap, r, section, layers)
        slot = layer - first
        source = r * SECTIONS + section
        places.append((source, slot))
        term = jnp.where(slot == 0, first_ref[source].astype(F32), second_ref[source].astype(F32))
        total = term if total is None else total + term
    mean = total / reps
    m1 = BETA_ONE * one[...] + (1.0 - BETA_ONE) * mean
    m2 = BETA_TWO * two[...] + (1.0 - BETA_TWO) * mean * mean
    move = m1 / CORRECT_ONE / (jnp.sqrt(m2 / CORRECT_TWO) + EPSILON)
    updated = master[...] - LEARN_RATE * (move + DECAY_RATE * master[...])
    new_master[...] = updated
    new_one[...] = m1
    new_two[...] = m2
    rounded = updated.astype(BF)
    for source, slot in places:
        send[source, slot] = rounded


def adam(lmap, received, master, one, two):
    layers, _, rows, wide = master.shape
    group = received[0].shape[0]
    slots = 2
    state = pl.BlockSpec((None, None, rows, wide), lambda l, *_: (l, 0, 0, 0))
    whole = pl.BlockSpec((group, rows, wide), lambda l, *_: (0, 0, 0))
    f32 = jax.ShapeDtypeStruct(master.shape, F32)
    return pl.pallas_call(
        functools.partial(adam_kernel, lmap.shape[0], layers),
        grid_spec=pltpu.PrefetchScalarGridSpec(
            num_scalar_prefetch=1,
            grid=(layers,),
            in_specs=[whole, whole, state, state, state],
            out_specs=[state, state, state,
                       pl.BlockSpec((group, slots, rows, wide), lambda l, *_: (0, 0, 0, 0))],
        ),
        out_shape=[f32, f32, f32, jax.ShapeDtypeStruct((group, slots, rows, wide), BF)],
        compiler_params=pltpu.CompilerParams(vmem_limit_bytes=40 << 20),
        cost_estimate=pl.CostEstimate(flops=20 * master.size, bytes_accessed=4 << 20,
                                      transcendentals=master.size),
        name="adamw",
    )(lmap, *received, master, one, two)


def shift(value, axis, by):
    n = lax.axis_size(axis)
    return lax.ppermute(value, axis, [(i, (i + by) % n) for i in range(n)])


def gather_pieces(block):
    half = block.shape[0] // 2
    p, q = block[:half], block[half:]
    px = [shift(p, "x", k) for k in range(1, 4)]
    qy = [shift(q, "y", k) for k in range(1, 4)]
    p_row = jnp.stack([p] + px)
    q_col = jnp.stack([q] + qy)
    py = [shift(p_row, "y", k) for k in range(1, 4)]
    qx = [shift(q_col, "x", k) for k in range(1, 4)]
    return [p] + px + [q] + qy + py + qx


def body(layer_section, token_count, window_size, normed_input, queries, key_rows, out_grad,
         master, moment_one, moment_two):
    layers = layer_section.shape[1]
    group_axes = ("rep", "z", "core")
    ids = jnp.stack([
        lax.axis_index("rep"), lax.axis_index(("z", "core")),
        lax.axis_index("y"), lax.axis_index("x")]).astype(jnp.int32)
    scalars = (ids, layer_section, token_count, window_size)
    rows = master.shape[2]
    received = []
    for slot in range(2):
        parts = attention(slot, scalars, queries, key_rows, out_grad, layers)
        total = parts[0].astype(F32)
        for k in range(1, 4):
            total = total + shift(parts[k], "x", k).astype(F32)
        pieces = gather_pieces(total.astype(BF))
        grad = layer_grad(slot, scalars, normed_input, pieces)
        grad = grad.reshape(-1, rows, grad.shape[1])
        received.append(lax.all_to_all(grad, group_axes, 0, 0, tiled=True))
    updated, first, second, send = adam(layer_section, received, master, moment_one, moment_two)
    arrived = lax.all_to_all(send, group_axes, 0, 0, tiled=True)
    own = jnp.transpose(arrived, (1, 0, 2, 3)).reshape(2, -1, arrived.shape[3])
    return updated, first, second, own[None, None]


def solution(mesh):
    reps, sections, tps = mesh.devices.shape
    fine = Mesh(mesh.devices.reshape(reps, 2, sections // 2, 4, tps // 4),
                ("rep", "z", "core", "y", "x"))
    section, tp = ("z", "core"), ("y", "x")
    wide = P("rep", section, None, None, tp)
    state = P(None, tp, ("rep",) + section, None)
    in_specs = (P(), P(), P(), wide, wide, P("rep", section, None, None, None), wide,
                state, state, state)
    out_specs = (state, state, state, P("rep", section, None, tp, None))
    return jax.shard_map(body, mesh=fine, in_specs=in_specs, out_specs=out_specs, check_vma=False)
```

profile of v0, /device:TPU:1, one launch (start us, length us, event | category | flops | bytes accessed | tf_op | source)
XLA Modules:
  0.0 163.0 jit_solution(1004406926191259482)
XLA Ops:
  0.7 1.9 %copy-done = bf16[1,1,2,1536,512]{4,3,2,1,0:T(8,128)(2,1)S(1)} copy-done((bf16[1,1,2,1536,512]{4,3,2,1,0:T(8,128)(2,1)S(1)}, bf16[1,1,2,1536,512]{4,3,2,1,0:T(8,128)(2,1)}, u32[]{:S(2)}) %copy-start) | copy-done | bytes 3145752
  8.7 2.1 %collective-permute-start.15 = (bf16[384,128]{1,0:T(8,128)(2,1)S(1)}, bf16[384,128]{1,0:T(8,128)(2,1)S(1)}, u32[]{:S(2)}, u32[]{:S(2)}) collective-permute-start(bf16[384,128]{1,0:T(8,128)(2,1)S(1)} %get-tuple-element.21), channel_id=1, source_target_pairs={{0,1},{1,2},{2,3},{3,0},{4,5},{5,6},{6,7},{7,4},{8,9},{9,10},{10,1... | collective-permute-start | bytes 294920 | tf_op jit(solution)/shard_map/ppermute | solution.py:246
  10.8 2.5 %collective-permute-start.16 = (bf16[384,128]{1,0:T(8,128)(2,1)S(1)}, bf16[384,128]{1,0:T(8,128)(2,1)S(1)}, u32[]{:S(2)}, u32[]{:S(2)}) collective-permute-start(bf16[384,128]{1,0:T(8,128)(2,1)S(1)} %get-tuple-element.22), channel_id=1, source_target_pairs={{0,2},{1,3},{2,0},{3,1},{4,6},{5,7},{6,4},{7,5},{8,10},{9,11},{10,... | collective-permute-start | bytes 294920 | tf_op jit(solution)/shard_map/ppermute | solution.py:246
  14.4 2.9 %collective-permute-done.16 = bf16[384,128]{1,0:T(8,128)(2,1)S(1)} collective-permute-done((bf16[384,128]{1,0:T(8,128)(2,1)S(1)}, bf16[384,128]{1,0:T(8,128)(2,1)S(1)}, u32[]{:S(2)}, u32[]{:S(2)}) %collective-permute-start.16) | collective-permute-done | bytes 98336 | tf_op jit(solution)/shard_map/ppermute | solution.py:246
  17.4 2.9 %collective-permute-start.23 = (bf16[192,128]{1,0:T(8,128)(2,1)S(1)}, bf16[192,128]{1,0:T(8,128)(2,1)S(1)}, u32[]{:S(2)}, u32[]{:S(2)}) collective-permute-start(bf16[192,128]{1,0:T(8,128)(2,1)S(1)} %get-tuple-element.30.refs_4_), channel_id=1, source_target_pairs={{0,12},{4,0},{8,4},{12,8},{1,13},{5,1},{9,5},{13,9},{2,14},{6,2},{... | collective-permute-start | bytes 147464 | tf_op jit(solution)/shard_map/ppermute | solution.py:246
  21.3 2.4 %collective-permute-start.20 = (bf16[192,128]{1,0:T(8,128)(2,1)S(1)}, bf16[192,128]{1,0:T(8,128)(2,1)S(1)}, u32[]{:S(2)}, u32[]{:S(2)}) collective-permute-start(bf16[192,128]{1,0:T(8,128)(2,1)S(1)} %get-tuple-element.31.refs_0_), channel_id=1, source_target_pairs={{0,3},{1,0},{2,1},{3,2},{4,7},{5,4},{6,5},{7,6},{8,11},{9,8},{10,9... | collective-permute-start | bytes 147464 | tf_op jit(solution)/shard_map/ppermute | solution.py:246
  25.3 2.7 %collective-permute-start.29 = (bf16[4,192,128]{2,1,0:T(8,128)(2,1)S(1)}, bf16[4,192,128]{2,1,0:T(8,128)(2,1)S(1)}, u32[]{:S(2)}, u32[]{:S(2)}) collective-permute-start(bf16[4,192,128]{2,1,0:T(8,128)(2,1)S(1)} %pad_maximum_fusion.3), channel_id=1, source_target_pairs={{0,3},{1,0},{2,1},{3,2},{4,7},{5,4},{6,5},{7,6},{8,11},{9,8},{10,9... | collective-permute-start | bytes 589832 | tf_op jit(solution)/shard_map/ppermute | solution.py:246
  27.9 2.9 %attn0.1 = (bf16[384,128]{1,0:T(8,128)(2,1)S(1)}, bf16[384,128]{1,0:T(8,128)(2,1)S(1)}, bf16[384,128]{1,0:T(8,128)(2,1)S(1)}, bf16[384,128]{1,0:T(8,128)(2,1)S(1)}) custom-call(s32[4]{0:T(128)S(1)} %pad_add_fusion.ids, s32[4,6]{1,0:T(4,128)S(1)} %copy-done.7, s32[4]{0:T(128)S(1)} %copy-done.9, s32[6]{0:T(128)S(1)} %copy-done.10, ...), custom_call_target="tpu_custom_call" | custom-call | flops 1207959552 | bytes 2097152 | tf_op jit(solution)/shard_map/attn0/pallas_call | solution.py:118
  33.6 2.3 %collective-permute-start.28 = (bf16[4,192,128]{2,1,0:T(8,128)(2,1)S(1)}, bf16[4,192,128]{2,1,0:T(8,128)(2,1)S(1)}, u32[]{:S(2)}, u32[]{:S(2)}) collective-permute-start(bf16[4,192,128]{2,1,0:T(8,128)(2,1)S(1)} %pad_maximum_fusion.3), channel_id=1, source_target_pairs={{0,2},{1,3},{2,0},{3,1},{4,6},{5,7},{6,4},{7,5},{8,10},{9,11},{10,... | collective-permute-start | bytes 589832 | tf_op jit(solution)/shard_map/ppermute | solution.py:246
  37.5 2.4 %collective-permute-start.25 = (bf16[4,192,128]{2,1,0:T(8,128)(2,1)S(1)}, bf16[4,192,128]{2,1,0:T(8,128)(2,1)S(1)}, u32[]{:S(2)}, u32[]{:S(2)}) collective-permute-start(bf16[4,192,128]{2,1,0:T(8,128)(2,1)S(1)} %pad_maximum_fusion.2), channel_id=1, source_target_pairs={{0,8},{4,12},{8,0},{12,4},{1,9},{5,13},{9,1},{13,5},{2,10},{6,14},... | collective-permute-start | bytes 589832 | tf_op jit(solution)/shard_map/ppermute | solution.py:246
  41.5 4.9 %collective-permute-done.27.refs_11_ = bf16[4,192,128]{2,1,0:T(8,128)(2,1)S(1)} collective-permute-done((bf16[4,192,128]{2,1,0:T(8,128)(2,1)S(1)}, bf16[4,192,128]{2,1,0:T(8,128)(2,1)S(1)}, u32[]{:S(2)}, u32[]{:S(2)}) %collective-permute-start.27) | collective-permute-done | bytes 196640 | tf_op jit(solution)/shard_map/ppermute | solution.py:246
  46.4 2.4 %grad1.1 = bf16[384,512]{1,0:T(8,128)(2,1)} custom-call(s32[4]{0:T(128)S(1)} %pad_add_fusion.ids, bf16[1,1,2,1536,384]{4,3,2,1,0:T(8,128)(2,1)S(1)} %copy-done.1, bf16[192,128]{1,0:T(8,128)(2,1)S(1)} %get-tuple-element.31.refs_0_, bf16[192,128]{1,0:T(8,128)(2,1)S(1)} %collective-permute-done.18.refs_1_, ...), custom_call_target="tpu_custom_call" | custom-call | flops 603979776 | bytes 3145728 | tf_op jit(solution)/shard_map/grad1/pallas_call | solution.py:170
  48.8 28.5 %all-to-all-start.1 = ((bf16[16,24,512]{2,1,0:T(8,128)(2,1)}), bf16[16,24,512]{2,1,0:T(8,128)(2,1)S(1)}, u32[]{:S(2)}, u32[]{:S(2)}) async-start(bf16[16,24,512]{2,1,0:T(8,128)(2,1)} %bitcast.21), calls=%async_computation.1 | async-start | bytes 786432 | tf_op jit(solution)/shard_map/all_to_all | solution.py:279
  77.7 1.4 collective-permute-start.7
  80.4 1.8 %collective-permute-done.7.refs_6_ = bf16[192,128]{1,0:T(8,128)(2,1)S(1)} collective-permute-done((bf16[192,128]{1,0:T(8,128)(2,1)S(1)}, bf16[192,128]{1,0:T(8,128)(2,1)S(1)}, u32[]{:S(2)}, u32[]{:S(2)}) %collective-permute-start.7) | collective-permute-done | bytes 49184 | tf_op jit(solution)/shard_map/ppermute | solution.py:246
  82.2 1.5 collective-permute-done.6.refs_5_
  83.7 3.0 %collective-permute-start.14 = (bf16[4,192,128]{2,1,0:T(8,128)(2,1)S(1)}, bf16[4,192,128]{2,1,0:T(8,128)(2,1)S(1)}, u32[]{:S(2)}, u32[]{:S(2)}) collective-permute-start(bf16[4,192,128]{2,1,0:T(8,128)(2,1)S(1)} %pad_maximum_fusion.1), channel_id=1, source_target_pairs={{0,3},{1,0},{2,1},{3,2},{4,7},{5,4},{6,5},{7,6},{8,11},{9,8},{10,9... | collective-permute-start | bytes 589832 | tf_op jit(solution)/shard_map/ppermute | solution.py:246
  88.2 3.6 %collective-permute-start.13 = (bf16[4,192,128]{2,1,0:T(8,128)(2,1)S(1)}, bf16[4,192,128]{2,1,0:T(8,128)(2,1)S(1)}, u32[]{:S(2)}, u32[]{:S(2)}) collective-permute-start(bf16[4,192,128]{2,1,0:T(8,128)(2,1)S(1)} %pad_maximum_fusion.1), channel_id=1, source_target_pairs={{0,2},{1,3},{2,0},{3,1},{4,6},{5,7},{6,4},{7,5},{8,10},{9,11},{10,... | collective-permute-start | bytes 589832 | tf_op jit(solution)/shard_map/ppermute | solution.py:246
  94.4 1.8 %collective-permute-done.13.refs_12_ = bf16[4,192,128]{2,1,0:T(8,128)(2,1)S(1)} collective-permute-done((bf16[4,192,128]{2,1,0:T(8,128)(2,1)S(1)}, bf16[4,192,128]{2,1,0:T(8,128)(2,1)S(1)}, u32[]{:S(2)}, u32[]{:S(2)}) %collective-permute-start.13) | collective-permute-done | bytes 196640 | tf_op jit(solution)/shard_map/ppermute | solution.py:246
  96.2 4.5 %collective-permute-done.12.refs_11_ = bf16[4,192,128]{2,1,0:T(8,128)(2,1)S(1)} collective-permute-done((bf16[4,192,128]{2,1,0:T(8,128)(2,1)S(1)}, bf16[4,192,128]{2,1,0:T(8,128)(2,1)S(1)}, u32[]{:S(2)}, u32[]{:S(2)}) %collective-permute-start.12) | collective-permute-done | bytes 196640 | tf_op jit(solution)/shard_map/ppermute | solution.py:246
  101.2 1.6 grad0.1
  102.8 28.8 %all_to_all.15.first_ref = bf16[16,24,512]{2,1,0:T(8,128)(2,1)S(1)} all-to-all(bf16[16,24,512]{2,1,0:T(8,128)(2,1)S(1)} %bitcast.28), channel_id=1, replica_groups=mesh['rep'=4,'z'=2,'core'=2,'y'=4,'x'=4] {'rep','z','core'}, dimensions={0} | all-to-all | bytes 786432 | tf_op jit(solution)/shard_map/all_to_all | solution.py:279
  133.5 3.0 %adamw.1 = (f32[6,1,24,512]{3,2,1,0:T(8,128)}, f32[6,1,24,512]{3,2,1,0:T(8,128)}, f32[6,1,24,512]{3,2,1,0:T(8,128)}, bf16[16,2,24,512]{3,2,1,0:T(8,128)(2,1)S(1)}) custom-call(s32[4,6]{1,0:T(4,128)S(1)} %copy-done.8, bf16[16,24,512]{2,1,0:T(8,128)(2,1)S(1)} %all_to_all.15.first_ref, bf16[16,24,512]{2,1,0:T(8,128)(2,1)S(1)} %all-to-all-done.1.second_ref, ...), custom_call_target="tpu_custom_call" | custom-call | flops 1474560 | bytes 4194304 | tf_op jit(solution)/shard_map/adamw/pallas_call | solution.py:227
  136.5 25.6 %all_to_all.16 = bf16[16,2,24,512]{3,2,1,0:T(8,128)(2,1)S(1)} all-to-all(bf16[16,2,24,512]{3,2,1,0:T(8,128)(2,1)S(1)} %get-tuple-element.27), channel_id=1, replica_groups=mesh['rep'=4,'z'=2,'core'=2,'y'=4,'x'=4] {'rep','z','core'}, dimensions={0} | all-to-all | bytes 1572864 | tf_op jit(solution)/shard_map/all_to_all | solution.py:281
  (77 shorter events, 25.2 us)
Async XLA Ops:
  8.7 5.7 %collective-permute-start.15 = (bf16[384,128]{1,0:T(8,128)(2,1)S(1)}, bf16[384,128]{1,0:T(8,128)(2,1)S(1)}, u32[]{:S(2)}, u32[]{:S(2)}) collective-permute-start(bf16[384,128]{1,0:T(8,128)(2,1)S(1)} %get-tuple-element.21), channel_id=1, source_target_pairs={{0,1},{1,2},{2,3},{3,0},{4,5},{5,6},{6,7},{7,4},{8,9},{9,10},{10,1... | collective-permute-start | bytes 294920 | tf_op jit(solution)/shard_map/ppermute | solution.py:246
  10.8 6.5 %collective-permute-start.16 = (bf16[384,128]{1,0:T(8,128)(2,1)S(1)}, bf16[384,128]{1,0:T(8,128)(2,1)S(1)}, u32[]{:S(2)}, u32[]{:S(2)}) collective-permute-start(bf16[384,128]{1,0:T(8,128)(2,1)S(1)} %get-tuple-element.22), channel_id=1, source_target_pairs={{0,2},{1,3},{2,0},{3,1},{4,6},{5,7},{6,4},{7,5},{8,10},{9,11},{10,... | collective-permute-start | bytes 294920 | tf_op jit(solution)/shard_map/ppermute | solution.py:246
  17.4 6.4 %collective-permute-start.23 = (bf16[192,128]{1,0:T(8,128)(2,1)S(1)}, bf16[192,128]{1,0:T(8,128)(2,1)S(1)}, u32[]{:S(2)}, u32[]{:S(2)}) collective-permute-start(bf16[192,128]{1,0:T(8,128)(2,1)S(1)} %get-tuple-element.30.refs_4_), channel_id=1, source_target_pairs={{0,12},{4,0},{8,4},{12,8},{1,13},{5,1},{9,5},{13,9},{2,14},{6,2},{... | collective-permute-start | bytes 147464 | tf_op jit(solution)/shard_map/ppermute | solution.py:246
  21.3 9.6 %collective-permute-start.20 = (bf16[192,128]{1,0:T(8,128)(2,1)S(1)}, bf16[192,128]{1,0:T(8,128)(2,1)S(1)}, u32[]{:S(2)}, u32[]{:S(2)}) collective-permute-start(bf16[192,128]{1,0:T(8,128)(2,1)S(1)} %get-tuple-element.31.refs_0_), channel_id=1, source_target_pairs={{0,3},{1,0},{2,1},{3,2},{4,7},{5,4},{6,5},{7,6},{8,11},{9,8},{10,9... | collective-permute-start | bytes 147464 | tf_op jit(solution)/shard_map/ppermute | solution.py:246
  23.7 8.6 %collective-permute-start.19 = (bf16[192,128]{1,0:T(8,128)(2,1)S(1)}, bf16[192,128]{1,0:T(8,128)(2,1)S(1)}, u32[]{:S(2)}, u32[]{:S(2)}) collective-permute-start(bf16[192,128]{1,0:T(8,128)(2,1)S(1)} %get-tuple-element.31.refs_0_), channel_id=1, source_target_pairs={{0,2},{1,3},{2,0},{3,1},{4,6},{5,7},{6,4},{7,5},{8,10},{9,11},{10,... | collective-permute-start | bytes 147464 | tf_op jit(solution)/shard_map/ppermute | solution.py:246
  23.8 9.8 %collective-permute-start.18 = (bf16[192,128]{1,0:T(8,128)(2,1)S(1)}, bf16[192,128]{1,0:T(8,128)(2,1)S(1)}, u32[]{:S(2)}, u32[]{:S(2)}) collective-permute-start(bf16[192,128]{1,0:T(8,128)(2,1)S(1)} %get-tuple-element.31.refs_0_), channel_id=1, source_target_pairs={{0,1},{1,2},{2,3},{3,0},{4,5},{5,6},{6,7},{7,4},{8,9},{9,10},{10,1... | collective-permute-start | bytes 147464 | tf_op jit(solution)/shard_map/ppermute | solution.py:246
  25.3 14.6 %collective-permute-start.29 = (bf16[4,192,128]{2,1,0:T(8,128)(2,1)S(1)}, bf16[4,192,128]{2,1,0:T(8,128)(2,1)S(1)}, u32[]{:S(2)}, u32[]{:S(2)}) collective-permute-start(bf16[4,192,128]{2,1,0:T(8,128)(2,1)S(1)} %pad_maximum_fusion.3), channel_id=1, source_target_pairs={{0,3},{1,0},{2,1},{3,2},{4,7},{5,4},{6,5},{7,6},{8,11},{9,8},{10,9... | collective-permute-start | bytes 589832 | tf_op jit(solution)/shard_map/ppermute | solution.py:246
  30.8 5.8 %collective-permute-start = (bf16[384,128]{1,0:T(8,128)(2,1)S(1)}, bf16[384,128]{1,0:T(8,128)(2,1)S(1)}, u32[]{:S(2)}, u32[]{:S(2)}) collective-permute-start(bf16[384,128]{1,0:T(8,128)(2,1)S(1)} %get-tuple-element.17), channel_id=1, source_target_pairs={{0,1},{1,2},{2,3},{3,0},{4,5},{5,6},{6,7},{7,4},{8,9},{9,10},{10,1... | collective-permute-start | bytes 294920 | tf_op jit(solution)/shard_map/ppermute | solution.py:246
  30.9 5.7 %collective-permute-start.1 = (bf16[384,128]{1,0:T(8,128)(2,1)S(1)}, bf16[384,128]{1,0:T(8,128)(2,1)S(1)}, u32[]{:S(2)}, u32[]{:S(2)}) collective-permute-start(bf16[384,128]{1,0:T(8,128)(2,1)S(1)} %get-tuple-element.18), channel_id=1, source_target_pairs={{0,2},{1,3},{2,0},{3,1},{4,6},{5,7},{6,4},{7,5},{8,10},{9,11},{10,... | collective-permute-start | bytes 294920 | tf_op jit(solution)/shard_map/ppermute | solution.py:246
  32.3 5.2 %collective-permute-start.2 = (bf16[384,128]{1,0:T(8,128)(2,1)S(1)}, bf16[384,128]{1,0:T(8,128)(2,1)S(1)}, u32[]{:S(2)}, u32[]{:S(2)}) collective-permute-start(bf16[384,128]{1,0:T(8,128)(2,1)S(1)} %get-tuple-element.19), channel_id=1, source_target_pairs={{0,3},{1,0},{2,1},{3,2},{4,7},{5,4},{6,5},{7,6},{8,11},{9,8},{10,9... | collective-permute-start | bytes 294920 | tf_op jit(solution)/shard_map/ppermute | solution.py:246
  33.6 7.9 %collective-permute-start.28 = (bf16[4,192,128]{2,1,0:T(8,128)(2,1)S(1)}, bf16[4,192,128]{2,1,0:T(8,128)(2,1)S(1)}, u32[]{:S(2)}, u32[]{:S(2)}) collective-permute-start(bf16[4,192,128]{2,1,0:T(8,128)(2,1)S(1)} %pad_maximum_fusion.3), channel_id=1, source_target_pairs={{0,2},{1,3},{2,0},{3,1},{4,6},{5,7},{6,4},{7,5},{8,10},{9,11},{10,... | collective-permute-start | bytes 589832 | tf_op jit(solution)/shard_map/ppermute | solution.py:246
  36.6 9.8 %collective-permute-start.27 = (bf16[4,192,128]{2,1,0:T(8,128)(2,1)S(1)}, bf16[4,192,128]{2,1,0:T(8,128)(2,1)S(1)}, u32[]{:S(2)}, u32[]{:S(2)}) collective-permute-start(bf16[4,192,128]{2,1,0:T(8,128)(2,1)S(1)} %pad_maximum_fusion.3), channel_id=1, source_target_pairs={{0,1},{1,2},{2,3},{3,0},{4,5},{5,6},{6,7},{7,4},{8,9},{9,10},{10,1... | collective-permute-start | bytes 589832 | tf_op jit(solution)/shard_map/ppermute | solution.py:246
  36.6 9.8 %collective-permute-start.26 = (bf16[4,192,128]{2,1,0:T(8,128)(2,1)S(1)}, bf16[4,192,128]{2,1,0:T(8,128)(2,1)S(1)}, u32[]{:S(2)}, u32[]{:S(2)}) collective-permute-start(bf16[4,192,128]{2,1,0:T(8,128)(2,1)S(1)} %pad_maximum_fusion.2), channel_id=1, source_target_pairs={{0,12},{4,0},{8,4},{12,8},{1,13},{5,1},{9,5},{13,9},{2,14},{6,2},{... | collective-permute-start | bytes 589832 | tf_op jit(solution)/shard_map/ppermute | solution.py:246
  37.5 8.9 %collective-permute-start.25 = (bf16[4,192,128]{2,1,0:T(8,128)(2,1)S(1)}, bf16[4,192,128]{2,1,0:T(8,128)(2,1)S(1)}, u32[]{:S(2)}, u32[]{:S(2)}) collective-permute-start(bf16[4,192,128]{2,1,0:T(8,128)(2,1)S(1)} %pad_maximum_fusion.2), channel_id=1, source_target_pairs={{0,8},{4,12},{8,0},{12,4},{1,9},{5,13},{9,1},{13,5},{2,10},{6,14},... | collective-permute-start | bytes 589832 | tf_op jit(solution)/shard_map/ppermute | solution.py:246
  39.8 6.6 %collective-permute-start.24 = (bf16[4,192,128]{2,1,0:T(8,128)(2,1)S(1)}, bf16[4,192,128]{2,1,0:T(8,128)(2,1)S(1)}, u32[]{:S(2)}, u32[]{:S(2)}) collective-permute-start(bf16[4,192,128]{2,1,0:T(8,128)(2,1)S(1)} %pad_maximum_fusion.2), channel_id=1, source_target_pairs={{0,4},{4,8},{8,12},{12,0},{1,5},{5,9},{9,13},{13,1},{2,6},{6,10},{... | collective-permute-start | bytes 589832 | tf_op jit(solution)/shard_map/ppermute | solution.py:246
  48.8 54.0 %all-to-all-start.1 = ((bf16[16,24,512]{2,1,0:T(8,128)(2,1)}), bf16[16,24,512]{2,1,0:T(8,128)(2,1)S(1)}, u32[]{:S(2)}, u32[]{:S(2)}) async-start(bf16[16,24,512]{2,1,0:T(8,128)(2,1)} %bitcast.21), calls=%async_computation.1 | async-start | bytes 786432 | tf_op jit(solution)/shard_map/all_to_all | solution.py:279
  83.7 10.3 %collective-permute-start.14 = (bf16[4,192,128]{2,1,0:T(8,128)(2,1)S(1)}, bf16[4,192,128]{2,1,0:T(8,128)(2,1)S(1)}, u32[]{:S(2)}, u32[]{:S(2)}) collective-permute-start(bf16[4,192,128]{2,1,0:T(8,128)(2,1)S(1)} %pad_maximum_fusion.1), channel_id=1, source_target_pairs={{0,3},{1,0},{2,1},{3,2},{4,7},{5,4},{6,5},{7,6},{8,11},{9,8},{10,9... | collective-permute-start | bytes 589832 | tf_op jit(solution)/shard_map/ppermute | solution.py:246
  86.7 5.0 %collective-permute-start.5 = (bf16[192,128]{1,0:T(8,128)(2,1)S(1)}, bf16[192,128]{1,0:T(8,128)(2,1)S(1)}, u32[]{:S(2)}, u32[]{:S(2)}) collective-permute-start(bf16[192,128]{1,0:T(8,128)(2,1)S(1)} %get-tuple-element.35.refs_0_), channel_id=1, source_target_pairs={{0,3},{1,0},{2,1},{3,2},{4,7},{5,4},{6,5},{7,6},{8,11},{9,8},{10,9... | collective-permute-start | bytes 147464 | tf_op jit(solution)/shard_map/ppermute | solution.py:246
  87.0 5.0 %collective-permute-start.3 = (bf16[192,128]{1,0:T(8,128)(2,1)S(1)}, bf16[192,128]{1,0:T(8,128)(2,1)S(1)}, u32[]{:S(2)}, u32[]{:S(2)}) collective-permute-start(bf16[192,128]{1,0:T(8,128)(2,1)S(1)} %get-tuple-element.35.refs_0_), channel_id=1, source_target_pairs={{0,1},{1,2},{2,3},{3,0},{4,5},{5,6},{6,7},{7,4},{8,9},{9,10},{10,1... | collective-permute-start | bytes 147464 | tf_op jit(solution)/shard_map/ppermute | solution.py:246
  88.2 8.0 %collective-permute-start.13 = (bf16[4,192,128]{2,1,0:T(8,128)(2,1)S(1)}, bf16[4,192,128]{2,1,0:T(8,128)(2,1)S(1)}, u32[]{:S(2)}, u32[]{:S(2)}) collective-permute-start(bf16[4,192,128]{2,1,0:T(8,128)(2,1)S(1)} %pad_maximum_fusion.1), channel_id=1, source_target_pairs={{0,2},{1,3},{2,0},{3,1},{4,6},{5,7},{6,4},{7,5},{8,10},{9,11},{10,... | collective-permute-start | bytes 589832 | tf_op jit(solution)/shard_map/ppermute | solution.py:246
  91.8 9.0 %collective-permute-start.12 = (bf16[4,192,128]{2,1,0:T(8,128)(2,1)S(1)}, bf16[4,192,128]{2,1,0:T(8,128)(2,1)S(1)}, u32[]{:S(2)}, u32[]{:S(2)}) collective-permute-start(bf16[4,192,128]{2,1,0:T(8,128)(2,1)S(1)} %pad_maximum_fusion.1), channel_id=1, source_target_pairs={{0,1},{1,2},{2,3},{3,0},{4,5},{5,6},{6,7},{7,4},{8,9},{9,10},{10,1... | collective-permute-start | bytes 589832 | tf_op jit(solution)/shard_map/ppermute | solution.py:246
  92.1 8.6 %collective-permute-start.11 = (bf16[4,192,128]{2,1,0:T(8,128)(2,1)S(1)}, bf16[4,192,128]{2,1,0:T(8,128)(2,1)S(1)}, u32[]{:S(2)}, u32[]{:S(2)}) collective-permute-start(bf16[4,192,128]{2,1,0:T(8,128)(2,1)S(1)} %pad_maximum_fusion), channel_id=1, source_target_pairs={{0,12},{4,0},{8,4},{12,8},{1,13},{5,1},{9,5},{13,9},{2,14},{6,2},{... | collective-permute-start | bytes 589832 | tf_op jit(solution)/shard_map/ppermute | solution.py:246
  93.1 7.7 %collective-permute-start.10 = (bf16[4,192,128]{2,1,0:T(8,128)(2,1)S(1)}, bf16[4,192,128]{2,1,0:T(8,128)(2,1)S(1)}, u32[]{:S(2)}, u32[]{:S(2)}) collective-permute-start(bf16[4,192,128]{2,1,0:T(8,128)(2,1)S(1)} %pad_maximum_fusion), channel_id=1, source_target_pairs={{0,8},{4,12},{8,0},{12,4},{1,9},{5,13},{9,1},{13,5},{2,10},{6,14},... | collective-permute-start | bytes 589832 | tf_op jit(solution)/shard_map/ppermute | solution.py:246
  94.0 7.2 %collective-permute-start.9 = (bf16[4,192,128]{2,1,0:T(8,128)(2,1)S(1)}, bf16[4,192,128]{2,1,0:T(8,128)(2,1)S(1)}, u32[]{:S(2)}, u32[]{:S(2)}) collective-permute-start(bf16[4,192,128]{2,1,0:T(8,128)(2,1)S(1)} %pad_maximum_fusion), channel_id=1, source_target_pairs={{0,4},{4,8},{8,12},{12,0},{1,5},{5,9},{9,13},{13,1},{2,6},{6,10},{... | collective-permute-start | bytes 589832 | tf_op jit(solution)/shard_map/ppermute | solution.py:246
  (18 other events, 138.9 us)
where the time goes:
time: 164 us; the launch traced here: 163 us
  starting transfers between devices  65.7 us (40%)
  blocking collectives  54.3 us (33%)
  waiting for transfers between devices  21.1 us (13%)
  Pallas kernels  11.1 us (7%)
  local copies, waits for them, and re-layouts  9.63 us (6%)
    ppermute x30, starting transfers between devices, shift(): return lax.ppermute(value, axis, [(i, (i + by) % n) for i in range(n)])  37.2 us
    all_to_all x1, blocking collectives, body(): received.append(lax.all_to_all(grad, group_axes, 0, 0, tiled=True))  28.8 us
    all_to_all x1, starting transfers between devices, body(): received.append(lax.all_to_all(grad, group_axes, 0, 0, tiled=True))  28.5 us
    all_to_all x1, blocking collectives, body(): arrived = lax.all_to_all(send, group_axes, 0, 0, tiled=True)  25.6 us
    ppermute x30, waiting for transfers between devices, shift(): return lax.ppermute(value, axis, [(i, (i + by) % n) for i in range(n)])  21.1 us
    unnamed x22, local copies, waits for them, and re-layouts  8.64 us
    pallas_call x2, Pallas kernels, attention(): pl.pallas_call(functools.partial(attention_kernel, slot, layers, tokens,...  4.14 us
    pallas_call x2, Pallas kernels, layer_grad(): pl.pallas_call(functools.partial(grad_kernel, tokens), grid_spec=pltpu.Pr...  3.97 us
  transfers between devices with their start and end apart: 31, of which 13 were waited for; matrix products, arithmetic and copies ran while one was open for 0% of the time, Pallas kernels for 3%

commit v1 on v0

v1 whole, which is shorter than its diff:
```python
import functools

import jax
import jax.numpy as jnp
from jax import lax
from jax.experimental import pallas as pl
from jax.experimental.pallas import tpu as pltpu
from jax.sharding import Mesh, PartitionSpec as P

HQ = 32
KVH = 4
HD = 128
BETA_ONE = 0.9
BETA_TWO = 0.95
LEARN_RATE = 0.03
DECAY_RATE = 0.1
EPSILON = 1e-08
CORRECT_ONE = 0.9999734386011124
CORRECT_TWO = 0.994079470779667
LOG2E = 1.4426950408889634
TQ = 256
VMEM = 60 << 20
BF = jnp.bfloat16
F32 = jnp.float32


def first_and_count(map_ref, replica, section, layers):
    first = jnp.int32(0)
    count = jnp.int32(0)
    for l in range(layers):
        at = map_ref[replica, l]
        first += (at < section).astype(jnp.int32)
        count += (at == section).astype(jnp.int32)
    return first, count


def attention_kernel(layers, tokens, per_dev, ids, lmap, counts, windows,
                     q_ref, k_ref, g_ref, *rest):
    outs = rest[:4]
    acc, p_scr, g_scr = rest[4:]
    slot, step = pl.program_id(0), pl.program_id(1)
    steps = pl.num_programs(1)
    replica, section, x_id = ids[0], ids[1], ids[3]
    first, held = first_and_count(lmap, replica, section, layers)
    layer = jnp.minimum(first + slot, layers - 1)
    window = windows[layer]
    length = jnp.where(slot < held, counts[replica], 0)
    reach = tokens // 2 // TQ
    row0 = step * TQ

    @pl.when(step == 0)
    def _():
        acc[...] = jnp.zeros_like(acc)

    def work(chunks):
        base = pl.multiple_of((step - (chunks - 1)) * TQ, TQ)
        keys = k_ref[pl.ds(base, chunks * TQ), :]
        q_col = lax.broadcasted_iota(jnp.int32, (TQ, TQ), 1)
        k_row = lax.broadcasted_iota(jnp.int32, (TQ, TQ), 0)
        diff = q_col - k_row
        live = (row0 + lax.broadcasted_iota(jnp.int32, (TQ, HD), 0)) < length
        scale = HD ** (-0.5) * LOG2E
        for h in range(per_dev):
            query = q_ref[:, h * HD:(h + 1) * HD]
            parts = []
            peak = None
            for c in range(chunks):
                s = lax.dot_general(
                    keys[c * TQ:(c + 1) * TQ], query, (((1,), (1,)), ((), ())),
                    preferred_element_type=F32)
                off = (chunks - 1 - c) * TQ
                ok = diff < (window - off)
                if c == chunks - 1:
                    ok = ok & (diff >= 0)
                s = jnp.where(ok, s, -1e30)
                parts.append(s)
                m = jnp.max(s, axis=0, keepdims=True)
                peak = m if peak is None else jnp.maximum(peak, m)
            shift = peak * scale
            total = None
            for c in range(chunks):
                e = jnp.exp2(parts[c] * scale - shift)
                t = jnp.sum(e, axis=0, keepdims=True)
                total = t if total is None else total + t
                p_scr[c * TQ:(c + 1) * TQ, h * TQ:(h + 1) * TQ] = e.astype(BF)
            inverse = jnp.broadcast_to(1.0 / total, (HD, TQ)).T
            grad = g_ref[:, h * HD:(h + 1) * HD].astype(F32) * inverse
            g_scr[h * TQ:(h + 1) * TQ, :] = jnp.where(live, grad, 0.0).astype(BF)
        for c in range(chunks):
            rows = pl.ds(base + c * TQ, TQ)
            acc[rows, :] += jnp.dot(
                p_scr[c * TQ:(c + 1) * TQ, :], g_scr[...], preferred_element_type=F32)

    wanted = jnp.minimum(step, (window + TQ - 2) // TQ) + 1
    for chunks in range(1, reach + 2):
        @pl.when((row0 < length) & (wanted == chunks))
        def _(chunks=chunks):
            work(chunks)

    @pl.when(step == steps - 1)
    def _():
        part = tokens // 4
        for k in range(4):
            at = pl.multiple_of(lax.rem(x_id + k, 4) * part, part)
            outs[k][...] = acc[pl.ds(at, part), :].astype(BF)


def attention(scalars, queries, key_rows, out_grad, layers):
    slots, tokens = queries.shape[2], queries.shape[3]
    per_dev = queries.shape[4] // HD
    part = tokens // 4
    wide = per_dev * HD
    row_block = pl.BlockSpec((None, None, None, TQ, wide), lambda j, i, *_: (0, 0, j, i, 0))
    key_block = pl.BlockSpec(
        (None, None, None, tokens, HD), lambda j, i, ids, *_: (0, 0, j, 0, ids[2]))
    out_block = pl.BlockSpec((None, part, HD), lambda j, i, *_: (j, 0, 0))
    return pl.pallas_call(
        functools.partial(attention_kernel, layers, tokens, per_dev),
        grid_spec=pltpu.PrefetchScalarGridSpec(
            num_scalar_prefetch=4,
            grid=(slots, tokens // TQ),
            in_specs=[row_block, key_block, row_block],
            out_specs=[out_block] * 4,
            scratch_shapes=[
                pltpu.VMEM((tokens, HD), F32),
                pltpu.VMEM((tokens // 2 + TQ, per_dev * TQ), BF),
                pltpu.VMEM((per_dev * TQ, HD), BF),
            ],
        ),
        out_shape=[jax.ShapeDtypeStruct((slots, part, HD), BF)] * 4,
        compiler_params=pltpu.CompilerParams(vmem_limit_bytes=VMEM),
        cost_estimate=pl.CostEstimate(
            flops=36 * per_dev * 4 * TQ * TQ * HD, bytes_accessed=4 << 20,
            transcendentals=36 * per_dev * TQ * TQ),
        name="attention",
    )(*scalars, queries, key_rows, out_grad)


def grad_kernel(tokens, rows, ids, x_ref, piece_ref, own_ref, other_ref, value, result):
    core = lax.rem(ids[1], 2)
    part = tokens // 4
    for y in range(4):
        for x in range(4):
            value[x * part:(x + 1) * part, y * HD:(y + 1) * HD] = piece_ref[y * 4 + x]
    result[...] = lax.dot_general(
        x_ref[...], value[...], (((0,), (0,)), ((), ())), preferred_element_type=F32)
    for z in range(own_ref.shape[0]):
        for rel, ref in ((0, own_ref), (1, other_ref)):
            at = pl.multiple_of((2 * z + lax.rem(core + rel, 2)) * rows, 8)
            ref[z] = result[pl.ds(at, rows), :].astype(BF)


def layer_grads(ids, normed, pieces, rows):
    slots, tokens, width = normed.shape[2:]
    chips = width // rows // 2
    part = tokens // 4
    out_block = pl.BlockSpec((chips, None, rows, KVH * HD), lambda j, *_: (0, j, 0, 0))
    return pl.pallas_call(
        functools.partial(grad_kernel, tokens, rows),
        grid_spec=pltpu.PrefetchScalarGridSpec(
            num_scalar_prefetch=1,
            grid=(slots,),
            in_specs=[pl.BlockSpec((None, None, None, tokens, width),
                                   lambda j, *_: (0, 0, j, 0, 0)),
                      pl.BlockSpec((16, None, part, HD), lambda j, *_: (0, j, 0, 0))],
            out_specs=[out_block, out_block],
            scratch_shapes=[pltpu.VMEM((tokens, KVH * HD), BF),
                            pltpu.VMEM((width, KVH * HD), F32)],
        ),
        out_shape=[jax.ShapeDtypeStruct((chips, slots, rows, KVH * HD), BF)] * 2,
        compiler_params=pltpu.CompilerParams(vmem_limit_bytes=VMEM),
        cost_estimate=pl.CostEstimate(
            flops=4 * tokens * width * KVH * HD, bytes_accessed=6 << 20, transcendentals=0),
        name="layer_grads",
    )(ids, normed, pieces)


def adam_kernel(reps, layers, ids, lmap, arrived, master, one, two,
                new_master, new_one, new_two, own, other):
    layer = pl.program_id(0)
    core = lax.rem(ids[1], 2)

    @pl.when(layer == 0)
    def _():
        own[...] = jnp.zeros_like(own)
        other[...] = jnp.zeros_like(other)

    total = None
    places = []
    for r in range(reps):
        section = lmap[r, layer]
        first, _ = first_and_count(lmap, r, section, layers)
        slot = layer - first
        chip = 2 * r + section // 2
        rel = lax.rem(section + core, 2)
        places.append((rel, chip, slot))
        term = arrived[chip, rel, slot].astype(F32)
        total = term if total is None else total + term
    mean = total / reps
    m1 = BETA_ONE * one[...] + (1.0 - BETA_ONE) * mean
    m2 = BETA_TWO * two[...] + (1.0 - BETA_TWO) * mean * mean
    move = m1 / CORRECT_ONE / (jnp.sqrt(m2 / CORRECT_TWO) + EPSILON)
    updated = master[...] - LEARN_RATE * (move + DECAY_RATE * master[...])
    new_master[...] = updated
    new_one[...] = m1
    new_two[...] = m2
    rounded = updated.astype(BF)
    for rel, chip, slot in places:
        @pl.when(rel == 0)
        def _(chip=chip, slot=slot):
            own[chip, slot] = rounded

        @pl.when(rel != 0)
        def _(chip=chip, slot=slot):
            other[chip, slot] = rounded


def adam(ids, lmap, arrived, master, one, two):
    layers, _, rows, wide = master.shape
    chips, _, slots = arrived.shape[:3]
    state = pl.BlockSpec((None, None, rows, wide), lambda l, *_: (l, 0, 0, 0))
    send = pl.BlockSpec((chips, slots, rows, wide), lambda l, *_: (0, 0, 0, 0))
    f32 = jax.ShapeDtypeStruct(master.shape, F32)
    return pl.pallas_call(
        functools.partial(adam_kernel, lmap.shape[0], layers),
        grid_spec=pltpu.PrefetchScalarGridSpec(
            num_scalar_prefetch=2,
            grid=(layers,),
            in_specs=[pl.BlockSpec(arrived.shape, lambda l, *_: (0, 0, 0, 0, 0)),
                      state, state, state],
            out_specs=[state, state, state, send, send],
        ),
        out_shape=[f32, f32, f32] + [jax.ShapeDtypeStruct((chips, slots, rows, wide), BF)] * 2,
        compiler_params=pltpu.CompilerParams(vmem_limit_bytes=VMEM),
        cost_estimate=pl.CostEstimate(flops=20 * master.size, bytes_accessed=4 << 20,
                                      transcendentals=master.size),
        name="adamw",
    )(ids, lmap, arrived, master, one, two)


def shift(value, axis, by):
    n = lax.axis_size(axis)
    return lax.ppermute(value, axis, [(i, (i + by) % n) for i in range(n)])


def body(layer_section, token_count, window_size, normed_input, queries, key_rows, out_grad,
         master, moment_one, moment_two):
    layers = layer_section.shape[1]
    chip_axes = ("rep", "z")
    core = lax.axis_index("core")
    ids = jnp.stack([
        lax.axis_index("rep"), lax.axis_index(("z", "core")),
        lax.axis_index("y"), lax.axis_index("x")]).astype(jnp.int32)
    rows = master.shape[2]
    parts = attention((ids, layer_section, token_count, window_size),
                      queries, key_rows, out_grad, layers)
    total = parts[0].astype(F32)
    for k in range(1, 4):
        total = total + shift(parts[k], "x", k).astype(F32)
    block = total.astype(BF)
    spread = lax.optimization_barrier(jnp.broadcast_to(block[None], (16,) + block.shape))
    pieces = lax.all_to_all(spread, ("y", "x"), 0, 0, tiled=True)
    own, other = layer_grads(ids, normed_input, pieces, rows)
    arrived = lax.all_to_all(jnp.stack([own, shift(other, "core", 1)], axis=1),
                             chip_axes, 0, 0, tiled=True)
    updated, first, second, own, other = adam(
        ids, layer_section, arrived, master, moment_one, moment_two)
    arrived = lax.all_to_all(jnp.stack([own, shift(other, "core", 1)], axis=1),
                             chip_axes, 0, 0, tiled=True)
    arrived = jnp.where(core == 0, arrived, arrived[:, ::-1])
    weights = jnp.transpose(arrived, (2, 0, 1, 3, 4)).reshape(
        arrived.shape[2], -1, arrived.shape[4])
    return updated, first, second, weights[None, None]


def solution(mesh):
    reps, sections, tps = mesh.devices.shape
    fine = Mesh(mesh.devices.reshape(reps, 2, sections // 2, 4, tps // 4),
                ("rep", "z", "core", "y", "x"))
    section, tp = ("z", "core"), ("y", "x")
    wide = P("rep", section, None, None, tp)
    state = P(None, tp, ("rep",) + section, None)
    in_specs = (P(), P(), P(), wide, wide, P("rep", section, None, None, None), wide,
                state, state, state)
    out_specs = (state, state, state, P("rep", section, None, tp, None))
    return jax.shard_map(body, mesh=fine, in_specs=in_specs, out_specs=out_specs, check_vma=False)
```

time: 164 us -> 156 us (0.951)
  starting transfers between devices: 65.7 us -> 18.3 us
  blocking collectives: 54.3 us -> 73.1 us
  Pallas kernels: 11.1 us -> 24.4 us
  waiting for transfers between devices: 21.1 us -> 30.9 us
  local copies, waits for them, and re-layouts: 9.63 us -> 1.74 us
  other arithmetic: 0.3 us -> 4.89 us
    all_to_all x1, starting transfers between devices: 28.5 us -> 3.55 us  [body(): lax.all_to_all(jnp.stack([own, shift(other, 'core', 1)], axis=1), chip_ax...]
    all_to_all x1, waiting for transfers between devices: 0.01 us -> 23.5 us  [body(): lax.all_to_all(jnp.stack([own, shift(other, 'core', 1)], axis=1), chip_ax...]
    ppermute x30 -> x5, starting transfers between devices: 37.2 us -> 14.8 us  [shift(): return lax.ppermute(value, axis, [(i, (i + by) % n) for i in range(n)])]
    all_to_all x2, blocking collectives: 54.3 us -> 73.1 us  [the longest x1 40 us: body(): pieces = lax.all_to_all(spread, ('y', 'x'), 0, 0, tiled=True)]
    ppermute x30 -> x5, waiting for transfers between devices: 21.1 us -> 7.32 us  [shift(): return lax.ppermute(value, axis, [(i, (i + by) % n) for i in range(n)])]
    pallas_call x4 -> x2, Pallas kernels: 8.11 us -> 18.6 us  [the longest x1 13.4 us: attention(): pl.pallas_call(functools.partial(attention_kernel, layers, tokens, per_de...]
    unnamed x22 -> x0, local copies, waits for them, and re-layouts: 8.64 us -> none
    pallas_call x1, Pallas kernels: 2.97 us -> 5.86 us  [adam(): pl.pallas_call(functools.partial(adam_kernel, lmap.shape[0], layers), gri...]
  transfers between devices with their start and end apart: 31 -> 6, of which waited for: 13 -> 5; matrix products, arithmetic and copies ran while one was open for 0% -> 0% of each run, Pallas kernels for 3% -> 0%
where the time goes in v1:
time: 156 us; the launch traced here: 154 us
  blocking collectives  73.1 us (47%)
  waiting for transfers between devices  30.9 us (20%)
  Pallas kernels  24.4 us (16%)
  starting transfers between devices  18.3 us (12%)
  other arithmetic  4.89 us (3%)
  local copies, waits for them, and re-layouts  1.74 us (1%)
    all_to_all x1, blocking collectives, body(): pieces = lax.all_to_all(spread, ('y', 'x'), 0, 0, tiled=True)  40 us
    all_to_all x1, blocking collectives, body(): lax.all_to_all(jnp.stack([own, shift(other, 'core', 1)], axis=1), chip_ax...  33.1 us
    all_to_all x1, waiting for transfers between devices, body(): lax.all_to_all(jnp.stack([own, shift(other, 'core', 1)], axis=1), chip_ax...  23.5 us
    ppermute x5, starting transfers between devices, shift(): return lax.ppermute(value, axis, [(i, (i + by) % n) for i in range(n)])  14.8 us
    pallas_call x1, Pallas kernels, attention(): pl.pallas_call(functools.partial(attention_kernel, layers, tokens, per_de...  13.4 us
    ppermute x5, waiting for transfers between devices, shift(): return lax.ppermute(value, axis, [(i, (i + by) % n) for i in range(n)])  7.32 us
    pallas_call x1, Pallas kernels, adam(): pl.pallas_call(functools.partial(adam_kernel, lmap.shape[0], layers), gri...  5.86 us
    pallas_call x1, Pallas kernels, layer_grads(): pl.pallas_call(functools.partial(grad_kernel, tokens, rows), grid_spec=pl...  5.16 us
  transfers between devices with their start and end apart: 6, of which 5 were waited for; matrix products, arithmetic and copies ran while one was open for 0% of the time, Pallas kernels for 0%

profile of v1, /device:TPU:1, one launch (start us, length us, event | category | flops | bytes accessed | tf_op | source)
XLA Modules:
  0.0 154.1 jit_solution(9023074013098589691)
XLA Ops:
  0.6 0.7 pad_add_fusion.ids
  1.3 13.4 %attention.1 = (bf16[2,384,128]{2,1,0:T(8,128)(2,1)}, bf16[2,384,128]{2,1,0:T(8,128)(2,1)}, bf16[2,384,128]{2,1,0:T(8,128)(2,1)}, bf16[2,384,128]{2,1,0:T(8,128)(2,1)}) custom-call(s32[4]{0:T(128)} %pad_add_fusion.ids, s32[4,6]{1,0:T(4,128)} %lmap.3, s32[4]{0:T(128)} %counts.1, s32[6]{0:T(128)} %windows.1, bf16[1,1,2,1536,256]{4,3,2,1,0:T(8,128)(2,1)} %q_ref.1, ...), custom_call_target="tpu_custom_call" | custom-call | flops 2415919104 | bytes 4194304 | tf_op jit(solution)/shard_map/attention/pallas_call | solution.py:117
  14.7 2.0 %collective-permute-start = (bf16[2,384,128]{2,1,0:T(8,128)(2,1)}, bf16[2,384,128]{2,1,0:T(8,128)(2,1)S(1)}, u32[]{:S(2)}, u32[]{:S(2)}) collective-permute-start(bf16[2,384,128]{2,1,0:T(8,128)(2,1)} %get-tuple-element.16), channel_id=1, source_target_pairs={{0,1},{1,2},{2,3},{3,0},{4,5},{5,6},{6,7},{7,4},{8,9},{9,10},{10,1... | collective-permute-start | bytes 589832 | tf_op jit(solution)/shard_map/ppermute | solution.py:243
  16.7 2.4 %collective-permute-start.1 = (bf16[2,384,128]{2,1,0:T(8,128)(2,1)}, bf16[2,384,128]{2,1,0:T(8,128)(2,1)S(1)}, u32[]{:S(2)}, u32[]{:S(2)}) collective-permute-start(bf16[2,384,128]{2,1,0:T(8,128)(2,1)} %get-tuple-element.17), channel_id=1, source_target_pairs={{0,2},{1,3},{2,0},{3,1},{4,6},{5,7},{6,4},{7,5},{8,10},{9,11},{10,... | collective-permute-start | bytes 589832 | tf_op jit(solution)/shard_map/ppermute | solution.py:243
  19.2 1.2 collective-permute-start.2
  20.4 0.9 collective-permute-done
  21.3 3.3 %collective-permute-done.1 = bf16[2,384,128]{2,1,0:T(8,128)(2,1)S(1)} collective-permute-done((bf16[2,384,128]{2,1,0:T(8,128)(2,1)}, bf16[2,384,128]{2,1,0:T(8,128)(2,1)S(1)}, u32[]{:S(2)}, u32[]{:S(2)}) %collective-permute-start.1) | collective-permute-done | bytes 196640 | tf_op jit(solution)/shard_map/ppermute | solution.py:243
  24.6 1.0 add_convert_fusion
  25.6 0.7 broadcast_in_dim.2
  26.3 40.0 %all_to_all.15.piece_ref = bf16[16,2,384,128]{3,2,1,0:T(8,128)(2,1)} all-to-all(bf16[16,2,384,128]{3,2,1,0:T(8,128)(2,1)S(1)} %broadcast_in_dim.2), channel_id=1, replica_groups=mesh['rep'=4,'z'=2,'core'=2,'y'=4,'x'=4] {'y','x'}, dimensions={0} | all-to-all | bytes 6291456 | tf_op jit(solution)/shard_map/all_to_all | solution.py:262
  66.3 5.2 %layer_grads.1 = (bf16[8,2,24,512]{3,2,1,0:T(8,128)(2,1)}, bf16[8,2,24,512]{3,2,1,0:T(8,128)(2,1)}) custom-call(s32[4]{0:T(128)} %pad_add_fusion.ids, bf16[1,1,2,1536,384]{4,3,2,1,0:T(8,128)(2,1)} %x_ref.1, bf16[16,2,384,128]{3,2,1,0:T(8,128)(2,1)} %all_to_all.15.piece_ref), custom_call_target="tpu_custom_call" | custom-call | flops 1207959552 | bytes 6291456 | tf_op jit(solution)/shard_map/layer_grads/pallas_call | solution.py:158
  71.5 7.3 %collective-permute-start.3 = (bf16[8,2,24,512]{3,2,1,0:T(8,128)(2,1)}, bf16[8,2,24,512]{3,2,1,0:T(8,128)(2,1)S(1)}, u32[]{:S(2)}, u32[]{:S(2)}) collective-permute-start(bf16[8,2,24,512]{3,2,1,0:T(8,128)(2,1)} %get-tuple-element.20), channel_id=1, source_target_pairs={{0,16},{16,0},{1,17},{17,1},{2,18},{18,2},{3,19},{19,3},{4,20},{20... | collective-permute-start | bytes 1179656 | tf_op jit(solution)/shard_map/ppermute | solution.py:243
  78.8 1.6 %collective-permute-done.3 = bf16[8,2,24,512]{3,2,1,0:T(8,128)(2,1)S(1)} collective-permute-done((bf16[8,2,24,512]{3,2,1,0:T(8,128)(2,1)}, bf16[8,2,24,512]{3,2,1,0:T(8,128)(2,1)S(1)}, u32[]{:S(2)}, u32[]{:S(2)}) %collective-permute-start.3) | collective-permute-done | bytes 393248 | tf_op jit(solution)/shard_map/ppermute | solution.py:243
  80.3 1.1 pad_maximum_fusion
  81.4 33.1 %all_to_all.16.arrived = bf16[8,2,2,24,512]{4,3,2,1,0:T(8,128)(2,1)} all-to-all(bf16[8,2,2,24,512]{4,3,2,1,0:T(8,128)(2,1)S(1)} %pad_maximum_fusion), channel_id=1, replica_groups=mesh['rep'=4,'z'=2,'core'=2,'y'=4,'x'=4] {'rep','z'}, dimensions={0} | all-to-all | bytes 1572864 | tf_op jit(solution)/shard_map/all_to_all | solution.py:264
  114.5 5.9 %adamw.1 = (f32[6,1,24,512]{3,2,1,0:T(8,128)}, f32[6,1,24,512]{3,2,1,0:T(8,128)}, f32[6,1,24,512]{3,2,1,0:T(8,128)}, bf16[8,2,24,512]{3,2,1,0:T(8,128)(2,1)}, bf16[8,2,24,512]{3,2,1,0:T(8,128)(2,1)}) custom-call(s32[4]{0:T(128)} %pad_add_fusion.ids, s32[4,6]{1,0:T(4,128)} %lmap.3, bf16[8,2,2,24,512]{4,3,2,1,0:T(8,128)(2,1)} %all_to_all.16.arrived, ...), custom_call_target="tpu_custom_call" | custom-call | flops 1474560 | bytes 4194304 | tf_op jit(solution)/shard_map/adamw/pallas_call | solution.py:224
  120.4 1.8 %collective-permute-start.4 = (bf16[8,2,24,512]{3,2,1,0:T(8,128)(2,1)}, bf16[8,2,24,512]{3,2,1,0:T(8,128)(2,1)S(1)}, u32[]{:S(2)}, u32[]{:S(2)}) collective-permute-start(bf16[8,2,24,512]{3,2,1,0:T(8,128)(2,1)} %get-tuple-element.25), channel_id=1, source_target_pairs={{0,16},{16,0},{1,17},{17,1},{2,18},{18,2},{3,19},{19,3},{4,20},{20... | collective-permute-start | bytes 1179656 | tf_op jit(solution)/shard_map/ppermute | solution.py:243
  122.2 1.6 %collective-permute-done.4 = bf16[8,2,24,512]{3,2,1,0:T(8,128)(2,1)S(1)} collective-permute-done((bf16[8,2,24,512]{3,2,1,0:T(8,128)(2,1)}, bf16[8,2,24,512]{3,2,1,0:T(8,128)(2,1)S(1)}, u32[]{:S(2)}, u32[]{:S(2)}) %collective-permute-start.4) | collective-permute-done | bytes 393248 | tf_op jit(solution)/shard_map/ppermute | solution.py:243
  123.8 1.1 pad_maximum_fusion.1
  124.9 0.9 copy.15
  125.8 3.5 %all-to-all-start.2 = ((bf16[8,2,2,24,512]{4,3,2,1,0:T(8,128)(2,1)}), bf16[8,2,2,24,512]{4,3,2,1,0:T(8,128)(2,1)S(1)}, u32[]{:S(2)}, u32[]{:S(2)}) async-start(bf16[8,2,2,24,512]{4,3,2,1,0:T(8,128)(2,1)} %copy.15), calls=%async_computation.2 | async-start | bytes 1572864 | tf_op jit(solution)/shard_map/all_to_all | solution.py:268
  129.4 23.5 %all-to-all-done.2 = bf16[8,2,2,24,512]{4,3,2,1,0:T(8,128)(2,1)S(1)} async-done(((bf16[8,2,2,24,512]{4,3,2,1,0:T(8,128)(2,1)}), bf16[8,2,2,24,512]{4,3,2,1,0:T(8,128)(2,1)S(1)}, u32[]{:S(2)}, u32[]{:S(2)}) %all-to-all-start.2) | async-done | bytes 786464 | tf_op jit(solution)/shard_map/all_to_all | solution.py:268
  152.9 0.1 copy.17
  153.0 1.1 reverse_select_fusion
  (1 shorter events, 0.0 us)
Async XLA Ops:
  14.7 6.6 %collective-permute-start = (bf16[2,384,128]{2,1,0:T(8,128)(2,1)}, bf16[2,384,128]{2,1,0:T(8,128)(2,1)S(1)}, u32[]{:S(2)}, u32[]{:S(2)}) collective-permute-start(bf16[2,384,128]{2,1,0:T(8,128)(2,1)} %get-tuple-element.16), channel_id=1, source_target_pairs={{0,1},{1,2},{2,3},{3,0},{4,5},{5,6},{6,7},{7,4},{8,9},{9,10},{10,1... | collective-permute-start | bytes 589832 | tf_op jit(solution)/shard_map/ppermute | solution.py:243
  16.7 7.8 %collective-permute-start.1 = (bf16[2,384,128]{2,1,0:T(8,128)(2,1)}, bf16[2,384,128]{2,1,0:T(8,128)(2,1)S(1)}, u32[]{:S(2)}, u32[]{:S(2)}) collective-permute-start(bf16[2,384,128]{2,1,0:T(8,128)(2,1)} %get-tuple-element.17), channel_id=1, source_target_pairs={{0,2},{1,3},{2,0},{3,1},{4,6},{5,7},{6,4},{7,5},{8,10},{9,11},{10,... | collective-permute-start | bytes 589832 | tf_op jit(solution)/shard_map/ppermute | solution.py:243
  19.2 5.4 %collective-permute-start.2 = (bf16[2,384,128]{2,1,0:T(8,128)(2,1)}, bf16[2,384,128]{2,1,0:T(8,128)(2,1)S(1)}, u32[]{:S(2)}, u32[]{:S(2)}) collective-permute-start(bf16[2,384,128]{2,1,0:T(8,128)(2,1)} %get-tuple-element.18), channel_id=1, source_target_pairs={{0,3},{1,0},{2,1},{3,2},{4,7},{5,4},{6,5},{7,6},{8,11},{9,8},{10,9... | collective-permute-start | bytes 589832 | tf_op jit(solution)/shard_map/ppermute | solution.py:243
  71.5 8.9 %collective-permute-start.3 = (bf16[8,2,24,512]{3,2,1,0:T(8,128)(2,1)}, bf16[8,2,24,512]{3,2,1,0:T(8,128)(2,1)S(1)}, u32[]{:S(2)}, u32[]{:S(2)}) collective-permute-start(bf16[8,2,24,512]{3,2,1,0:T(8,128)(2,1)} %get-tuple-element.20), channel_id=1, source_target_pairs={{0,16},{16,0},{1,17},{17,1},{2,18},{18,2},{3,19},{19,3},{4,20},{20... | collective-permute-start | bytes 1179656 | tf_op jit(solution)/shard_map/ppermute | solution.py:243
  120.4 3.4 %collective-permute-start.4 = (bf16[8,2,24,512]{3,2,1,0:T(8,128)(2,1)}, bf16[8,2,24,512]{3,2,1,0:T(8,128)(2,1)S(1)}, u32[]{:S(2)}, u32[]{:S(2)}) collective-permute-start(bf16[8,2,24,512]{3,2,1,0:T(8,128)(2,1)} %get-tuple-element.25), channel_id=1, source_target_pairs={{0,16},{16,0},{1,17},{17,1},{2,18},{18,2},{3,19},{19,3},{4,20},{20... | collective-permute-start | bytes 1179656 | tf_op jit(solution)/shard_map/ppermute | solution.py:243
  125.8 27.1 %all-to-all-start.2 = ((bf16[8,2,2,24,512]{4,3,2,1,0:T(8,128)(2,1)}), bf16[8,2,2,24,512]{4,3,2,1,0:T(8,128)(2,1)S(1)}, u32[]{:S(2)}, u32[]{:S(2)}) async-start(bf16[8,2,2,24,512]{4,3,2,1,0:T(8,128)(2,1)} %copy.15), calls=%async_computation.2 | async-start | bytes 1572864 | tf_op jit(solution)/shard_map/all_to_all | solution.py:268

commit v2 on v1

v2 whole, which is shorter than its diff:
```python
import functools

import jax
import jax.numpy as jnp
from jax import lax
from jax.experimental import pallas as pl
from jax.experimental.pallas import tpu as pltpu
from jax.sharding import Mesh, PartitionSpec as P

HQ = 32
KVH = 4
HD = 128
BETA_ONE = 0.9
BETA_TWO = 0.95
LEARN_RATE = 0.03
DECAY_RATE = 0.1
EPSILON = 1e-08
CORRECT_ONE = 0.9999734386011124
CORRECT_TWO = 0.994079470779667
LOG2E = 1.4426950408889634
TQ = 256
RB = 512
VMEM = 60 << 20
BF = jnp.bfloat16
F32 = jnp.float32


def first_and_count(map_ref, replica, section, layers):
    first = jnp.int32(0)
    count = jnp.int32(0)
    for l in range(layers):
        at = map_ref[replica, l]
        first += (at < section).astype(jnp.int32)
        count += (at == section).astype(jnp.int32)
    return first, count


def attention_kernel(layers, tokens, per_dev, ids, lmap, counts, windows,
                     q_ref, k_ref, g_ref, *rest):
    outs = rest[:4]
    acc, p_scr, g_scr = rest[4:]
    slot, step = pl.program_id(0), pl.program_id(1)
    steps = pl.num_programs(1)
    replica, section, x_id = ids[0], ids[1], ids[3]
    first, held = first_and_count(lmap, replica, section, layers)
    layer = jnp.minimum(first + slot, layers - 1)
    window = windows[layer]
    length = jnp.where(slot < held, counts[replica], 0)
    reach = tokens // 2 // TQ
    scale = HD ** (-0.5) * LOG2E

    @pl.when(step == 0)
    def _():
        acc[...] = jnp.zeros_like(acc)

    diff = (lax.broadcasted_iota(jnp.int32, (TQ, TQ), 1)
            - lax.broadcasted_iota(jnp.int32, (TQ, TQ), 0))

    def scores(sub, index, chunks, h):
        base = pl.multiple_of((index - (chunks - 1)) * TQ, TQ)
        query = q_ref[sub * TQ:(sub + 1) * TQ, h * HD:(h + 1) * HD]
        parts = []
        peak = None
        for c in range(chunks):
            s = lax.dot_general(
                k_ref[pl.ds(base + c * TQ, TQ), :], query, (((1,), (1,)), ((), ())),
                preferred_element_type=F32)
            off = (chunks - 1 - c) * TQ
            ok = None
            if c < 2:
                ok = diff < (window - off)
            if c == chunks - 1:
                ok = diff >= 0 if ok is None else ok & (diff >= 0)
            if ok is not None:
                s = jnp.where(ok, s, -1e30)
            parts.append(s)
            m = jnp.max(s, axis=0, keepdims=True)
            peak = m if peak is None else jnp.maximum(peak, m)
        return parts, peak

    def weigh(sub, index, h, parts, peak):
        shift = peak * scale
        total = None
        for c, s in enumerate(parts):
            e = jnp.exp2(s * scale - shift)
            t = jnp.sum(e, axis=0, keepdims=True)
            total = t if total is None else total + t
            p_scr[sub, c * TQ:(c + 1) * TQ, h * TQ:(h + 1) * TQ] = e.astype(BF)
        live = (index * TQ + lax.broadcasted_iota(jnp.int32, (1, TQ), 1)) < length
        inverse = jnp.where(live, 1.0 / total, 0.0)
        column = jnp.broadcast_to(inverse, (HD, TQ)).T
        grad = g_ref[sub * TQ:(sub + 1) * TQ, h * HD:(h + 1) * HD].astype(F32) * column
        g_scr[sub, h * TQ:(h + 1) * TQ, :] = grad.astype(BF)

    def spread(sub, index, chunks):
        base = pl.multiple_of((index - (chunks - 1)) * TQ, TQ)
        for c in range(chunks):
            acc[pl.ds(base + c * TQ, TQ), :] += jnp.dot(
                p_scr[sub, c * TQ:(c + 1) * TQ, :], g_scr[sub], preferred_element_type=F32)

    def pair(one, two):
        a, b = 2 * step, 2 * step + 1
        a0 = scores(0, a, one, 0)
        a1 = scores(0, a, one, 1)
        weigh(0, a, 0, *a0)
        b0 = scores(1, b, two, 0)
        weigh(0, a, 1, *a1)
        b1 = scores(1, b, two, 1)
        spread(0, a, one)
        weigh(1, b, 0, *b0)
        weigh(1, b, 1, *b1)
        spread(1, b, two)

    deep = (window + TQ - 2) // TQ
    want_a = jnp.minimum(2 * step, deep) + 1
    want_b = jnp.minimum(2 * step + 1, deep) + 1
    for one, two in ((1, 2), (2, 2), (3, 3), (3, 4), (4, 4)):
        @pl.when((2 * step * TQ < length) & (want_a == one) & (want_b == two))
        def _(one=one, two=two):
            pair(one, two)

    @pl.when(step == steps - 1)
    def _():
        part = tokens // 4
        for k in range(4):
            at = pl.multiple_of(lax.rem(x_id + k, 4) * part, part)
            outs[k][...] = acc[pl.ds(at, part), :].astype(BF)


def attention(scalars, queries, key_rows, out_grad, layers):
    slots, tokens = queries.shape[2], queries.shape[3]
    per_dev = queries.shape[4] // HD
    part = tokens // 4
    wide = per_dev * HD
    row_block = pl.BlockSpec((None, None, None, RB, wide), lambda j, i, *_: (0, 0, j, i, 0))
    key_block = pl.BlockSpec(
        (None, None, None, tokens, HD), lambda j, i, ids, *_: (0, 0, j, 0, ids[2]))
    out_block = pl.BlockSpec((None, part, HD), lambda j, i, *_: (j, 0, 0))
    return pl.pallas_call(
        functools.partial(attention_kernel, layers, tokens, per_dev),
        grid_spec=pltpu.PrefetchScalarGridSpec(
            num_scalar_prefetch=4,
            grid=(slots, tokens // RB),
            in_specs=[row_block, key_block, row_block],
            out_specs=[out_block] * 4,
            scratch_shapes=[
                pltpu.VMEM((tokens, HD), F32),
                pltpu.VMEM((2, tokens // 2 + TQ, per_dev * TQ), BF),
                pltpu.VMEM((2, per_dev * TQ, HD), BF),
            ],
        ),
        out_shape=[jax.ShapeDtypeStruct((slots, part, HD), BF)] * 4,
        compiler_params=pltpu.CompilerParams(vmem_limit_bytes=VMEM),
        cost_estimate=pl.CostEstimate(
            flops=36 * per_dev * 4 * TQ * TQ * HD, bytes_accessed=4 << 20,
            transcendentals=36 * per_dev * TQ * TQ),
        name="attention",
    )(*scalars, queries, key_rows, out_grad)


def grad_kernel(tokens, rows, ids, x_ref, *refs):
    pieces = refs[:4]
    out_ref, value, result = refs[-3:]
    core = lax.rem(ids[1], 2)
    y_id, x_id = ids[2], ids[3]
    part = tokens // 4
    for k in range(4):
        for i in range(4):
            y = lax.rem(y_id + 4 - jnp.where(core == 0, k, i), 4)
            x = lax.rem(x_id + 4 - jnp.where(core == 0, i, k), 4)
            at = pl.multiple_of(x * part, part)
            col = pl.multiple_of(y * HD, HD)
            value[pl.ds(at, part), pl.ds(col, HD)] = pieces[k][i]
    result[...] = lax.dot_general(
        x_ref[...], value[...], (((0,), (0,)), ((), ())), preferred_element_type=F32)
    for z in range(out_ref.shape[0]):
        out_ref[z] = result[z * rows:(z + 1) * rows, :].astype(BF)


def layer_grad(fixed, ids, normed, pieces, rows, earlier):
    slots, tokens, width = normed.shape[2:]
    group = width // rows
    part = tokens // 4
    out_block = pl.BlockSpec((group, None, rows, KVH * HD), lambda i, *_: (0, fixed, 0, 0))
    extra = [] if earlier is None else [earlier]
    return pl.pallas_call(
        functools.partial(grad_kernel, tokens, rows),
        grid_spec=pltpu.PrefetchScalarGridSpec(
            num_scalar_prefetch=1,
            grid=(1,),
            in_specs=[pl.BlockSpec((None, None, None, tokens, width),
                                   lambda i, *_: (0, 0, fixed, 0, 0))]
            + [pl.BlockSpec((4, part, HD), lambda i, *_: (0, 0, 0))] * 4
            + [pl.BlockSpec(memory_space=pl.ANY)] * len(extra),
            out_specs=out_block,
            scratch_shapes=[pltpu.VMEM((tokens, KVH * HD), BF),
                            pltpu.VMEM((width, KVH * HD), F32)],
        ),
        out_shape=jax.ShapeDtypeStruct((group, slots, rows, KVH * HD), BF),
        input_output_aliases={6: 0} if extra else {},
        compiler_params=pltpu.CompilerParams(vmem_limit_bytes=16 << 20),
        cost_estimate=pl.CostEstimate(
            flops=2 * tokens * width * KVH * HD, bytes_accessed=3 << 20, transcendentals=0),
        name="layer_grad%d" % fixed,
    )(ids, normed, *pieces, *extra)


def adam_kernel(reps, sections, layers, batch, lmap, arrived, master, one, two,
                new_master, new_one, new_two, send):
    step = pl.program_id(0)

    @pl.when(step == 0)
    def _():
        send[...] = jnp.zeros_like(send)

    for i in range(batch):
        layer = step * batch + i
        total = None
        places = []
        for r in range(reps):
            section = lmap[r, layer]
            first, _ = first_and_count(lmap, r, section, layers)
            slot = layer - first
            source = r * sections + section
            places.append((source, slot))
            term = arrived[source, slot].astype(F32)
            total = term if total is None else total + term
        mean = total / reps
        m1 = BETA_ONE * one[i] + (1.0 - BETA_ONE) * mean
        m2 = BETA_TWO * two[i] + (1.0 - BETA_TWO) * mean * mean
        move = m1 / CORRECT_ONE / (jnp.sqrt(m2 / CORRECT_TWO) + EPSILON)
        updated = master[i] - LEARN_RATE * (move + DECAY_RATE * master[i])
        new_master[i] = updated
        new_one[i] = m1
        new_two[i] = m2
        rounded = updated.astype(BF)
        for source, slot in places:
            send[source, slot] = rounded


def adam(lmap, arrived, master, one, two):
    layers, _, rows, wide = master.shape
    reps = lmap.shape[0]
    batch = layers // 2
    state = pl.BlockSpec((batch, None, rows, wide), lambda l, *_: (l, 0, 0, 0))
    whole = pl.BlockSpec(arrived.shape, lambda l, *_: (0, 0, 0, 0))
    f32 = jax.ShapeDtypeStruct(master.shape, F32)
    return pl.pallas_call(
        functools.partial(adam_kernel, reps, arrived.shape[0] // reps, layers, batch),
        grid_spec=pltpu.PrefetchScalarGridSpec(
            num_scalar_prefetch=1,
            grid=(layers // batch,),
            in_specs=[whole, state, state, state],
            out_specs=[state, state, state, whole],
        ),
        out_shape=[f32, f32, f32, jax.ShapeDtypeStruct(arrived.shape, BF)],
        compiler_params=pltpu.CompilerParams(vmem_limit_bytes=16 << 20),
        cost_estimate=pl.CostEstimate(flops=20 * master.size, bytes_accessed=4 << 20,
                                      transcendentals=master.size),
        name="adamw",
    )(lmap, arrived, master, one, two)


def place_kernel(arrived, out, sem):
    copies = []
    for i in range(arrived.shape[0]):
        for j in range(arrived.shape[1]):
            copies.append(pltpu.make_async_copy(
                arrived.at[i, j], out.at[j, i], sem.at[len(copies)]))
    for c in copies:
        c.start()
    for c in copies:
        c.wait()


def place(arrived):
    group, slots, rows, wide = arrived.shape
    return pl.pallas_call(
        place_kernel,
        in_specs=[pl.BlockSpec(memory_space=pl.ANY)],
        out_specs=pl.BlockSpec(memory_space=pl.ANY),
        scratch_shapes=[pltpu.SemaphoreType.DMA((group * slots,))],
        out_shape=jax.ShapeDtypeStruct((slots, group, rows, wide), BF),
        compiler_params=pltpu.CompilerParams(vmem_limit_bytes=4 << 20),
        cost_estimate=pl.CostEstimate(flops=0, bytes_accessed=2 << 20, transcendentals=0),
        name="place",
    )(arrived)


def shift(value, axis, by):
    n = lax.axis_size(axis)
    return lax.ppermute(value, axis, [(i, (i + by) % n) for i in range(n)])


def turn(value, by, along_x):
    pairs = []
    for core in range(2):
        for y in range(4):
            for x in range(4):
                if along_x == (core == 0):
                    to = (y, (x + by) % 4)
                else:
                    to = ((y + by) % 4, x)
                pairs.append(((core * 4 + y) * 4 + x, (core * 4 + to[0]) * 4 + to[1]))
    return lax.ppermute(value, ("core", "y", "x"), pairs)


def body(layer_section, token_count, window_size, normed_input, queries, key_rows, out_grad,
         master, moment_one, moment_two):
    layers = layer_section.shape[1]
    group_axes = ("rep", "z", "core")
    ids = jnp.stack([
        lax.axis_index("rep"), lax.axis_index(("z", "core")),
        lax.axis_index("y"), lax.axis_index("x")]).astype(jnp.int32)
    rows = master.shape[2]
    parts = attention((ids, layer_section, token_count, window_size),
                      queries, key_rows, out_grad, layers)
    total = parts[0].astype(F32)
    for k in range(1, 4):
        total = total + shift(parts[k], "x", k).astype(F32)
    block = total.astype(BF)
    near = [block] + [turn(block, k, True) for k in range(1, 4)]
    low, high = jnp.stack([n[0] for n in near]), jnp.stack([n[1] for n in near])
    low_up, high_down = turn(low, 1, False), turn(high, 3, False)
    high_up, low_down = turn(high, 1, False), turn(low, 3, False)
    low_far, high_far = turn(low_up, 1, False), turn(high_down, 3, False)
    grads = layer_grad(0, ids, normed_input, [low, low_up, low_far, low_down], rows, None)
    grads = layer_grad(1, ids, normed_input, [high, high_up, high_far, high_down], rows, grads)
    arrived = lax.all_to_all(grads, group_axes, 0, 0, tiled=True)
    updated, first, second, send = adam(
        layer_section, arrived, master, moment_one, moment_two)
    weights = place(lax.all_to_all(send, group_axes, 0, 0, tiled=True))
    weights = weights.reshape(weights.shape[0], -1, weights.shape[3])
    return updated, first, second, weights[None, None]


def solution(mesh):
    reps, sections, tps = mesh.devices.shape
    fine = Mesh(mesh.devices.reshape(reps, 2, sections // 2, 4, tps // 4),
                ("rep", "z", "core", "y", "x"))
    section, tp = ("z", "core"), ("y", "x")
    wide = P("rep", section, None, None, tp)
    state = P(None, tp, ("rep",) + section, None)
    in_specs = (P(), P(), P(), wide, wide, P("rep", section, None, None, None), wide,
                state, state, state)
    out_specs = (state, state, state, P("rep", section, None, tp, None))
    return jax.shard_map(body, mesh=fine, in_specs=in_specs, out_specs=out_specs, check_vma=False)
```

time: 156 us -> 122 us (0.78); the launches traced: 154 us -> 122 us
  Pallas kernels: 24.4 us -> 13.8 us
  blocking collectives: 73.1 us -> 63.4 us
  waiting for transfers between devices: 30.9 us -> 25.1 us
  other arithmetic: 4.89 us -> 1.79 us
  local copies, waits for them, and re-layouts: 1.74 us -> 0.09 us
    all_to_all x1 -> x0, waiting for transfers between devices: 23.5 us -> none  [body(): lax.all_to_all(jnp.stack([own, shift(other, 'core', 1)], axis=1), chip_ax...]
    ppermute x0 -> x9, waiting for transfers between devices: none -> 16.7 us  [turn(): return lax.ppermute(value, ('core', 'y', 'x'), pairs)]
    ppermute x0 -> x9, starting transfers between devices: none -> 11.5 us  [turn(): return lax.ppermute(value, ('core', 'y', 'x'), pairs)]
    all_to_all x2, blocking collectives: 73.1 us -> 63.4 us  [the longest x1 37.8 us: body(): arrived = lax.all_to_all(grads, group_axes, 0, 0, tiled=True)]
    ppermute x5 -> x3, starting transfers between devices: 14.8 us -> 5.72 us  [shift(): return lax.ppermute(value, axis, [(i, (i + by) % n) for i in range(n)])]
    pallas_call x1, Pallas kernels: 13.4 us -> 7.54 us  [attention(): pl.pallas_call(functools.partial(attention_kernel, layers, tokens, per_de...]
    pallas_call x2 -> x4, Pallas kernels: 11 us -> 6.26 us  [the longest x2 3.27 us: layer_grad(): pl.pallas_call(functools.partial(grad_kernel, tokens, rows), grid_spec=pl...]
    all_to_all x1 -> x0, starting transfers between devices: 3.55 us -> none  [body(): lax.all_to_all(jnp.stack([own, shift(other, 'core', 1)], axis=1), chip_ax...]
  transfers between devices with their start and end apart: 6 -> 12, of which waited for: 5 -> 8; matrix products, arithmetic and copies ran while one was open for 0% -> 0% of each run, Pallas kernels for 0% -> 1%
where the time goes in v2:
time: 122 us
  blocking collectives  63.4 us (52%)
  waiting for transfers between devices  25.1 us (21%)
  starting transfers between devices  17.2 us (14%)
  Pallas kernels  13.8 us (11%)
  other arithmetic  1.79 us (1%)
    all_to_all x1, blocking collectives, body(): arrived = lax.all_to_all(grads, group_axes, 0, 0, tiled=True)  37.8 us
    all_to_all x1, blocking collectives, body(): weights = place(lax.all_to_all(send, group_axes, 0, 0, tiled=True))  25.6 us
    ppermute x9, waiting for transfers between devices, turn(): return lax.ppermute(value, ('core', 'y', 'x'), pairs)  16.7 us
    ppermute x9, starting transfers between devices, turn(): return lax.ppermute(value, ('core', 'y', 'x'), pairs)  11.5 us
    ppermute x3, waiting for transfers between devices, shift(): return lax.ppermute(value, axis, [(i, (i + by) % n) for i in range(n)])  8.34 us
    pallas_call x1, Pallas kernels, attention(): pl.pallas_call(functools.partial(attention_kernel, layers, tokens, per_de...  7.54 us
    ppermute x3, starting transfers between devices, shift(): return lax.ppermute(value, axis, [(i, (i + by) % n) for i in range(n)])  5.72 us
    pallas_call x2, Pallas kernels, layer_grad(): pl.pallas_call(functools.partial(grad_kernel, tokens, rows), grid_spec=pl...  3.27 us
  transfers between devices with their start and end apart: 12, of which 8 were waited for; matrix products, arithmetic and copies ran while one was open for 0% of the time, Pallas kernels for 1%

profile of v2, /device:TPU:1, one launch (start us, length us, event | category | flops | bytes accessed | tf_op | source)
XLA Modules:
  0.0 122.3 jit_solution(16337535516021388073)
XLA Ops:
  1.3 7.5 %attention.1 = (bf16[2,384,128]{2,1,0:T(8,128)(2,1)}, bf16[2,384,128]{2,1,0:T(8,128)(2,1)}, bf16[2,384,128]{2,1,0:T(8,128)(2,1)}, bf16[2,384,128]{2,1,0:T(8,128)(2,1)}) custom-call(s32[4]{0:T(128)} %pad_add_fusion.ids, s32[4,6]{1,0:T(4,128)} %lmap.3, s32[4]{0:T(128)} %counts.1, s32[6]{0:T(128)} %windows.1, bf16[1,1,2,1536,256]{4,3,2,1,0:T(8,128)(2,1)} %q_ref.1, ...), custom_call_target="tpu_custom_call" | custom-call | flops 2415919104 | bytes 4194304 | tf_op jit(solution)/shard_map/attention/pallas_call | solution.py:139
  8.8 2.1 %collective-permute-start = (bf16[2,384,128]{2,1,0:T(8,128)(2,1)}, bf16[2,384,128]{2,1,0:T(8,128)(2,1)S(1)}, u32[]{:S(2)}, u32[]{:S(2)}) collective-permute-start(bf16[2,384,128]{2,1,0:T(8,128)(2,1)} %get-tuple-element.13), channel_id=1, source_target_pairs={{0,1},{1,2},{2,3},{3,0},{4,5},{5,6},{6,7},{7,4},{8,9},{9,10},{10,1... | collective-permute-start | bytes 589832 | tf_op jit(solution)/shard_map/ppermute | solution.py:292
  11.0 2.5 %collective-permute-start.1 = (bf16[2,384,128]{2,1,0:T(8,128)(2,1)}, bf16[2,384,128]{2,1,0:T(8,128)(2,1)S(1)}, u32[]{:S(2)}, u32[]{:S(2)}) collective-permute-start(bf16[2,384,128]{2,1,0:T(8,128)(2,1)} %get-tuple-element.14), channel_id=1, source_target_pairs={{0,2},{1,3},{2,0},{3,1},{4,6},{5,7},{6,4},{7,5},{8,10},{9,11},{10,... | collective-permute-start | bytes 589832 | tf_op jit(solution)/shard_map/ppermute | solution.py:292
  13.4 1.1 collective-permute-start.2
  14.6 0.9 collective-permute-done
  15.5 7.4 %collective-permute-done.1 = bf16[2,384,128]{2,1,0:T(8,128)(2,1)S(1)} collective-permute-done((bf16[2,384,128]{2,1,0:T(8,128)(2,1)}, bf16[2,384,128]{2,1,0:T(8,128)(2,1)S(1)}, u32[]{:S(2)}, u32[]{:S(2)}) %collective-permute-start.1) | collective-permute-done | bytes 196640 | tf_op jit(solution)/shard_map/ppermute | solution.py:292
  22.9 1.0 add_convert_fusion
  23.9 1.4 %collective-permute-start.3 = (bf16[2,384,128]{2,1,0:T(8,128)(2,1)S(1)}, bf16[2,384,128]{2,1,0:T(8,128)(2,1)S(1)}, u32[]{:S(2)}, u32[]{:S(2)}) collective-permute-start(bf16[2,384,128]{2,1,0:T(8,128)(2,1)S(1)} %add_convert_fusion), channel_id=1, source_target_pairs={{0,1},{1,2},{2,3},{3,0},{4,5},{5,6},{6,7},{7,4},{8,9},{9,10},{10,1... | collective-permute-start | bytes 589832 | tf_op jit(solution)/shard_map/ppermute | solution.py:305
  25.3 2.6 %collective-permute-start.4 = (bf16[2,384,128]{2,1,0:T(8,128)(2,1)S(1)}, bf16[2,384,128]{2,1,0:T(8,128)(2,1)S(1)}, u32[]{:S(2)}, u32[]{:S(2)}) collective-permute-start(bf16[2,384,128]{2,1,0:T(8,128)(2,1)S(1)} %add_convert_fusion), channel_id=1, source_target_pairs={{0,2},{1,3},{2,0},{3,1},{4,6},{5,7},{6,4},{7,5},{8,10},{9,11},{10,... | collective-permute-start | bytes 589832 | tf_op jit(solution)/shard_map/ppermute | solution.py:305
  27.9 1.1 collective-permute-start.5
  29.0 1.1 collective-permute-done.3
  30.1 3.3 %collective-permute-done.4 = bf16[2,384,128]{2,1,0:T(8,128)(2,1)S(1)} collective-permute-done((bf16[2,384,128]{2,1,0:T(8,128)(2,1)S(1)}, bf16[2,384,128]{2,1,0:T(8,128)(2,1)S(1)}, u32[]{:S(2)}, u32[]{:S(2)}) %collective-permute-start.4) | collective-permute-done | bytes 196640 | tf_op jit(solution)/shard_map/ppermute | solution.py:305
  34.0 2.4 %collective-permute-start.7 = (bf16[4,384,128]{2,1,0:T(8,128)(2,1)S(1)}, bf16[4,384,128]{2,1,0:T(8,128)(2,1)S(1)}, u32[]{:S(2)}, u32[]{:S(2)}) collective-permute-start(bf16[4,384,128]{2,1,0:T(8,128)(2,1)S(1)} %pad_maximum_fusion.refs_0_), channel_id=1, source_target_pairs={{0,12},{1,13},{2,14},{3,15},{4,0},{5,1},{6,2},{7,3},{8,4},{9,5},{1... | collective-permute-start | bytes 1179656 | tf_op jit(solution)/shard_map/ppermute | solution.py:305
  37.2 4.5 %collective-permute-done.9.refs_1_ = bf16[4,384,128]{2,1,0:T(8,128)(2,1)S(1)} collective-permute-done((bf16[4,384,128]{2,1,0:T(8,128)(2,1)S(1)}, bf16[4,384,128]{2,1,0:T(8,128)(2,1)S(1)}, u32[]{:S(2)}, u32[]{:S(2)}) %collective-permute-start.9) | collective-permute-done | bytes 393248 | tf_op jit(solution)/shard_map/ppermute | solution.py:305
  41.9 2.6 %collective-permute-start.8 = (bf16[4,384,128]{2,1,0:T(8,128)(2,1)S(1)}, bf16[4,384,128]{2,1,0:T(8,128)(2,1)S(1)}, u32[]{:S(2)}, u32[]{:S(2)}) collective-permute-start(bf16[4,384,128]{2,1,0:T(8,128)(2,1)S(1)} %collective-permute-done.7.refs_3_), channel_id=1, source_target_pairs={{0,12},{1,13},{2,14},{3,15},{4,0},{5,1},{6,2},{7,3},{8,4},{9,5},{1... | collective-permute-start | bytes 1179656 | tf_op jit(solution)/shard_map/ppermute | solution.py:305
  44.5 0.8 collective-permute-done.11.refs_3_
  45.3 4.5 %collective-permute-done.10.refs_2_ = bf16[4,384,128]{2,1,0:T(8,128)(2,1)S(1)} collective-permute-done((bf16[4,384,128]{2,1,0:T(8,128)(2,1)S(1)}, bf16[4,384,128]{2,1,0:T(8,128)(2,1)S(1)}, u32[]{:S(2)}, u32[]{:S(2)}) %collective-permute-start.10) | collective-permute-done | bytes 393248 | tf_op jit(solution)/shard_map/ppermute | solution.py:305
  49.8 1.6 %layer_grad0.1.refs_4_ = bf16[16,2,24,512]{3,2,1,0:T(8,128)(2,1)S(1)} custom-call(s32[4]{0:T(128)S(1)} %copy-done.4, bf16[1,1,2,1536,384]{4,3,2,1,0:T(8,128)(2,1)S(1)} %copy-done, bf16[4,384,128]{2,1,0:T(8,128)(2,1)S(1)} %pad_maximum_fusion.1.refs_0_, bf16[4,384,128]{2,1,0:T(8,128)(2,1)S(1)} %collective-permute-done.9.refs_1_, ...), custom_call_target="tpu_custom_call" | custom-call | flops 603979776 | bytes 3145728 | tf_op jit(solution)/shard_map/layer_grad0/pallas_call | solution.py:186
  51.5 2.5 %collective-permute-done.6.refs_1_ = bf16[4,384,128]{2,1,0:T(8,128)(2,1)S(1)} collective-permute-done((bf16[4,384,128]{2,1,0:T(8,128)(2,1)S(1)}, bf16[4,384,128]{2,1,0:T(8,128)(2,1)S(1)}, u32[]{:S(2)}, u32[]{:S(2)}) %collective-permute-start.6) | collective-permute-done | bytes 393248 | tf_op jit(solution)/shard_map/ppermute | solution.py:305
  54.1 1.6 %layer_grad1.1 = bf16[16,2,24,512]{3,2,1,0:T(8,128)(2,1)S(1)} custom-call(s32[4]{0:T(128)S(1)} %copy-done.4, bf16[1,1,2,1536,384]{4,3,2,1,0:T(8,128)(2,1)S(1)} %copy-done, bf16[4,384,128]{2,1,0:T(8,128)(2,1)S(1)} %pad_maximum_fusion.refs_0_, bf16[4,384,128]{2,1,0:T(8,128)(2,1)S(1)} %collective-permute-done.6.refs_1_, ...), custom_call_target="tpu_custom_call", output_to_operand_aliasing={{}: (6, {})} | custom-call | flops 603979776 | bytes 3145728 | tf_op jit(solution)/shard_map/layer_grad1/pallas_call | solution.py:186
  55.7 37.8 %all_to_all.10.arrived = bf16[16,2,24,512]{3,2,1,0:T(8,128)(2,1)S(1)} all-to-all(bf16[16,2,24,512]{3,2,1,0:T(8,128)(2,1)S(1)} %layer_grad1.1), channel_id=1, replica_groups=mesh['rep'=4,'z'=2,'core'=2,'y'=4,'x'=4] {'rep','z','core'}, dimensions={0} | all-to-all | bytes 1572864 | tf_op jit(solution)/shard_map/all_to_all | solution.py:329
  93.5 1.8 %adamw.1 = (f32[6,1,24,512]{3,2,1,0:T(8,128)}, f32[6,1,24,512]{3,2,1,0:T(8,128)}, f32[6,1,24,512]{3,2,1,0:T(8,128)}, bf16[16,2,24,512]{3,2,1,0:T(8,128)(2,1)S(1)}) custom-call(s32[4,6]{1,0:T(4,128)S(1)} %copy-done.5, bf16[16,2,24,512]{3,2,1,0:T(8,128)(2,1)S(1)} %all_to_all.10.arrived, f32[6,1,24,512]{3,2,1,0:T(8,128)S(1)} %copy-done.1, ...), custom_call_target="tpu_custom_call" | custom-call | flops 1474560 | bytes 4194304 | tf_op jit(solution)/shard_map/adamw/pallas_call | solution.py:248
  95.4 25.6 %all_to_all.11.arrived = bf16[16,2,24,512]{3,2,1,0:T(8,128)(2,1)S(1)} all-to-all(bf16[16,2,24,512]{3,2,1,0:T(8,128)(2,1)S(1)} %get-tuple-element.19), channel_id=1, replica_groups=mesh['rep'=4,'z'=2,'core'=2,'y'=4,'x'=4] {'rep','z','core'}, dimensions={0} | all-to-all | bytes 1572864 | tf_op jit(solution)/shard_map/all_to_all | solution.py:332
  121.0 1.1 place.1
  (27 shorter events, 2.3 us)
Async XLA Ops:
  8.8 41.0 %copy-start = (bf16[1,1,2,1536,384]{4,3,2,1,0:T(8,128)(2,1)S(1)}, bf16[1,1,2,1536,384]{4,3,2,1,0:T(8,128)(2,1)}, u32[]{:S(2)}) copy-start(bf16[1,1,2,1536,384]{4,3,2,1,0:T(8,128)(2,1)} %x_ref.3) | copy-start | bytes 7077892
  8.8 41.0 %copy-start.4 = (s32[4]{0:T(128)S(1)}, s32[4]{0:T(128)}, u32[]{:S(2)}) copy-start(s32[4]{0:T(128)} %pad_add_fusion.ids) | copy-start | bytes 52
  8.8 6.7 %collective-permute-start = (bf16[2,384,128]{2,1,0:T(8,128)(2,1)}, bf16[2,384,128]{2,1,0:T(8,128)(2,1)S(1)}, u32[]{:S(2)}, u32[]{:S(2)}) collective-permute-start(bf16[2,384,128]{2,1,0:T(8,128)(2,1)} %get-tuple-element.13), channel_id=1, source_target_pairs={{0,1},{1,2},{2,3},{3,0},{4,5},{5,6},{6,7},{7,4},{8,9},{9,10},{10,1... | collective-permute-start | bytes 589832 | tf_op jit(solution)/shard_map/ppermute | solution.py:292
  11.0 11.9 %collective-permute-start.1 = (bf16[2,384,128]{2,1,0:T(8,128)(2,1)}, bf16[2,384,128]{2,1,0:T(8,128)(2,1)S(1)}, u32[]{:S(2)}, u32[]{:S(2)}) collective-permute-start(bf16[2,384,128]{2,1,0:T(8,128)(2,1)} %get-tuple-element.14), channel_id=1, source_target_pairs={{0,2},{1,3},{2,0},{3,1},{4,6},{5,7},{6,4},{7,5},{8,10},{9,11},{10,... | collective-permute-start | bytes 589832 | tf_op jit(solution)/shard_map/ppermute | solution.py:292
  13.4 9.5 %collective-permute-start.2 = (bf16[2,384,128]{2,1,0:T(8,128)(2,1)}, bf16[2,384,128]{2,1,0:T(8,128)(2,1)S(1)}, u32[]{:S(2)}, u32[]{:S(2)}) collective-permute-start(bf16[2,384,128]{2,1,0:T(8,128)(2,1)} %get-tuple-element.15), channel_id=1, source_target_pairs={{0,3},{1,0},{2,1},{3,2},{4,7},{5,4},{6,5},{7,6},{8,11},{9,8},{10,9... | collective-permute-start | bytes 589832 | tf_op jit(solution)/shard_map/ppermute | solution.py:292
  23.9 6.2 %collective-permute-start.3 = (bf16[2,384,128]{2,1,0:T(8,128)(2,1)S(1)}, bf16[2,384,128]{2,1,0:T(8,128)(2,1)S(1)}, u32[]{:S(2)}, u32[]{:S(2)}) collective-permute-start(bf16[2,384,128]{2,1,0:T(8,128)(2,1)S(1)} %add_convert_fusion), channel_id=1, source_target_pairs={{0,1},{1,2},{2,3},{3,0},{4,5},{5,6},{6,7},{7,4},{8,9},{9,10},{10,1... | collective-permute-start | bytes 589832 | tf_op jit(solution)/shard_map/ppermute | solution.py:305
  25.3 8.1 %collective-permute-start.4 = (bf16[2,384,128]{2,1,0:T(8,128)(2,1)S(1)}, bf16[2,384,128]{2,1,0:T(8,128)(2,1)S(1)}, u32[]{:S(2)}, u32[]{:S(2)}) collective-permute-start(bf16[2,384,128]{2,1,0:T(8,128)(2,1)S(1)} %add_convert_fusion), channel_id=1, source_target_pairs={{0,2},{1,3},{2,0},{3,1},{4,6},{5,7},{6,4},{7,5},{8,10},{9,11},{10,... | collective-permute-start | bytes 589832 | tf_op jit(solution)/shard_map/ppermute | solution.py:305
  27.9 5.5 %collective-permute-start.5 = (bf16[2,384,128]{2,1,0:T(8,128)(2,1)S(1)}, bf16[2,384,128]{2,1,0:T(8,128)(2,1)S(1)}, u32[]{:S(2)}, u32[]{:S(2)}) collective-permute-start(bf16[2,384,128]{2,1,0:T(8,128)(2,1)S(1)} %add_convert_fusion), channel_id=1, source_target_pairs={{0,3},{1,0},{2,1},{3,2},{4,7},{5,4},{6,5},{7,6},{8,11},{9,8},{10,9... | collective-permute-start | bytes 589832 | tf_op jit(solution)/shard_map/ppermute | solution.py:305
  33.5 8.2 %collective-permute-start.9 = (bf16[4,384,128]{2,1,0:T(8,128)(2,1)S(1)}, bf16[4,384,128]{2,1,0:T(8,128)(2,1)S(1)}, u32[]{:S(2)}, u32[]{:S(2)}) collective-permute-start(bf16[4,384,128]{2,1,0:T(8,128)(2,1)S(1)} %pad_maximum_fusion.1.refs_0_), channel_id=1, source_target_pairs={{0,4},{1,5},{2,6},{3,7},{4,8},{5,9},{6,10},{7,11},{8,12},{9,13},{1... | collective-permute-start | bytes 1179656 | tf_op jit(solution)/shard_map/ppermute | solution.py:305
  34.0 7.9 %collective-permute-start.7 = (bf16[4,384,128]{2,1,0:T(8,128)(2,1)S(1)}, bf16[4,384,128]{2,1,0:T(8,128)(2,1)S(1)}, u32[]{:S(2)}, u32[]{:S(2)}) collective-permute-start(bf16[4,384,128]{2,1,0:T(8,128)(2,1)S(1)} %pad_maximum_fusion.refs_0_), channel_id=1, source_target_pairs={{0,12},{1,13},{2,14},{3,15},{4,0},{5,1},{6,2},{7,3},{8,4},{9,5},{1... | collective-permute-start | bytes 1179656 | tf_op jit(solution)/shard_map/ppermute | solution.py:305
  36.4 8.9 %collective-permute-start.11 = (bf16[4,384,128]{2,1,0:T(8,128)(2,1)S(1)}, bf16[4,384,128]{2,1,0:T(8,128)(2,1)S(1)}, u32[]{:S(2)}, u32[]{:S(2)}) collective-permute-start(bf16[4,384,128]{2,1,0:T(8,128)(2,1)S(1)} %pad_maximum_fusion.1.refs_0_), channel_id=1, source_target_pairs={{0,12},{1,13},{2,14},{3,15},{4,0},{5,1},{6,2},{7,3},{8,4},{9,5},{1... | collective-permute-start | bytes 1179656 | tf_op jit(solution)/shard_map/ppermute | solution.py:305
  41.7 8.1 %collective-permute-start.10 = (bf16[4,384,128]{2,1,0:T(8,128)(2,1)S(1)}, bf16[4,384,128]{2,1,0:T(8,128)(2,1)S(1)}, u32[]{:S(2)}, u32[]{:S(2)}) collective-permute-start(bf16[4,384,128]{2,1,0:T(8,128)(2,1)S(1)} %collective-permute-done.9.refs_1_), channel_id=1, source_target_pairs={{0,4},{1,5},{2,6},{3,7},{4,8},{5,9},{6,10},{7,11},{8,12},{9,13},{1... | collective-permute-start | bytes 1179656 | tf_op jit(solution)/shard_map/ppermute | solution.py:305
  41.7 12.3 %collective-permute-start.6 = (bf16[4,384,128]{2,1,0:T(8,128)(2,1)S(1)}, bf16[4,384,128]{2,1,0:T(8,128)(2,1)S(1)}, u32[]{:S(2)}, u32[]{:S(2)}) collective-permute-start(bf16[4,384,128]{2,1,0:T(8,128)(2,1)S(1)} %pad_maximum_fusion.refs_0_), channel_id=1, source_target_pairs={{0,4},{1,5},{2,6},{3,7},{4,8},{5,9},{6,10},{7,11},{8,12},{9,13},{1... | collective-permute-start | bytes 1179656 | tf_op jit(solution)/shard_map/ppermute | solution.py:305
  41.9 12.1 %collective-permute-start.8 = (bf16[4,384,128]{2,1,0:T(8,128)(2,1)S(1)}, bf16[4,384,128]{2,1,0:T(8,128)(2,1)S(1)}, u32[]{:S(2)}, u32[]{:S(2)}) collective-permute-start(bf16[4,384,128]{2,1,0:T(8,128)(2,1)S(1)} %collective-permute-done.7.refs_3_), channel_id=1, source_target_pairs={{0,12},{1,13},{2,14},{3,15},{4,0},{5,1},{6,2},{7,3},{8,4},{9,5},{1... | collective-permute-start | bytes 1179656 | tf_op jit(solution)/shard_map/ppermute | solution.py:305
  51.5 42.0 %copy-start.1 = (f32[6,1,24,512]{3,2,1,0:T(8,128)S(1)}, f32[6,1,24,512]{3,2,1,0:T(8,128)}, u32[]{:S(2)}) copy-start(f32[6,1,24,512]{3,2,1,0:T(8,128)} %master.1) | copy-start | bytes 884740
  51.5 42.0 %copy-start.2 = (f32[6,1,24,512]{3,2,1,0:T(8,128)S(1)}, f32[6,1,24,512]{3,2,1,0:T(8,128)}, u32[]{:S(2)}) copy-start(f32[6,1,24,512]{3,2,1,0:T(8,128)} %one.1) | copy-start | bytes 884740
  51.5 42.0 %copy-start.3 = (f32[6,1,24,512]{3,2,1,0:T(8,128)S(1)}, f32[6,1,24,512]{3,2,1,0:T(8,128)}, u32[]{:S(2)}) copy-start(f32[6,1,24,512]{3,2,1,0:T(8,128)} %two.1) | copy-start | bytes 884740
  51.5 42.0 %copy-start.5 = (s32[4,6]{1,0:T(4,128)S(1)}, s32[4,6]{1,0:T(4,128)}, u32[]{:S(2)}) copy-start(s32[4,6]{1,0:T(4,128)} %lmap.3) | copy-start | bytes 292

commit v3 on v2

--- a/solution.py
+++ b/solution.py
@@ -19,10 +19,14 @@
 CORRECT_TWO = 0.994079470779667
 LOG2E = 1.4426950408889634
 TQ = 256
-RB = 512
+RB = 1536
 VMEM = 60 << 20
 BF = jnp.bfloat16
 F32 = jnp.float32
+
+
+def section_index():
+    return 2 * lax.axis_index("z") + lax.axis_index("core")
 
 
 def first_and_count(map_ref, replica, section, layers):
@@ -35,13 +39,13 @@
     return first, count
 
 
-def attention_kernel(layers, tokens, per_dev, ids, lmap, counts, windows,
+def attention_kernel(layers, tokens, per_dev, lmap, counts, windows,
                      q_ref, k_ref, g_ref, *rest):
     outs = rest[:4]
     acc, p_scr, g_scr = rest[4:]
     slot, step = pl.program_id(0), pl.program_id(1)
     steps = pl.num_programs(1)
-    replica, section, x_id = ids[0], ids[1], ids[3]
+    replica, section, x_id = lax.axis_index("rep"), section_index(), lax.axis_index("x")
     first, held = first_and_count(lmap, replica, section, layers)
     layer = jnp.minimum(first + slot, layers - 1)
     window = windows[layer]
@@ -98,26 +102,40 @@
             acc[pl.ds(base + c * TQ, TQ), :] += jnp.dot(
                 p_scr[sub, c * TQ:(c + 1) * TQ, :], g_scr[sub], preferred_element_type=F32)
 
-    def pair(one, two):
-        a, b = 2 * step, 2 * step + 1
-        a0 = scores(0, a, one, 0)
-        a1 = scores(0, a, one, 1)
-        weigh(0, a, 0, *a0)
-        b0 = scores(1, b, two, 0)
-        weigh(0, a, 1, *a1)
-        b1 = scores(1, b, two, 1)
-        spread(0, a, one)
-        weigh(1, b, 0, *b0)
-        weigh(1, b, 1, *b1)
-        spread(1, b, two)
+    def run(counts):
+        units = [(sub, h) for sub in range(len(counts)) for h in range(per_dev)]
+        ready = {}
+        late = []
+
+        def score(u):
+            if u < len(units):
+                sub, h = units[u]
+                ready[u] = scores(sub, len(counts) * step + sub, counts[sub], h)
+
+        for u in range(2):
+            score(u)
+        for u, (sub, h) in enumerate(units):
+            score(u + 2)
+            for wait in [w for w in late if w[0] <= u]:
+                spread(wait[1], len(counts) * step + wait[1], counts[wait[1]])
+                late.remove(wait)
+            weigh(sub, len(counts) * step + sub, h, *ready.pop(u))
+            if h == per_dev - 1:
+                late.append((u + 2, sub))
+        for wait in late:
+            spread(wait[1], len(counts) * step + wait[1], counts[wait[1]])
 
     deep = (window + TQ - 2) // TQ
-    want_a = jnp.minimum(2 * step, deep) + 1
-    want_b = jnp.minimum(2 * step + 1, deep) + 1
-    for one, two in ((1, 2), (2, 2), (3, 3), (3, 4), (4, 4)):
-        @pl.when((2 * step * TQ < length) & (want_a == one) & (want_b == two))
-        def _(one=one, two=two):
-            pair(one, two)
+    blocks = RB // TQ
+    want = [jnp.minimum(blocks * step + i, deep) + 1 for i in range(blocks)]
+    for counts in ((1, 2, 2, 2, 2, 2), (1, 2, 3, 3, 3, 3), (1, 2, 3, 4, 4, 4)):
+        match = blocks * step * TQ < length
+        for w, c in zip(want, counts):
+            match = match & (w == c)
+
+        @pl.when(match)
+        def _(counts=counts):
+            run(counts)
 
     @pl.when(step == steps - 1)
     def _():
@@ -134,19 +152,19 @@
     wide = per_dev * HD
     row_block = pl.BlockSpec((None, None, None, RB, wide), lambda j, i, *_: (0, 0, j, i, 0))
     key_block = pl.BlockSpec(
-        (None, None, None, tokens, HD), lambda j, i, ids, *_: (0, 0, j, 0, ids[2]))
+        (None, None, None, tokens, HD), lambda j, i, *_: (0, 0, j, 0, lax.axis_index("y")))
     out_block = pl.BlockSpec((None, part, HD), lambda j, i, *_: (j, 0, 0))
     return pl.pallas_call(
         functools.partial(attention_kernel, layers, tokens, per_dev),
         grid_spec=pltpu.PrefetchScalarGridSpec(
-            num_scalar_prefetch=4,
+            num_scalar_prefetch=3,
             grid=(slots, tokens // RB),
             in_specs=[row_block, key_block, row_block],
             out_specs=[out_block] * 4,
             scratch_shapes=[
                 pltpu.VMEM((tokens, HD), F32),
-                pltpu.VMEM((2, tokens // 2 + TQ, per_dev * TQ), BF),
-                pltpu.VMEM((2, per_dev * TQ, HD), BF),
+                pltpu.VMEM((6, tokens // 2 + TQ, per_dev * TQ), BF),
+                pltpu.VMEM((6, per_dev * TQ, HD), BF),
             ],
         ),
         out_shape=[jax.ShapeDtypeStruct((slots, part, HD), BF)] * 4,
@@ -158,51 +176,50 @@
     )(*scalars, queries, key_rows, out_grad)
 
 
-def grad_kernel(tokens, rows, ids, x_ref, *refs):
-    pieces = refs[:4]
+def grad_kernel(tokens, rows, x_ref, *refs):
     out_ref, value, result = refs[-3:]
-    core = lax.rem(ids[1], 2)
-    y_id, x_id = ids[2], ids[3]
+    core, y_id, x_id = (lax.axis_index(n) for n in ("core", "y", "x"))
     part = tokens // 4
-    for k in range(4):
-        for i in range(4):
-            y = lax.rem(y_id + 4 - jnp.where(core == 0, k, i), 4)
-            x = lax.rem(x_id + 4 - jnp.where(core == 0, i, k), 4)
-            at = pl.multiple_of(x * part, part)
-            col = pl.multiple_of(y * HD, HD)
-            value[pl.ds(at, part), pl.ds(col, HD)] = pieces[k][i]
+    for slot in range(2):
+        @pl.when(pl.program_id(0) == slot)
+        def _(pieces=refs[4 * slot:4 * slot + 4]):
+            for k in range(4):
+                for i in range(4):
+                    y = lax.rem(y_id + 4 - jnp.where(core == 0, k, i), 4)
+                    x = lax.rem(x_id + 4 - jnp.where(core == 0, i, k), 4)
+                    at = pl.multiple_of(x * part, part)
+                    col = pl.multiple_of(y * HD, HD)
+                    value[pl.ds(at, part), pl.ds(col, HD)] = pieces[k][i]
+
     result[...] = lax.dot_general(
         x_ref[...], value[...], (((0,), (0,)), ((), ())), preferred_element_type=F32)
     for z in range(out_ref.shape[0]):
         out_ref[z] = result[z * rows:(z + 1) * rows, :].astype(BF)
 
 
-def layer_grad(fixed, ids, normed, pieces, rows, earlier):
+def layer_grads(normed, low, high, rows):
     slots, tokens, width = normed.shape[2:]
     group = width // rows
     part = tokens // 4
-    out_block = pl.BlockSpec((group, None, rows, KVH * HD), lambda i, *_: (0, fixed, 0, 0))
-    extra = [] if earlier is None else [earlier]
+    out_block = pl.BlockSpec((group, None, rows, KVH * HD), lambda j, *_: (0, j, 0, 0))
     return pl.pallas_call(
         functools.partial(grad_kernel, tokens, rows),
         grid_spec=pltpu.PrefetchScalarGridSpec(
-            num_scalar_prefetch=1,
-            grid=(1,),
+            num_scalar_prefetch=0,
+            grid=(slots,),
             in_specs=[pl.BlockSpec((None, None, None, tokens, width),
-                                   lambda i, *_: (0, 0, fixed, 0, 0))]
-            + [pl.BlockSpec((4, part, HD), lambda i, *_: (0, 0, 0))] * 4
-            + [pl.BlockSpec(memory_space=pl.ANY)] * len(extra),
+                                   lambda j, *_: (0, 0, j, 0, 0))]
+            + [pl.BlockSpec((4, part, HD), lambda j, *_: (0, 0, 0))] * 8,
             out_specs=out_block,
             scratch_shapes=[pltpu.VMEM((tokens, KVH * HD), BF),
                             pltpu.VMEM((width, KVH * HD), F32)],
         ),
         out_shape=jax.ShapeDtypeStruct((group, slots, rows, KVH * HD), BF),
-        input_output_aliases={6: 0} if extra else {},
         compiler_params=pltpu.CompilerParams(vmem_limit_bytes=16 << 20),
         cost_estimate=pl.CostEstimate(
-            flops=2 * tokens * width * KVH * HD, bytes_accessed=3 << 20, transcendentals=0),
-        name="layer_grad%d" % fixed,
-    )(ids, normed, *pieces, *extra)
+            flops=4 * tokens * width * KVH * HD, bytes_accessed=6 << 20, transcendentals=0),
+        name="layer_grads",
+    )(normed, *low, *high)
 
 
 def adam_kernel(reps, sections, layers, batch, lmap, arrived, master, one, two,
@@ -309,11 +326,8 @@
          master, moment_one, moment_two):
     layers = layer_section.shape[1]
     group_axes = ("rep", "z", "core")
-    ids = jnp.stack([
-        lax.axis_index("rep"), lax.axis_index(("z", "core")),
-        lax.axis_index("y"), lax.axis_index("x")]).astype(jnp.int32)
     rows = master.shape[2]
-    parts = attention((ids, layer_section, token_count, window_size),
+    parts = attention((layer_section, token_count, window_size),
                       queries, key_rows, out_grad, layers)
     total = parts[0].astype(F32)
     for k in range(1, 4):
@@ -324,8 +338,8 @@
     low_up, high_down = turn(low, 1, False), turn(high, 3, False)
     high_up, low_down = turn(high, 1, False), turn(low, 3, False)
     low_far, high_far = turn(low_up, 1, False), turn(high_down, 3, False)
-    grads = layer_grad(0, ids, normed_input, [low, low_up, low_far, low_down], rows, None)
-    grads = layer_grad(1, ids, normed_input, [high, high_up, high_far, high_down], rows, grads)
+    grads = layer_grads(normed_input, [low, low_up, low_far, low_down],
+                        [high, high_up, high_far, high_down], rows)
     arrived = lax.all_to_all(grads, group_axes, 0, 0, tiled=True)
     updated, first, second, send = adam(
         layer_section, arrived, master, moment_one, moment_two)

time: 122 us -> 120 us (0.984)
  Pallas kernels: 13.8 us -> 17.4 us
  starting transfers between devices: 17.2 us -> 14.9 us
  waiting for transfers between devices: 25.1 us -> 23.4 us
    pallas_call x1, Pallas kernels: 7.54 us -> 12 us  [attention(): pl.pallas_call(functools.partial(attention_kernel, layers, tokens, per_de...]
    ppermute x9, starting transfers between devices: 11.5 us -> 9.17 us  [turn(): return lax.ppermute(value, ('core', 'y', 'x'), pairs)]
    ppermute x3, waiting for transfers between devices: 8.34 us -> 6.2 us  [shift(): return lax.ppermute(value, axis, [(i, (i + by) % n) for i in range(n)])]
    pallas_call x2 -> x1, Pallas kernels: 3.27 us -> 2.45 us  [layer_grads(): pl.pallas_call(functools.partial(grad_kernel, tokens, rows), grid_spec=pl...]
  transfers between devices with their start and end apart: 12 -> 12, of which waited for: 8 -> 10; matrix products, arithmetic and copies ran while one was open for 0% -> 0% of each run, Pallas kernels for 1% -> 0%
where the time goes in v3:
time: 120 us; the launch traced here: 121 us
  blocking collectives  62.7 us (52%)
  waiting for transfers between devices  23.4 us (20%)
  Pallas kernels  17.4 us (14%)
  starting transfers between devices  14.9 us (12%)
    all_to_all x1, blocking collectives, body(): arrived = lax.all_to_all(grads, group_axes, 0, 0, tiled=True)  37.1 us
    all_to_all x1, blocking collectives, body(): weights = place(lax.all_to_all(send, group_axes, 0, 0, tiled=True))  25.6 us
    ppermute x9, waiting for transfers between devices, turn(): return lax.ppermute(value, ('core', 'y', 'x'), pairs)  17.2 us
    pallas_call x1, Pallas kernels, attention(): pl.pallas_call(functools.partial(attention_kernel, layers, tokens, per_de...  12 us
    ppermute x9, starting transfers between devices, turn(): return lax.ppermute(value, ('core', 'y', 'x'), pairs)  9.17 us
    ppermute x3, waiting for transfers between devices, shift(): return lax.ppermute(value, axis, [(i, (i + by) % n) for i in range(n)])  6.2 us
    ppermute x3, starting transfers between devices, shift(): return lax.ppermute(value, axis, [(i, (i + by) % n) for i in range(n)])  5.7 us
    pallas_call x1, Pallas kernels, layer_grads(): pl.pallas_call(functools.partial(grad_kernel, tokens, rows), grid_spec=pl...  2.45 us
  transfers between devices with their start and end apart: 12, of which 10 were waited for; matrix products, arithmetic and copies ran while one was open for 0% of the time, Pallas kernels for 0%

profile of v3, /device:TPU:1, one launch (start us, length us, event | category | flops | bytes accessed | tf_op | source)
XLA Modules:
  0.0 120.5 jit_solution(1116199829415177235)
XLA Ops:
  0.6 12.0 %attention.1 = (bf16[2,384,128]{2,1,0:T(8,128)(2,1)}, bf16[2,384,128]{2,1,0:T(8,128)(2,1)}, bf16[2,384,128]{2,1,0:T(8,128)(2,1)}, bf16[2,384,128]{2,1,0:T(8,128)(2,1)}) custom-call(s32[4,6]{1,0:T(4,128)} %lmap.3, s32[4]{0:T(128)} %counts.1, s32[6]{0:T(128)} %windows.1, bf16[1,1,2,1536,256]{4,3,2,1,0:T(8,128)(2,1)} %q_ref.1, ...), custom_call_target="tpu_custom_call" | custom-call | flops 2415919104 | bytes 4194304 | tf_op jit(solution)/shard_map/attention/pallas_call | solution.py:157
  12.6 2.1 %collective-permute-start = (bf16[2,384,128]{2,1,0:T(8,128)(2,1)}, bf16[2,384,128]{2,1,0:T(8,128)(2,1)S(1)}, u32[]{:S(2)}, u32[]{:S(2)}) collective-permute-start(bf16[2,384,128]{2,1,0:T(8,128)(2,1)} %get-tuple-element.13), channel_id=1, source_target_pairs={{0,1},{1,2},{2,3},{3,0},{4,5},{5,6},{6,7},{7,4},{8,9},{9,10},{10,1... | collective-permute-start | bytes 589832 | tf_op jit(solution)/shard_map/ppermute | solution.py:309
  14.7 2.4 %collective-permute-start.1 = (bf16[2,384,128]{2,1,0:T(8,128)(2,1)}, bf16[2,384,128]{2,1,0:T(8,128)(2,1)S(1)}, u32[]{:S(2)}, u32[]{:S(2)}) collective-permute-start(bf16[2,384,128]{2,1,0:T(8,128)(2,1)} %get-tuple-element.14), channel_id=1, source_target_pairs={{0,2},{1,3},{2,0},{3,1},{4,6},{5,7},{6,4},{7,5},{8,10},{9,11},{10,... | collective-permute-start | bytes 589832 | tf_op jit(solution)/shard_map/ppermute | solution.py:309
  17.2 1.2 collective-permute-start.2
  18.3 5.3 %collective-permute-done = bf16[2,384,128]{2,1,0:T(8,128)(2,1)S(1)} collective-permute-done((bf16[2,384,128]{2,1,0:T(8,128)(2,1)}, bf16[2,384,128]{2,1,0:T(8,128)(2,1)S(1)}, u32[]{:S(2)}, u32[]{:S(2)}) %collective-permute-start) | collective-permute-done | bytes 196640 | tf_op jit(solution)/shard_map/ppermute | solution.py:309
  23.6 0.9 collective-permute-done.2
  24.5 1.0 add_convert_fusion
  25.6 1.2 collective-permute-start.5
  27.1 0.7 collective-permute-start.3
  27.8 2.4 %collective-permute-done.5 = bf16[2,384,128]{2,1,0:T(8,128)(2,1)S(1)} collective-permute-done((bf16[2,384,128]{2,1,0:T(8,128)(2,1)S(1)}, bf16[2,384,128]{2,1,0:T(8,128)(2,1)S(1)}, u32[]{:S(2)}, u32[]{:S(2)}) %collective-permute-start.5) | collective-permute-done | bytes 196640 | tf_op jit(solution)/shard_map/ppermute | solution.py:322
  30.2 2.9 %collective-permute-done.4 = bf16[2,384,128]{2,1,0:T(8,128)(2,1)S(1)} collective-permute-done((bf16[2,384,128]{2,1,0:T(8,128)(2,1)S(1)}, bf16[2,384,128]{2,1,0:T(8,128)(2,1)S(1)}, u32[]{:S(2)}, u32[]{:S(2)}) %collective-permute-start.4) | collective-permute-done | bytes 196640 | tf_op jit(solution)/shard_map/ppermute | solution.py:322
  33.1 2.0 %collective-permute-done.3 = bf16[2,384,128]{2,1,0:T(8,128)(2,1)S(1)} collective-permute-done((bf16[2,384,128]{2,1,0:T(8,128)(2,1)S(1)}, bf16[2,384,128]{2,1,0:T(8,128)(2,1)S(1)}, u32[]{:S(2)}, u32[]{:S(2)}) %collective-permute-start.3) | collective-permute-done | bytes 196640 | tf_op jit(solution)/shard_map/ppermute | solution.py:322
  35.2 1.4 %collective-permute-start.6 = (bf16[4,384,128]{2,1,0:T(8,128)(2,1)S(1)}, bf16[4,384,128]{2,1,0:T(8,128)(2,1)S(1)}, u32[]{:S(2)}, u32[]{:S(2)}) collective-permute-start(bf16[4,384,128]{2,1,0:T(8,128)(2,1)S(1)} %pad_maximum_fusion.refs_0_), channel_id=1, source_target_pairs={{0,4},{1,5},{2,6},{3,7},{4,8},{5,9},{6,10},{7,11},{8,12},{9,13},{1... | collective-permute-start | bytes 1179656 | tf_op jit(solution)/shard_map/ppermute | solution.py:322
  36.7 1.4 %collective-permute-start.10 = (bf16[4,384,128]{2,1,0:T(8,128)(2,1)S(1)}, bf16[4,384,128]{2,1,0:T(8,128)(2,1)S(1)}, u32[]{:S(2)}, u32[]{:S(2)}) collective-permute-start(bf16[4,384,128]{2,1,0:T(8,128)(2,1)S(1)} %pad_maximum_fusion.1.refs_4_), channel_id=1, source_target_pairs={{0,12},{1,13},{2,14},{3,15},{4,0},{5,1},{6,2},{7,3},{8,4},{9,5},{1... | collective-permute-start | bytes 1179656 | tf_op jit(solution)/shard_map/ppermute | solution.py:322
  38.2 0.8 collective-permute-start.8
  39.6 3.8 %collective-permute-done.6.refs_1_ = bf16[4,384,128]{2,1,0:T(8,128)(2,1)S(1)} collective-permute-done((bf16[4,384,128]{2,1,0:T(8,128)(2,1)S(1)}, bf16[4,384,128]{2,1,0:T(8,128)(2,1)S(1)}, u32[]{:S(2)}, u32[]{:S(2)}) %collective-permute-start.6) | collective-permute-done | bytes 393248 | tf_op jit(solution)/shard_map/ppermute | solution.py:322
  43.7 2.6 %collective-permute-start.11 = (bf16[4,384,128]{2,1,0:T(8,128)(2,1)S(1)}, bf16[4,384,128]{2,1,0:T(8,128)(2,1)S(1)}, u32[]{:S(2)}, u32[]{:S(2)}) collective-permute-start(bf16[4,384,128]{2,1,0:T(8,128)(2,1)S(1)} %collective-permute-done.10.refs_7_), channel_id=1, source_target_pairs={{0,12},{1,13},{2,14},{3,15},{4,0},{5,1},{6,2},{7,3},{8,4},{9,5},{1... | collective-permute-start | bytes 1179656 | tf_op jit(solution)/shard_map/ppermute | solution.py:322
  46.3 1.7 %collective-permute-done.8.refs_3_ = bf16[4,384,128]{2,1,0:T(8,128)(2,1)S(1)} collective-permute-done((bf16[4,384,128]{2,1,0:T(8,128)(2,1)S(1)}, bf16[4,384,128]{2,1,0:T(8,128)(2,1)S(1)}, u32[]{:S(2)}, u32[]{:S(2)}) %collective-permute-start.8) | collective-permute-done | bytes 393248 | tf_op jit(solution)/shard_map/ppermute | solution.py:322
  48.0 3.9 %collective-permute-done.7.refs_2_ = bf16[4,384,128]{2,1,0:T(8,128)(2,1)S(1)} collective-permute-done((bf16[4,384,128]{2,1,0:T(8,128)(2,1)S(1)}, bf16[4,384,128]{2,1,0:T(8,128)(2,1)S(1)}, u32[]{:S(2)}, u32[]{:S(2)}) %collective-permute-start.7) | collective-permute-done | bytes 393248 | tf_op jit(solution)/shard_map/ppermute | solution.py:322
  52.2 2.5 %layer_grads.1 = bf16[16,2,24,512]{3,2,1,0:T(8,128)(2,1)S(1)} custom-call(bf16[1,1,2,1536,384]{4,3,2,1,0:T(8,128)(2,1)S(1)} %copy-done, bf16[4,384,128]{2,1,0:T(8,128)(2,1)S(1)} %pad_maximum_fusion.refs_0_, bf16[4,384,128]{2,1,0:T(8,128)(2,1)S(1)} %collective-permute-done.6.refs_1_, bf16[4,384,128]{2,1,0:T(8,128)(2,1)S(1)} %collective-permute-done.7.refs_2_, ...), custom_call_target="tpu_custom_call" | custom-call | flops 1207959552 | bytes 6291456 | tf_op jit(solution)/shard_map/layer_grads/pallas_call | solution.py:205
  54.6 37.1 %all_to_all.10.arrived = bf16[16,2,24,512]{3,2,1,0:T(8,128)(2,1)S(1)} all-to-all(bf16[16,2,24,512]{3,2,1,0:T(8,128)(2,1)S(1)} %layer_grads.1), channel_id=1, replica_groups=mesh['rep'=4,'z'=2,'core'=2,'y'=4,'x'=4] {'rep','z','core'}, dimensions={0} | all-to-all | bytes 1572864 | tf_op jit(solution)/shard_map/all_to_all | solution.py:343
  91.7 1.8 %adamw.1 = (f32[6,1,24,512]{3,2,1,0:T(8,128)}, f32[6,1,24,512]{3,2,1,0:T(8,128)}, f32[6,1,24,512]{3,2,1,0:T(8,128)}, bf16[16,2,24,512]{3,2,1,0:T(8,128)(2,1)S(1)}) custom-call(s32[4,6]{1,0:T(4,128)S(1)} %copy-done.4, bf16[16,2,24,512]{3,2,1,0:T(8,128)(2,1)S(1)} %all_to_all.10.arrived, f32[6,1,24,512]{3,2,1,0:T(8,128)S(1)} %copy-done.1, ...), custom_call_target="tpu_custom_call" | custom-call | flops 1474560 | bytes 4194304 | tf_op jit(solution)/shard_map/adamw/pallas_call | solution.py:265
  93.6 25.6 %all_to_all.11.arrived = bf16[16,2,24,512]{3,2,1,0:T(8,128)(2,1)S(1)} all-to-all(bf16[16,2,24,512]{3,2,1,0:T(8,128)(2,1)S(1)} %get-tuple-element.19), channel_id=1, replica_groups=mesh['rep'=4,'z'=2,'core'=2,'y'=4,'x'=4] {'rep','z','core'}, dimensions={0} | all-to-all | bytes 1572864 | tf_op jit(solution)/shard_map/all_to_all | solution.py:346
  119.2 1.1 place.1
  (23 shorter events, 1.8 us)
Async XLA Ops:
  12.6 39.5 %copy-start = (bf16[1,1,2,1536,384]{4,3,2,1,0:T(8,128)(2,1)S(1)}, bf16[1,1,2,1536,384]{4,3,2,1,0:T(8,128)(2,1)}, u32[]{:S(2)}) copy-start(bf16[1,1,2,1536,384]{4,3,2,1,0:T(8,128)(2,1)} %x_ref.1) | copy-start | bytes 7077892
  12.6 11.0 %collective-permute-start = (bf16[2,384,128]{2,1,0:T(8,128)(2,1)}, bf16[2,384,128]{2,1,0:T(8,128)(2,1)S(1)}, u32[]{:S(2)}, u32[]{:S(2)}) collective-permute-start(bf16[2,384,128]{2,1,0:T(8,128)(2,1)} %get-tuple-element.13), channel_id=1, source_target_pairs={{0,1},{1,2},{2,3},{3,0},{4,5},{5,6},{6,7},{7,4},{8,9},{9,10},{10,1... | collective-permute-start | bytes 589832 | tf_op jit(solution)/shard_map/ppermute | solution.py:309
  14.7 8.9 %collective-permute-start.1 = (bf16[2,384,128]{2,1,0:T(8,128)(2,1)}, bf16[2,384,128]{2,1,0:T(8,128)(2,1)S(1)}, u32[]{:S(2)}, u32[]{:S(2)}) collective-permute-start(bf16[2,384,128]{2,1,0:T(8,128)(2,1)} %get-tuple-element.14), channel_id=1, source_target_pairs={{0,2},{1,3},{2,0},{3,1},{4,6},{5,7},{6,4},{7,5},{8,10},{9,11},{10,... | collective-permute-start | bytes 589832 | tf_op jit(solution)/shard_map/ppermute | solution.py:309
  17.2 7.4 %collective-permute-start.2 = (bf16[2,384,128]{2,1,0:T(8,128)(2,1)}, bf16[2,384,128]{2,1,0:T(8,128)(2,1)S(1)}, u32[]{:S(2)}, u32[]{:S(2)}) collective-permute-start(bf16[2,384,128]{2,1,0:T(8,128)(2,1)} %get-tuple-element.15), channel_id=1, source_target_pairs={{0,3},{1,0},{2,1},{3,2},{4,7},{5,4},{6,5},{7,6},{8,11},{9,8},{10,9... | collective-permute-start | bytes 589832 | tf_op jit(solution)/shard_map/ppermute | solution.py:309
  25.6 4.6 %collective-permute-start.5 = (bf16[2,384,128]{2,1,0:T(8,128)(2,1)S(1)}, bf16[2,384,128]{2,1,0:T(8,128)(2,1)S(1)}, u32[]{:S(2)}, u32[]{:S(2)}) collective-permute-start(bf16[2,384,128]{2,1,0:T(8,128)(2,1)S(1)} %add_convert_fusion), channel_id=1, source_target_pairs={{0,3},{1,0},{2,1},{3,2},{4,7},{5,4},{6,5},{7,6},{8,11},{9,8},{10,9... | collective-permute-start | bytes 589832 | tf_op jit(solution)/shard_map/ppermute | solution.py:322
  26.7 6.4 %collective-permute-start.4 = (bf16[2,384,128]{2,1,0:T(8,128)(2,1)S(1)}, bf16[2,384,128]{2,1,0:T(8,128)(2,1)S(1)}, u32[]{:S(2)}, u32[]{:S(2)}) collective-permute-start(bf16[2,384,128]{2,1,0:T(8,128)(2,1)S(1)} %add_convert_fusion), channel_id=1, source_target_pairs={{0,2},{1,3},{2,0},{3,1},{4,6},{5,7},{6,4},{7,5},{8,10},{9,11},{10,... | collective-permute-start | bytes 589832 | tf_op jit(solution)/shard_map/ppermute | solution.py:322
  27.1 8.1 %collective-permute-start.3 = (bf16[2,384,128]{2,1,0:T(8,128)(2,1)S(1)}, bf16[2,384,128]{2,1,0:T(8,128)(2,1)S(1)}, u32[]{:S(2)}, u32[]{:S(2)}) collective-permute-start(bf16[2,384,128]{2,1,0:T(8,128)(2,1)S(1)} %add_convert_fusion), channel_id=1, source_target_pairs={{0,1},{1,2},{2,3},{3,0},{4,5},{5,6},{6,7},{7,4},{8,9},{9,10},{10,1... | collective-permute-start | bytes 589832 | tf_op jit(solution)/shard_map/ppermute | solution.py:322
  35.2 8.2 %collective-permute-start.6 = (bf16[4,384,128]{2,1,0:T(8,128)(2,1)S(1)}, bf16[4,384,128]{2,1,0:T(8,128)(2,1)S(1)}, u32[]{:S(2)}, u32[]{:S(2)}) collective-permute-start(bf16[4,384,128]{2,1,0:T(8,128)(2,1)S(1)} %pad_maximum_fusion.refs_0_), channel_id=1, source_target_pairs={{0,4},{1,5},{2,6},{3,7},{4,8},{5,9},{6,10},{7,11},{8,12},{9,13},{1... | collective-permute-start | bytes 1179656 | tf_op jit(solution)/shard_map/ppermute | solution.py:322
  36.7 55.0 %copy-start.1 = (f32[6,1,24,512]{3,2,1,0:T(8,128)S(1)}, f32[6,1,24,512]{3,2,1,0:T(8,128)}, u32[]{:S(2)}) copy-start(f32[6,1,24,512]{3,2,1,0:T(8,128)} %master.1) | copy-start | bytes 884740
  36.7 55.0 %copy-start.2 = (f32[6,1,24,512]{3,2,1,0:T(8,128)S(1)}, f32[6,1,24,512]{3,2,1,0:T(8,128)}, u32[]{:S(2)}) copy-start(f32[6,1,24,512]{3,2,1,0:T(8,128)} %one.1) | copy-start | bytes 884740
  36.7 55.0 %copy-start.3 = (f32[6,1,24,512]{3,2,1,0:T(8,128)S(1)}, f32[6,1,24,512]{3,2,1,0:T(8,128)}, u32[]{:S(2)}) copy-start(f32[6,1,24,512]{3,2,1,0:T(8,128)} %two.1) | copy-start | bytes 884740
  36.7 55.0 %copy-start.4 = (s32[4,6]{1,0:T(4,128)S(1)}, s32[4,6]{1,0:T(4,128)}, u32[]{:S(2)}) copy-start(s32[4,6]{1,0:T(4,128)} %lmap.3) | copy-start | bytes 292
  36.7 7.0 %collective-permute-start.10 = (bf16[4,384,128]{2,1,0:T(8,128)(2,1)S(1)}, bf16[4,384,128]{2,1,0:T(8,128)(2,1)S(1)}, u32[]{:S(2)}, u32[]{:S(2)}) collective-permute-start(bf16[4,384,128]{2,1,0:T(8,128)(2,1)S(1)} %pad_maximum_fusion.1.refs_4_), channel_id=1, source_target_pairs={{0,12},{1,13},{2,14},{3,15},{4,0},{5,1},{6,2},{7,3},{8,4},{9,5},{1... | collective-permute-start | bytes 1179656 | tf_op jit(solution)/shard_map/ppermute | solution.py:322
  38.2 9.8 %collective-permute-start.8 = (bf16[4,384,128]{2,1,0:T(8,128)(2,1)S(1)}, bf16[4,384,128]{2,1,0:T(8,128)(2,1)S(1)}, u32[]{:S(2)}, u32[]{:S(2)}) collective-permute-start(bf16[4,384,128]{2,1,0:T(8,128)(2,1)S(1)} %pad_maximum_fusion.refs_0_), channel_id=1, source_target_pairs={{0,12},{1,13},{2,14},{3,15},{4,0},{5,1},{6,2},{7,3},{8,4},{9,5},{1... | collective-permute-start | bytes 1179656 | tf_op jit(solution)/shard_map/ppermute | solution.py:322
  39.0 9.0 %collective-permute-start.9 = (bf16[4,384,128]{2,1,0:T(8,128)(2,1)S(1)}, bf16[4,384,128]{2,1,0:T(8,128)(2,1)S(1)}, u32[]{:S(2)}, u32[]{:S(2)}) collective-permute-start(bf16[4,384,128]{2,1,0:T(8,128)(2,1)S(1)} %pad_maximum_fusion.1.refs_4_), channel_id=1, source_target_pairs={{0,4},{1,5},{2,6},{3,7},{4,8},{5,9},{6,10},{7,11},{8,12},{9,13},{1... | collective-permute-start | bytes 1179656 | tf_op jit(solution)/shard_map/ppermute | solution.py:322
  43.4 8.4 %collective-permute-start.7 = (bf16[4,384,128]{2,1,0:T(8,128)(2,1)S(1)}, bf16[4,384,128]{2,1,0:T(8,128)(2,1)S(1)}, u32[]{:S(2)}, u32[]{:S(2)}) collective-permute-start(bf16[4,384,128]{2,1,0:T(8,128)(2,1)S(1)} %collective-permute-done.6.refs_1_), channel_id=1, source_target_pairs={{0,4},{1,5},{2,6},{3,7},{4,8},{5,9},{6,10},{7,11},{8,12},{9,13},{1... | collective-permute-start | bytes 1179656 | tf_op jit(solution)/shard_map/ppermute | solution.py:322
  43.7 8.4 %collective-permute-start.11 = (bf16[4,384,128]{2,1,0:T(8,128)(2,1)S(1)}, bf16[4,384,128]{2,1,0:T(8,128)(2,1)S(1)}, u32[]{:S(2)}, u32[]{:S(2)}) collective-permute-start(bf16[4,384,128]{2,1,0:T(8,128)(2,1)S(1)} %collective-permute-done.10.refs_7_), channel_id=1, source_target_pairs={{0,12},{1,13},{2,14},{3,15},{4,0},{5,1},{6,2},{7,3},{8,4},{9,5},{1... | collective-permute-start | bytes 1179656 | tf_op jit(solution)/shard_map/ppermute | solution.py:322

commit v4 on v3

--- a/solution.py
+++ b/solution.py
@@ -42,11 +42,12 @@
 def attention_kernel(layers, tokens, per_dev, lmap, counts, windows,
                      q_ref, k_ref, g_ref, *rest):
     outs = rest[:4]
-    acc, p_scr, g_scr = rest[4:]
+    flag, acc, p_scr, g_scr = rest[4:]
     slot, step = pl.program_id(0), pl.program_id(1)
     steps = pl.num_programs(1)
     replica, section, x_id = lax.axis_index("rep"), section_index(), lax.axis_index("x")
     first, held = first_and_count(lmap, replica, section, layers)
+    flag[0] = held
     layer = jnp.minimum(first + slot, layers - 1)
     window = windows[layer]
     length = jnp.where(slot < held, counts[replica], 0)
@@ -160,14 +161,15 @@
             num_scalar_prefetch=3,
             grid=(slots, tokens // RB),
             in_specs=[row_block, key_block, row_block],
-            out_specs=[out_block] * 4,
+            out_specs=[out_block] * 4 + [pl.BlockSpec(memory_space=pltpu.SMEM)],
             scratch_shapes=[
                 pltpu.VMEM((tokens, HD), F32),
                 pltpu.VMEM((6, tokens // 2 + TQ, per_dev * TQ), BF),
                 pltpu.VMEM((6, per_dev * TQ, HD), BF),
             ],
         ),
-        out_shape=[jax.ShapeDtypeStruct((slots, part, HD), BF)] * 4,
+        out_shape=[jax.ShapeDtypeStruct((slots, part, HD), BF)] * 4
+        + [jax.ShapeDtypeStruct((1,), jnp.int32)],
         compiler_params=pltpu.CompilerParams(vmem_limit_bytes=VMEM),
         cost_estimate=pl.CostEstimate(
             flops=36 * per_dev * 4 * TQ * TQ * HD, bytes_accessed=4 << 20,
@@ -176,25 +178,53 @@
     )(*scalars, queries, key_rows, out_grad)
 
 
-def grad_kernel(tokens, rows, x_ref, *refs):
-    out_ref, value, result = refs[-3:]
+def grad_slot(tokens, rows, x_ref, pieces, out_ref, value, result):
     core, y_id, x_id = (lax.axis_index(n) for n in ("core", "y", "x"))
     part = tokens // 4
-    for slot in range(2):
-        @pl.when(pl.program_id(0) == slot)
-        def _(pieces=refs[4 * slot:4 * slot + 4]):
-            for k in range(4):
-                for i in range(4):
-                    y = lax.rem(y_id + 4 - jnp.where(core == 0, k, i), 4)
-                    x = lax.rem(x_id + 4 - jnp.where(core == 0, i, k), 4)
-                    at = pl.multiple_of(x * part, part)
-                    col = pl.multiple_of(y * HD, HD)
-                    value[pl.ds(at, part), pl.ds(col, HD)] = pieces[k][i]
-
+    for k in range(4):
+        for i in range(4):
+            y = lax.rem(y_id + 4 - jnp.where(core == 0, k, i), 4)
+            x = lax.rem(x_id + 4 - jnp.where(core == 0, i, k), 4)
+            at = pl.multiple_of(x * part, part)
+            col = pl.multiple_of(y * HD, HD)
+            value[pl.ds(at, part), pl.ds(col, HD)] = pieces[k][i]
     result[...] = lax.dot_general(
         x_ref[...], value[...], (((0,), (0,)), ((), ())), preferred_element_type=F32)
     for z in range(out_ref.shape[0]):
         out_ref[z] = result[z * rows:(z + 1) * rows, :].astype(BF)
+
+
+def grad_kernel(tokens, rows, x_ref, *refs):
+    for slot in range(2):
+        @pl.when(pl.program_id(0) == slot)
+        def _(pieces=refs[4 * slot:4 * slot + 4]):
+            grad_slot(tokens, rows, x_ref, pieces, *refs[8:])
+
+
+def first_kernel(tokens, rows, x_ref, *refs):
+    out_ref = refs[4]
+    grad_slot(tokens, rows, x_ref, refs[:4], out_ref.at[:, 0], *refs[5:])
+    out_ref[:, 1] = jnp.zeros(out_ref.shape[:1] + out_ref.shape[2:], BF)
+
+
+def first_grad(normed, low, rows):
+    slots, tokens, width = normed.shape[2:]
+    group = width // rows
+    part = tokens // 4
+    return pl.pallas_call(
+        functools.partial(first_kernel, tokens, rows),
+        grid=(1,),
+        in_specs=[pl.BlockSpec((None, None, None, tokens, width), lambda j: (0, 0, 0, 0, 0))]
+        + [pl.BlockSpec((4, part, HD), lambda j: (0, 0, 0))] * 4,
+        out_specs=pl.BlockSpec((group, slots, rows, KVH * HD), lambda j: (0, 0, 0, 0)),
+        scratch_shapes=[pltpu.VMEM((tokens, KVH * HD), BF),
+                        pltpu.VMEM((width, KVH * HD), F32)],
+        out_shape=jax.ShapeDtypeStruct((group, slots, rows, KVH * HD), BF),
+        compiler_params=pltpu.CompilerParams(vmem_limit_bytes=16 << 20),
+        cost_estimate=pl.CostEstimate(
+            flops=2 * tokens * width * KVH * HD, bytes_accessed=3 << 20, transcendentals=0),
+        name="first_grad",
+    )(normed, *low)
 
 
 def layer_grads(normed, low, high, rows):
@@ -322,24 +352,38 @@
     return lax.ppermute(value, ("core", "y", "x"), pairs)
 
 
+def across(parts):
+    total = parts[0].astype(F32)
+    for k in range(1, 4):
+        total = total + shift(parts[k], "x", k).astype(F32)
+    return total.astype(BF)
+
+
 def body(layer_section, token_count, window_size, normed_input, queries, key_rows, out_grad,
          master, moment_one, moment_two):
     layers = layer_section.shape[1]
     group_axes = ("rep", "z", "core")
     rows = master.shape[2]
-    parts = attention((layer_section, token_count, window_size),
-                      queries, key_rows, out_grad, layers)
-    total = parts[0].astype(F32)
-    for k in range(1, 4):
-        total = total + shift(parts[k], "x", k).astype(F32)
-    block = total.astype(BF)
-    near = [block] + [turn(block, k, True) for k in range(1, 4)]
-    low, high = jnp.stack([n[0] for n in near]), jnp.stack([n[1] for n in near])
-    low_up, high_down = turn(low, 1, False), turn(high, 3, False)
-    high_up, low_down = turn(high, 1, False), turn(low, 3, False)
-    low_far, high_far = turn(low_up, 1, False), turn(high_down, 3, False)
-    grads = layer_grads(normed_input, [low, low_up, low_far, low_down],
-                        [high, high_up, high_far, high_down], rows)
+    *parts, held = attention((layer_section, token_count, window_size),
+                             queries, key_rows, out_grad, layers)
+
+    def both_slots():
+        block = across(parts)
+        near = [block] + [turn(block, k, True) for k in range(1, 4)]
+        low, high = jnp.stack([n[0] for n in near]), jnp.stack([n[1] for n in near])
+        low_up, high_down = turn(low, 1, False), turn(high, 3, False)
+        high_up, low_down = turn(high, 1, False), turn(low, 3, False)
+        low_far, high_far = turn(low_up, 1, False), turn(high_down, 3, False)
+        return layer_grads(normed_input, [low, low_up, low_far, low_down],
+                           [high, high_up, high_far, high_down], rows)
+
+    def one_slot():
+        block = across([p[0] for p in parts])
+        low = jnp.stack([block] + [turn(block, k, True) for k in range(1, 4)])
+        low_up, low_down = turn(low, 1, False), turn(low, 3, False)
+        return first_grad(normed_input, [low, low_up, turn(low_up, 1, False), low_down], rows)
+
+    grads = lax.cond(held[0] == 2, both_slots, one_slot)
     arrived = lax.all_to_all(grads, group_axes, 0, 0, tiled=True)
     updated, first, second, send = adam(
         layer_section, arrived, master, moment_one, moment_two)

time: 120 us -> 120 us (level)
  starting transfers between devices: 14.9 us -> 17.1 us
  blocking collectives: 62.7 us -> 60.9 us
    ppermute x9, starting transfers between devices: 9.17 us -> 11.4 us  [turn(): return lax.ppermute(value, ('core', 'y', 'x'), pairs)]
    all_to_all x1, blocking collectives: 37.1 us -> 35.3 us  [body(): arrived = lax.all_to_all(grads, group_axes, 0, 0, tiled=True)]
    ppermute x3, waiting for transfers between devices: 6.2 us -> 4.8 us  [shift(): return lax.ppermute(value, axis, [(i, (i + by) % n) for i in range(n)])]
    ppermute x9, waiting for transfers between devices: 17.2 us -> 18.4 us  [turn(): return lax.ppermute(value, ('core', 'y', 'x'), pairs)]
where the time goes in v4:
time: 120 us
  blocking collectives  60.9 us (51%)
  waiting for transfers between devices  23.2 us (19%)
  starting transfers between devices  17.1 us (14%)
  Pallas kernels  16.5 us (14%)
  between operations  1.54 us (1%)
    all_to_all x1, blocking collectives, body(): arrived = lax.all_to_all(grads, group_axes, 0, 0, tiled=True)  35.3 us
    all_to_all x1, blocking collectives, body(): weights = place(lax.all_to_all(send, group_axes, 0, 0, tiled=True))  25.6 us
    ppermute x9, waiting for transfers between devices, turn(): return lax.ppermute(value, ('core', 'y', 'x'), pairs)  18.4 us
    ppermute x9, starting transfers between devices, turn(): return lax.ppermute(value, ('core', 'y', 'x'), pairs)  11.4 us
    pallas_call x1, Pallas kernels, attention(): pl.pallas_call(functools.partial(attention_kernel, layers, tokens, per_de...  11.2 us
    ppermute x3, starting transfers between devices, shift(): return lax.ppermute(value, axis, [(i, (i + by) % n) for i in range(n)])  5.72 us
    ppermute x3, waiting for transfers between devices, shift(): return lax.ppermute(value, axis, [(i, (i + by) % n) for i in range(n)])  4.8 us
  transfers between devices with their start and end apart: 12, of which 10 were waited for; matrix products, arithmetic and copies ran while one was open for 0% of the time, Pallas kernels for 0%

profile of v4, /device:TPU:1, one launch (start us, length us, event | category | flops | bytes accessed | tf_op | source)
XLA Modules:
  0.0 119.9 jit_solution(16286313933371569295)
XLA Ops:
  0.6 11.2 %attention.1 = (bf16[2,384,128]{2,1,0:T(8,128)(2,1)S(1)}, bf16[2,384,128]{2,1,0:T(8,128)(2,1)S(1)}, bf16[2,384,128]{2,1,0:T(8,128)(2,1)S(1)}, bf16[2,384,128]{2,1,0:T(8,128)(2,1)S(1)}, s32[1]{0:T(128)}) custom-call(s32[4,6]{1,0:T(4,128)} %lmap.3, s32[4]{0:T(128)} %counts.1, s32[6]{0:T(128)} %windows.1, bf16[1,1,2,1536,256]{4,3,2,1,0:T(8,128)(2,1)} %q_ref.1, ...), custom_call_target="tpu_custom_call" | custom-call | flops 2415919104 | bytes 4194304 | tf_op jit(solution)/shard_map/attention/pallas_call | solution.py:158
  12.6 43.2 %conditional.1 = (bf16[16,2,24,512]{3,2,1,0:T(8,128)(2,1)S(1)}) conditional(s32[]{:T(128)} %bitcast.9, (bf16[2,384,128]{2,1,0:T(8,128)(2,1)S(1)}, bf16[2,384,128]{2,1,0:T(8,128)(2,1)S(1)}, bf16[2,384,128]{2,1,0:T(8,128)(2,1)S(1)}, bf16[2,384,128]{2,1,0:T(8,128)(2,1)S(1)}, bf16[1,1,2,1536,384]{4,3,2,1,0:T(8,128)(2,1)S(1)}) %tuple.22, ...), branch_computations={%region_0.0_spmd, %region_1.0_spmd} | conditional | flops 1209925632 | bytes 24576488 | solution.py:386
  12.8 2.1 %collective-permute-start.9 = (bf16[2,384,128]{2,1,0:T(8,128)(2,1)S(1)}, bf16[2,384,128]{2,1,0:T(8,128)(2,1)S(1)}, u32[]{:S(2)}, u32[]{:S(2)}) collective-permute-start(bf16[2,384,128]{2,1,0:T(8,128)(2,1)S(1)} %get-tuple-element.30), channel_id=1, source_target_pairs={{0,1},{1,2},{2,3},{3,0},{4,5},{5,6},{6,7},{7,4},{8,9},{9,10},{10,1... | collective-permute-start | bytes 589832 | tf_op jit(solution)/shard_map/cond/branch_1_fun/ppermute | solution.py:339
  15.0 2.5 %collective-permute-start.10 = (bf16[2,384,128]{2,1,0:T(8,128)(2,1)S(1)}, bf16[2,384,128]{2,1,0:T(8,128)(2,1)S(1)}, u32[]{:S(2)}, u32[]{:S(2)}) collective-permute-start(bf16[2,384,128]{2,1,0:T(8,128)(2,1)S(1)} %get-tuple-element.31), channel_id=1, source_target_pairs={{0,2},{1,3},{2,0},{3,1},{4,6},{5,7},{6,4},{7,5},{8,10},{9,11},{10,... | collective-permute-start | bytes 589832 | tf_op jit(solution)/shard_map/cond/branch_1_fun/ppermute | solution.py:339
  17.4 1.1 collective-permute-start.11
  18.6 1.9 %collective-permute-done.9 = bf16[2,384,128]{2,1,0:T(8,128)(2,1)S(1)} collective-permute-done((bf16[2,384,128]{2,1,0:T(8,128)(2,1)S(1)}, bf16[2,384,128]{2,1,0:T(8,128)(2,1)S(1)}, u32[]{:S(2)}, u32[]{:S(2)}) %collective-permute-start.9) | collective-permute-done | bytes 196640 | tf_op jit(solution)/shard_map/cond/branch_1_fun/ppermute | solution.py:339
  20.4 2.9 %collective-permute-done.10 = bf16[2,384,128]{2,1,0:T(8,128)(2,1)S(1)} collective-permute-done((bf16[2,384,128]{2,1,0:T(8,128)(2,1)S(1)}, bf16[2,384,128]{2,1,0:T(8,128)(2,1)S(1)}, u32[]{:S(2)}, u32[]{:S(2)}) %collective-permute-start.10) | collective-permute-done | bytes 196640 | tf_op jit(solution)/shard_map/cond/branch_1_fun/ppermute | solution.py:339
  23.5 2.0 %collective-permute-start.14 = (bf16[2,384,128]{2,1,0:T(8,128)(2,1)S(1)}, bf16[2,384,128]{2,1,0:T(8,128)(2,1)S(1)}, u32[]{:S(2)}, u32[]{:S(2)}) collective-permute-start(bf16[2,384,128]{2,1,0:T(8,128)(2,1)S(1)} %add_convert_fusion), channel_id=1, source_target_pairs={{0,3},{1,0},{2,1},{3,2},{4,7},{5,4},{6,5},{7,6},{8,11},{9,8},{10,9... | collective-permute-start | bytes 589832 | tf_op jit(solution)/shard_map/cond/branch_1_fun/ppermute | solution.py:352
  26.6 3.7 %collective-permute-done.14 = bf16[2,384,128]{2,1,0:T(8,128)(2,1)S(1)} collective-permute-done((bf16[2,384,128]{2,1,0:T(8,128)(2,1)S(1)}, bf16[2,384,128]{2,1,0:T(8,128)(2,1)S(1)}, u32[]{:S(2)}, u32[]{:S(2)}) %collective-permute-start.14) | collective-permute-done | bytes 196640 | tf_op jit(solution)/shard_map/cond/branch_1_fun/ppermute | solution.py:352
  30.2 1.4 %collective-permute-done.13 = bf16[2,384,128]{2,1,0:T(8,128)(2,1)S(1)} collective-permute-done((bf16[2,384,128]{2,1,0:T(8,128)(2,1)S(1)}, bf16[2,384,128]{2,1,0:T(8,128)(2,1)S(1)}, u32[]{:S(2)}, u32[]{:S(2)}) %collective-permute-start.13) | collective-permute-done | bytes 196640 | tf_op jit(solution)/shard_map/cond/branch_1_fun/ppermute | solution.py:352
  31.6 3.1 %collective-permute-done.12 = bf16[2,384,128]{2,1,0:T(8,128)(2,1)S(1)} collective-permute-done((bf16[2,384,128]{2,1,0:T(8,128)(2,1)S(1)}, bf16[2,384,128]{2,1,0:T(8,128)(2,1)S(1)}, u32[]{:S(2)}, u32[]{:S(2)}) %collective-permute-start.12) | collective-permute-done | bytes 196640 | tf_op jit(solution)/shard_map/cond/branch_1_fun/ppermute | solution.py:352
  34.8 3.5 %collective-permute-start.15 = (bf16[4,384,128]{2,1,0:T(8,128)(2,1)S(1)}, bf16[4,384,128]{2,1,0:T(8,128)(2,1)S(1)}, u32[]{:S(2)}, u32[]{:S(2)}) collective-permute-start(bf16[4,384,128]{2,1,0:T(8,128)(2,1)S(1)} %pad_maximum_fusion.1.refs_0_), channel_id=1, source_target_pairs={{0,4},{1,5},{2,6},{3,7},{4,8},{5,9},{6,10},{7,11},{8,12},{9,13},{1... | collective-permute-start | bytes 1179656 | tf_op jit(solution)/shard_map/cond/branch_1_fun/ppermute | solution.py:352
  39.1 1.4 %collective-permute-start.17 = (bf16[4,384,128]{2,1,0:T(8,128)(2,1)S(1)}, bf16[4,384,128]{2,1,0:T(8,128)(2,1)S(1)}, u32[]{:S(2)}, u32[]{:S(2)}) collective-permute-start(bf16[4,384,128]{2,1,0:T(8,128)(2,1)S(1)} %pad_maximum_fusion.1.refs_0_), channel_id=1, source_target_pairs={{0,12},{1,13},{2,14},{3,15},{4,0},{5,1},{6,2},{7,3},{8,4},{9,5},{1... | collective-permute-start | bytes 1179656 | tf_op jit(solution)/shard_map/cond/branch_1_fun/ppermute | solution.py:352
  40.6 3.8 %collective-permute-done.15.refs_1_ = bf16[4,384,128]{2,1,0:T(8,128)(2,1)S(1)} collective-permute-done((bf16[4,384,128]{2,1,0:T(8,128)(2,1)S(1)}, bf16[4,384,128]{2,1,0:T(8,128)(2,1)S(1)}, u32[]{:S(2)}, u32[]{:S(2)}) %collective-permute-start.15) | collective-permute-done | bytes 393248 | tf_op jit(solution)/shard_map/cond/branch_1_fun/ppermute | solution.py:352
  44.4 0.8 collective-permute-start.16
  45.4 1.9 %collective-permute-start.20 = (bf16[4,384,128]{2,1,0:T(8,128)(2,1)S(1)}, bf16[4,384,128]{2,1,0:T(8,128)(2,1)S(1)}, u32[]{:S(2)}, u32[]{:S(2)}) collective-permute-start(bf16[4,384,128]{2,1,0:T(8,128)(2,1)S(1)} %collective-permute-done.19.refs_7_), channel_id=1, source_target_pairs={{0,12},{1,13},{2,14},{3,15},{4,0},{5,1},{6,2},{7,3},{8,4},{9,5},{1... | collective-permute-start | bytes 1179656 | tf_op jit(solution)/shard_map/cond/branch_1_fun/ppermute | solution.py:352
  47.2 2.1 %collective-permute-done.17.refs_3_ = bf16[4,384,128]{2,1,0:T(8,128)(2,1)S(1)} collective-permute-done((bf16[4,384,128]{2,1,0:T(8,128)(2,1)S(1)}, bf16[4,384,128]{2,1,0:T(8,128)(2,1)S(1)}, u32[]{:S(2)}, u32[]{:S(2)}) %collective-permute-start.17) | collective-permute-done | bytes 393248 | tf_op jit(solution)/shard_map/cond/branch_1_fun/ppermute | solution.py:352
  49.3 3.3 %collective-permute-done.16.refs_2_ = bf16[4,384,128]{2,1,0:T(8,128)(2,1)S(1)} collective-permute-done((bf16[4,384,128]{2,1,0:T(8,128)(2,1)S(1)}, bf16[4,384,128]{2,1,0:T(8,128)(2,1)S(1)}, u32[]{:S(2)}, u32[]{:S(2)}) %collective-permute-start.16) | collective-permute-done | bytes 393248 | tf_op jit(solution)/shard_map/cond/branch_1_fun/ppermute | solution.py:352
  52.6 0.9 collective-permute-done.20.refs_6_
  53.5 2.3 %layer_grads.1 = bf16[16,2,24,512]{3,2,1,0:T(8,128)(2,1)S(1)} custom-call(bf16[1,1,2,1536,384]{4,3,2,1,0:T(8,128)(2,1)S(1)} %get-tuple-element.28.x_ref, bf16[4,384,128]{2,1,0:T(8,128)(2,1)S(1)} %pad_maximum_fusion.1.refs_0_, bf16[4,384,128]{2,1,0:T(8,128)(2,1)S(1)} %collective-permute-done.15.refs_1_, ...), custom_call_target="tpu_custom_call" | custom-call | flops 1207959552 | bytes 6291456 | tf_op jit(solution)/shard_map/cond/branch_1_fun/layer_grads/pallas_call | solution.py:235
  55.8 35.3 %all_to_all.10.arrived = bf16[16,2,24,512]{3,2,1,0:T(8,128)(2,1)S(1)} all-to-all(bf16[16,2,24,512]{3,2,1,0:T(8,128)(2,1)S(1)} %get-tuple-element.63), channel_id=1, replica_groups=mesh['rep'=4,'z'=2,'core'=2,'y'=4,'x'=4] {'rep','z','core'}, dimensions={0} | all-to-all | bytes 1572864 | tf_op jit(solution)/shard_map/all_to_all | solution.py:387
  91.1 1.8 %adamw.1 = (f32[6,1,24,512]{3,2,1,0:T(8,128)}, f32[6,1,24,512]{3,2,1,0:T(8,128)}, f32[6,1,24,512]{3,2,1,0:T(8,128)}, bf16[16,2,24,512]{3,2,1,0:T(8,128)(2,1)S(1)}) custom-call(s32[4,6]{1,0:T(4,128)S(1)} %copy-done.3, bf16[16,2,24,512]{3,2,1,0:T(8,128)(2,1)S(1)} %all_to_all.10.arrived, f32[6,1,24,512]{3,2,1,0:T(8,128)S(1)} %copy-done, ...), custom_call_target="tpu_custom_call" | custom-call | flops 1474560 | bytes 4194304 | tf_op jit(solution)/shard_map/adamw/pallas_call | solution.py:295
  92.9 25.6 %all_to_all.11.arrived = bf16[16,2,24,512]{3,2,1,0:T(8,128)(2,1)S(1)} all-to-all(bf16[16,2,24,512]{3,2,1,0:T(8,128)(2,1)S(1)} %get-tuple-element.54), channel_id=1, replica_groups=mesh['rep'=4,'z'=2,'core'=2,'y'=4,'x'=4] {'rep','z','core'}, dimensions={0} | all-to-all | bytes 1572864 | tf_op jit(solution)/shard_map/all_to_all | solution.py:390
  118.5 1.1 place.1
  (24 shorter events, 2.2 us)
Async XLA Ops:
  0.6 11.9 %copy-start.4 = (bf16[1,1,2,1536,384]{4,3,2,1,0:T(8,128)(2,1)S(1)}, bf16[1,1,2,1536,384]{4,3,2,1,0:T(8,128)(2,1)}, u32[]{:S(2)}) copy-start(bf16[1,1,2,1536,384]{4,3,2,1,0:T(8,128)(2,1)} %param.15) | copy-start | bytes 7077892
  12.6 78.5 %copy-start = (f32[6,1,24,512]{3,2,1,0:T(8,128)S(1)}, f32[6,1,24,512]{3,2,1,0:T(8,128)}, u32[]{:S(2)}) copy-start(f32[6,1,24,512]{3,2,1,0:T(8,128)} %master.1) | copy-start | bytes 884740
  12.6 78.5 %copy-start.1 = (f32[6,1,24,512]{3,2,1,0:T(8,128)S(1)}, f32[6,1,24,512]{3,2,1,0:T(8,128)}, u32[]{:S(2)}) copy-start(f32[6,1,24,512]{3,2,1,0:T(8,128)} %one.1) | copy-start | bytes 884740
  12.6 78.5 %copy-start.2 = (f32[6,1,24,512]{3,2,1,0:T(8,128)S(1)}, f32[6,1,24,512]{3,2,1,0:T(8,128)}, u32[]{:S(2)}) copy-start(f32[6,1,24,512]{3,2,1,0:T(8,128)} %two.1) | copy-start | bytes 884740
  12.6 78.5 %copy-start.3 = (s32[4,6]{1,0:T(4,128)S(1)}, s32[4,6]{1,0:T(4,128)}, u32[]{:S(2)}) copy-start(s32[4,6]{1,0:T(4,128)} %lmap.3) | copy-start | bytes 292
  12.8 7.6 %collective-permute-start.9 = (bf16[2,384,128]{2,1,0:T(8,128)(2,1)S(1)}, bf16[2,384,128]{2,1,0:T(8,128)(2,1)S(1)}, u32[]{:S(2)}, u32[]{:S(2)}) collective-permute-start(bf16[2,384,128]{2,1,0:T(8,128)(2,1)S(1)} %get-tuple-element.30), channel_id=1, source_target_pairs={{0,1},{1,2},{2,3},{3,0},{4,5},{5,6},{6,7},{7,4},{8,9},{9,10},{10,1... | collective-permute-start | bytes 589832 | tf_op jit(solution)/shard_map/cond/branch_1_fun/ppermute | solution.py:339
  15.0 8.4 %collective-permute-start.10 = (bf16[2,384,128]{2,1,0:T(8,128)(2,1)S(1)}, bf16[2,384,128]{2,1,0:T(8,128)(2,1)S(1)}, u32[]{:S(2)}, u32[]{:S(2)}) collective-permute-start(bf16[2,384,128]{2,1,0:T(8,128)(2,1)S(1)} %get-tuple-element.31), channel_id=1, source_target_pairs={{0,2},{1,3},{2,0},{3,1},{4,6},{5,7},{6,4},{7,5},{8,10},{9,11},{10,... | collective-permute-start | bytes 589832 | tf_op jit(solution)/shard_map/cond/branch_1_fun/ppermute | solution.py:339
  17.4 6.0 %collective-permute-start.11 = (bf16[2,384,128]{2,1,0:T(8,128)(2,1)S(1)}, bf16[2,384,128]{2,1,0:T(8,128)(2,1)S(1)}, u32[]{:S(2)}, u32[]{:S(2)}) collective-permute-start(bf16[2,384,128]{2,1,0:T(8,128)(2,1)S(1)} %get-tuple-element.32), channel_id=1, source_target_pairs={{0,3},{1,0},{2,1},{3,2},{4,7},{5,4},{6,5},{7,6},{8,11},{9,8},{10,9... | collective-permute-start | bytes 589832 | tf_op jit(solution)/shard_map/cond/branch_1_fun/ppermute | solution.py:339
  23.5 6.7 %collective-permute-start.14 = (bf16[2,384,128]{2,1,0:T(8,128)(2,1)S(1)}, bf16[2,384,128]{2,1,0:T(8,128)(2,1)S(1)}, u32[]{:S(2)}, u32[]{:S(2)}) collective-permute-start(bf16[2,384,128]{2,1,0:T(8,128)(2,1)S(1)} %add_convert_fusion), channel_id=1, source_target_pairs={{0,3},{1,0},{2,1},{3,2},{4,7},{5,4},{6,5},{7,6},{8,11},{9,8},{10,9... | collective-permute-start | bytes 589832 | tf_op jit(solution)/shard_map/cond/branch_1_fun/ppermute | solution.py:352
  25.5 6.1 %collective-permute-start.13 = (bf16[2,384,128]{2,1,0:T(8,128)(2,1)S(1)}, bf16[2,384,128]{2,1,0:T(8,128)(2,1)S(1)}, u32[]{:S(2)}, u32[]{:S(2)}) collective-permute-start(bf16[2,384,128]{2,1,0:T(8,128)(2,1)S(1)} %add_convert_fusion), channel_id=1, source_target_pairs={{0,2},{1,3},{2,0},{3,1},{4,6},{5,7},{6,4},{7,5},{8,10},{9,11},{10,... | collective-permute-start | bytes 589832 | tf_op jit(solution)/shard_map/cond/branch_1_fun/ppermute | solution.py:352
  25.9 8.9 %collective-permute-start.12 = (bf16[2,384,128]{2,1,0:T(8,128)(2,1)S(1)}, bf16[2,384,128]{2,1,0:T(8,128)(2,1)S(1)}, u32[]{:S(2)}, u32[]{:S(2)}) collective-permute-start(bf16[2,384,128]{2,1,0:T(8,128)(2,1)S(1)} %add_convert_fusion), channel_id=1, source_target_pairs={{0,1},{1,2},{2,3},{3,0},{4,5},{5,6},{6,7},{7,4},{8,9},{9,10},{10,1... | collective-permute-start | bytes 589832 | tf_op jit(solution)/shard_map/cond/branch_1_fun/ppermute | solution.py:352
  34.8 9.6 %collective-permute-start.15 = (bf16[4,384,128]{2,1,0:T(8,128)(2,1)S(1)}, bf16[4,384,128]{2,1,0:T(8,128)(2,1)S(1)}, u32[]{:S(2)}, u32[]{:S(2)}) collective-permute-start(bf16[4,384,128]{2,1,0:T(8,128)(2,1)S(1)} %pad_maximum_fusion.1.refs_0_), channel_id=1, source_target_pairs={{0,4},{1,5},{2,6},{3,7},{4,8},{5,9},{6,10},{7,11},{8,12},{9,13},{1... | collective-permute-start | bytes 1179656 | tf_op jit(solution)/shard_map/cond/branch_1_fun/ppermute | solution.py:352
  38.4 7.0 %collective-permute-start.19 = (bf16[4,384,128]{2,1,0:T(8,128)(2,1)S(1)}, bf16[4,384,128]{2,1,0:T(8,128)(2,1)S(1)}, u32[]{:S(2)}, u32[]{:S(2)}) collective-permute-start(bf16[4,384,128]{2,1,0:T(8,128)(2,1)S(1)} %pad_maximum_fusion.2.refs_4_), channel_id=1, source_target_pairs={{0,12},{1,13},{2,14},{3,15},{4,0},{5,1},{6,2},{7,3},{8,4},{9,5},{1... | collective-permute-start | bytes 1179656 | tf_op jit(solution)/shard_map/cond/branch_1_fun/ppermute | solution.py:352
  39.1 10.2 %collective-permute-start.17 = (bf16[4,384,128]{2,1,0:T(8,128)(2,1)S(1)}, bf16[4,384,128]{2,1,0:T(8,128)(2,1)S(1)}, u32[]{:S(2)}, u32[]{:S(2)}) collective-permute-start(bf16[4,384,128]{2,1,0:T(8,128)(2,1)S(1)} %pad_maximum_fusion.1.refs_0_), channel_id=1, source_target_pairs={{0,12},{1,13},{2,14},{3,15},{4,0},{5,1},{6,2},{7,3},{8,4},{9,5},{1... | collective-permute-start | bytes 1179656 | tf_op jit(solution)/shard_map/cond/branch_1_fun/ppermute | solution.py:352
  40.5 8.7 %collective-permute-start.18 = (bf16[4,384,128]{2,1,0:T(8,128)(2,1)S(1)}, bf16[4,384,128]{2,1,0:T(8,128)(2,1)S(1)}, u32[]{:S(2)}, u32[]{:S(2)}) collective-permute-start(bf16[4,384,128]{2,1,0:T(8,128)(2,1)S(1)} %pad_maximum_fusion.2.refs_4_), channel_id=1, source_target_pairs={{0,4},{1,5},{2,6},{3,7},{4,8},{5,9},{6,10},{7,11},{8,12},{9,13},{1... | collective-permute-start | bytes 1179656 | tf_op jit(solution)/shard_map/cond/branch_1_fun/ppermute | solution.py:352
  44.4 8.2 %collective-permute-start.16 = (bf16[4,384,128]{2,1,0:T(8,128)(2,1)S(1)}, bf16[4,384,128]{2,1,0:T(8,128)(2,1)S(1)}, u32[]{:S(2)}, u32[]{:S(2)}) collective-permute-start(bf16[4,384,128]{2,1,0:T(8,128)(2,1)S(1)} %collective-permute-done.15.refs_1_), channel_id=1, source_target_pairs={{0,4},{1,5},{2,6},{3,7},{4,8},{5,9},{6,10},{7,11},{8,12},{9,13},{1... | collective-permute-start | bytes 1179656 | tf_op jit(solution)/shard_map/cond/branch_1_fun/ppermute | solution.py:352
  45.4 8.1 %collective-permute-start.20 = (bf16[4,384,128]{2,1,0:T(8,128)(2,1)S(1)}, bf16[4,384,128]{2,1,0:T(8,128)(2,1)S(1)}, u32[]{:S(2)}, u32[]{:S(2)}) collective-permute-start(bf16[4,384,128]{2,1,0:T(8,128)(2,1)S(1)} %collective-permute-done.19.refs_7_), channel_id=1, source_target_pairs={{0,12},{1,13},{2,14},{3,15},{4,0},{5,1},{6,2},{7,3},{8,4},{9,5},{1... | collective-permute-start | bytes 1179656 | tf_op jit(solution)/shard_map/cond/branch_1_fun/ppermute | solution.py:352

commit v5 on v4

--- a/solution.py
+++ b/solution.py
@@ -309,11 +309,8 @@
 
 
 def place_kernel(arrived, out, sem):
-    copies = []
-    for i in range(arrived.shape[0]):
-        for j in range(arrived.shape[1]):
-            copies.append(pltpu.make_async_copy(
-                arrived.at[i, j], out.at[j, i], sem.at[len(copies)]))
+    copies = [pltpu.make_async_copy(arrived.at[:, j], out.at[j], sem.at[j])
+              for j in range(out.shape[0])]
     for c in copies:
         c.start()
     for c in copies:
@@ -326,7 +323,7 @@
         place_kernel,
         in_specs=[pl.BlockSpec(memory_space=pl.ANY)],
         out_specs=pl.BlockSpec(memory_space=pl.ANY),
-        scratch_shapes=[pltpu.SemaphoreType.DMA((group * slots,))],
+        scratch_shapes=[pltpu.SemaphoreType.DMA((slots,))],
         out_shape=jax.ShapeDtypeStruct((slots, group, rows, wide), BF),
         compiler_params=pltpu.CompilerParams(vmem_limit_bytes=4 << 20),
         cost_estimate=pl.CostEstimate(flops=0, bytes_accessed=2 << 20, transcendentals=0),
@@ -354,7 +351,7 @@
 
 def across(parts):
     total = parts[0].astype(F32)
-    for k in range(1, 4):
+    for k in (3, 1, 2):
         total = total + shift(parts[k], "x", k).astype(F32)
     return total.astype(BF)
 
@@ -369,11 +366,12 @@
 
     def both_slots():
         block = across(parts)
-        near = [block] + [turn(block, k, True) for k in range(1, 4)]
+        hops = {k: turn(block, k, True) for k in (3, 1, 2)}
+        near = [block] + [hops[k] for k in range(1, 4)]
         low, high = jnp.stack([n[0] for n in near]), jnp.stack([n[1] for n in near])
         low_up, high_down = turn(low, 1, False), turn(high, 3, False)
+        low_far, high_far = turn(low_up, 1, False), turn(high_down, 3, False)
         high_up, low_down = turn(high, 1, False), turn(low, 3, False)
-        low_far, high_far = turn(low_up, 1, False), turn(high_down, 3, False)
         return layer_grads(normed_input, [low, low_up, low_far, low_down],
                            [high, high_up, high_far, high_down], rows)
 

time: 120 us -> 119 us (level)
    ppermute x3, waiting for transfers between devices: 4.8 us -> 6.11 us  [shift(): return lax.ppermute(value, axis, [(i, (i + by) % n) for i in range(n)])]
  transfers between devices with their start and end apart: 12 -> 12, of which waited for: 10 -> 9; matrix products, arithmetic and copies ran while one was open for 0% -> 0% of each run, Pallas kernels for 0% -> 0%
where the time goes in v5:
time: 119 us; the launch traced here: 118 us
  blocking collectives  59.7 us (50%)
  waiting for transfers between devices  24.3 us (20%)
  Pallas kernels  16.3 us (14%)
  starting transfers between devices  16 us (13%)
  between operations  1.54 us (1%)
    all_to_all x1, blocking collectives, body(): arrived = lax.all_to_all(grads, group_axes, 0, 0, tiled=True)  34.1 us
    all_to_all x1, blocking collectives, body(): weights = place(lax.all_to_all(send, group_axes, 0, 0, tiled=True))  25.6 us
    ppermute x9, waiting for transfers between devices, turn(): return lax.ppermute(value, ('core', 'y', 'x'), pairs)  18.2 us
    pallas_call x1, Pallas kernels, attention(): pl.pallas_call(functools.partial(attention_kernel, layers, tokens, per_de...  11.2 us
    ppermute x9, starting transfers between devices, turn(): return lax.ppermute(value, ('core', 'y', 'x'), pairs)  10.9 us
    ppermute x3, waiting for transfers between devices, shift(): return lax.ppermute(value, axis, [(i, (i + by) % n) for i in range(n)])  6.11 us
    ppermute x3, starting transfers between devices, shift(): return lax.ppermute(value, axis, [(i, (i + by) % n) for i in range(n)])  5.12 us
  transfers between devices with their start and end apart: 12, of which 9 were waited for; matrix products, arithmetic and copies ran while one was open for 0% of the time, Pallas kernels for 0%

profile of v5, /device:TPU:1, one launch (start us, length us, event | category | flops | bytes accessed | tf_op | source)
XLA Modules:
  0.0 118.5 jit_solution(2491123922202210176)
XLA Ops:
  0.6 11.2 %attention.1 = (bf16[2,384,128]{2,1,0:T(8,128)(2,1)S(1)}, bf16[2,384,128]{2,1,0:T(8,128)(2,1)S(1)}, bf16[2,384,128]{2,1,0:T(8,128)(2,1)S(1)}, bf16[2,384,128]{2,1,0:T(8,128)(2,1)S(1)}, s32[1]{0:T(128)}) custom-call(s32[4,6]{1,0:T(4,128)} %lmap.3, s32[4]{0:T(128)} %counts.1, s32[6]{0:T(128)} %windows.1, bf16[1,1,2,1536,256]{4,3,2,1,0:T(8,128)(2,1)} %q_ref.1, ...), custom_call_target="tpu_custom_call" | custom-call | flops 2415919104 | bytes 4194304 | tf_op jit(solution)/shard_map/attention/pallas_call | solution.py:158
  12.6 43.2 %conditional.1 = (bf16[16,2,24,512]{3,2,1,0:T(8,128)(2,1)S(1)}) conditional(s32[]{:T(128)} %bitcast.9, (bf16[2,384,128]{2,1,0:T(8,128)(2,1)S(1)}, bf16[2,384,128]{2,1,0:T(8,128)(2,1)S(1)}, bf16[2,384,128]{2,1,0:T(8,128)(2,1)S(1)}, bf16[2,384,128]{2,1,0:T(8,128)(2,1)S(1)}, bf16[1,1,2,1536,384]{4,3,2,1,0:T(8,128)(2,1)S(1)}) %tuple.22, ...), branch_computations={%region_0.0_spmd, %region_1.0_spmd} | conditional | flops 1209925632 | bytes 24576488 | solution.py:384
  12.8 3.4 %collective-permute-start.9 = (bf16[2,384,128]{2,1,0:T(8,128)(2,1)S(1)}, bf16[2,384,128]{2,1,0:T(8,128)(2,1)S(1)}, u32[]{:S(2)}, u32[]{:S(2)}) collective-permute-start(bf16[2,384,128]{2,1,0:T(8,128)(2,1)S(1)} %get-tuple-element.30), channel_id=1, source_target_pairs={{0,3},{1,0},{2,1},{3,2},{4,7},{5,4},{6,5},{7,6},{8,11},{9,8},{10,9... | collective-permute-start | bytes 589832 | tf_op jit(solution)/shard_map/cond/branch_1_fun/ppermute | solution.py:336
  16.2 1.7 %collective-permute-start.11 = (bf16[2,384,128]{2,1,0:T(8,128)(2,1)S(1)}, bf16[2,384,128]{2,1,0:T(8,128)(2,1)S(1)}, u32[]{:S(2)}, u32[]{:S(2)}) collective-permute-start(bf16[2,384,128]{2,1,0:T(8,128)(2,1)S(1)} %get-tuple-element.32), channel_id=1, source_target_pairs={{0,2},{1,3},{2,0},{3,1},{4,6},{5,7},{6,4},{7,5},{8,10},{9,11},{10,... | collective-permute-start | bytes 589832 | tf_op jit(solution)/shard_map/cond/branch_1_fun/ppermute | solution.py:336
  18.0 1.5 %collective-permute-done.9 = bf16[2,384,128]{2,1,0:T(8,128)(2,1)S(1)} collective-permute-done((bf16[2,384,128]{2,1,0:T(8,128)(2,1)S(1)}, bf16[2,384,128]{2,1,0:T(8,128)(2,1)S(1)}, u32[]{:S(2)}, u32[]{:S(2)}) %collective-permute-start.9) | collective-permute-done | bytes 196640 | tf_op jit(solution)/shard_map/cond/branch_1_fun/ppermute | solution.py:336
  19.5 4.6 %collective-permute-done.10 = bf16[2,384,128]{2,1,0:T(8,128)(2,1)S(1)} collective-permute-done((bf16[2,384,128]{2,1,0:T(8,128)(2,1)S(1)}, bf16[2,384,128]{2,1,0:T(8,128)(2,1)S(1)}, u32[]{:S(2)}, u32[]{:S(2)}) %collective-permute-start.10) | collective-permute-done | bytes 196640 | tf_op jit(solution)/shard_map/cond/branch_1_fun/ppermute | solution.py:336
  24.2 2.8 %collective-permute-start.14 = (bf16[2,384,128]{2,1,0:T(8,128)(2,1)S(1)}, bf16[2,384,128]{2,1,0:T(8,128)(2,1)S(1)}, u32[]{:S(2)}, u32[]{:S(2)}) collective-permute-start(bf16[2,384,128]{2,1,0:T(8,128)(2,1)S(1)} %add_convert_fusion), channel_id=1, source_target_pairs={{0,3},{1,0},{2,1},{3,2},{4,7},{5,4},{6,5},{7,6},{8,11},{9,8},{10,9... | collective-permute-start | bytes 589832 | tf_op jit(solution)/shard_map/cond/branch_1_fun/ppermute | solution.py:349
  27.0 0.4 collective-permute-start.13
  27.3 0.7 collective-permute-start.12
  28.0 3.7 %collective-permute-done.14 = bf16[2,384,128]{2,1,0:T(8,128)(2,1)S(1)} collective-permute-done((bf16[2,384,128]{2,1,0:T(8,128)(2,1)S(1)}, bf16[2,384,128]{2,1,0:T(8,128)(2,1)S(1)}, u32[]{:S(2)}, u32[]{:S(2)}) %collective-permute-start.14) | collective-permute-done | bytes 196640 | tf_op jit(solution)/shard_map/cond/branch_1_fun/ppermute | solution.py:349
  31.7 1.4 %collective-permute-done.13 = bf16[2,384,128]{2,1,0:T(8,128)(2,1)S(1)} collective-permute-done((bf16[2,384,128]{2,1,0:T(8,128)(2,1)S(1)}, bf16[2,384,128]{2,1,0:T(8,128)(2,1)S(1)}, u32[]{:S(2)}, u32[]{:S(2)}) %collective-permute-start.13) | collective-permute-done | bytes 196640 | tf_op jit(solution)/shard_map/cond/branch_1_fun/ppermute | solution.py:349
  33.1 4.0 %collective-permute-done.12 = bf16[2,384,128]{2,1,0:T(8,128)(2,1)S(1)} collective-permute-done((bf16[2,384,128]{2,1,0:T(8,128)(2,1)S(1)}, bf16[2,384,128]{2,1,0:T(8,128)(2,1)S(1)}, u32[]{:S(2)}, u32[]{:S(2)}) %collective-permute-start.12) | collective-permute-done | bytes 196640 | tf_op jit(solution)/shard_map/cond/branch_1_fun/ppermute | solution.py:349
  37.3 2.7 %collective-permute-start.19 = (bf16[4,384,128]{2,1,0:T(8,128)(2,1)S(1)}, bf16[4,384,128]{2,1,0:T(8,128)(2,1)S(1)}, u32[]{:S(2)}, u32[]{:S(2)}) collective-permute-start(bf16[4,384,128]{2,1,0:T(8,128)(2,1)S(1)} %pad_maximum_fusion.2.refs_4_), channel_id=1, source_target_pairs={{0,12},{1,13},{2,14},{3,15},{4,0},{5,1},{6,2},{7,3},{8,4},{9,5},{1... | collective-permute-start | bytes 1179656 | tf_op jit(solution)/shard_map/cond/branch_1_fun/ppermute | solution.py:349
  40.1 1.0 collective-permute-start.17
  41.1 0.4 collective-permute-start.18
  41.5 3.9 %collective-permute-done.15.refs_1_ = bf16[4,384,128]{2,1,0:T(8,128)(2,1)S(1)} collective-permute-done((bf16[4,384,128]{2,1,0:T(8,128)(2,1)S(1)}, bf16[4,384,128]{2,1,0:T(8,128)(2,1)S(1)}, u32[]{:S(2)}, u32[]{:S(2)}) %collective-permute-start.15) | collective-permute-done | bytes 393248 | tf_op jit(solution)/shard_map/cond/branch_1_fun/ppermute | solution.py:349
  45.4 2.8 %collective-permute-start.20 = (bf16[4,384,128]{2,1,0:T(8,128)(2,1)S(1)}, bf16[4,384,128]{2,1,0:T(8,128)(2,1)S(1)}, u32[]{:S(2)}, u32[]{:S(2)}) collective-permute-start(bf16[4,384,128]{2,1,0:T(8,128)(2,1)S(1)} %collective-permute-done.19.refs_7_), channel_id=1, source_target_pairs={{0,12},{1,13},{2,14},{3,15},{4,0},{5,1},{6,2},{7,3},{8,4},{9,5},{1... | collective-permute-start | bytes 1179656 | tf_op jit(solution)/shard_map/cond/branch_1_fun/ppermute | solution.py:349
  48.2 0.8 collective-permute-done.17.refs_3_
  49.3 4.2 %collective-permute-done.16.refs_2_ = bf16[4,384,128]{2,1,0:T(8,128)(2,1)S(1)} collective-permute-done((bf16[4,384,128]{2,1,0:T(8,128)(2,1)S(1)}, bf16[4,384,128]{2,1,0:T(8,128)(2,1)S(1)}, u32[]{:S(2)}, u32[]{:S(2)}) %collective-permute-start.16) | collective-permute-done | bytes 393248 | tf_op jit(solution)/shard_map/cond/branch_1_fun/ppermute | solution.py:349
  53.5 2.3 %layer_grads.1 = bf16[16,2,24,512]{3,2,1,0:T(8,128)(2,1)S(1)} custom-call(bf16[1,1,2,1536,384]{4,3,2,1,0:T(8,128)(2,1)S(1)} %get-tuple-element.28.x_ref, bf16[4,384,128]{2,1,0:T(8,128)(2,1)S(1)} %pad_maximum_fusion.1.refs_0_, bf16[4,384,128]{2,1,0:T(8,128)(2,1)S(1)} %collective-permute-done.15.refs_1_, ...), custom_call_target="tpu_custom_call" | custom-call | flops 1207959552 | bytes 6291456 | tf_op jit(solution)/shard_map/cond/branch_1_fun/layer_grads/pallas_call | solution.py:235
  55.8 34.1 %all_to_all.10.arrived = bf16[16,2,24,512]{3,2,1,0:T(8,128)(2,1)S(1)} all-to-all(bf16[16,2,24,512]{3,2,1,0:T(8,128)(2,1)S(1)} %get-tuple-element.63), channel_id=1, replica_groups=mesh['rep'=4,'z'=2,'core'=2,'y'=4,'x'=4] {'rep','z','core'}, dimensions={0} | all-to-all | bytes 1572864 | tf_op jit(solution)/shard_map/all_to_all | solution.py:385
  90.0 1.8 %adamw.1 = (f32[6,1,24,512]{3,2,1,0:T(8,128)}, f32[6,1,24,512]{3,2,1,0:T(8,128)}, f32[6,1,24,512]{3,2,1,0:T(8,128)}, bf16[16,2,24,512]{3,2,1,0:T(8,128)(2,1)S(1)}) custom-call(s32[4,6]{1,0:T(4,128)S(1)} %copy-done.3, bf16[16,2,24,512]{3,2,1,0:T(8,128)(2,1)S(1)} %all_to_all.10.arrived, f32[6,1,24,512]{3,2,1,0:T(8,128)S(1)} %copy-done, ...), custom_call_target="tpu_custom_call" | custom-call | flops 1474560 | bytes 4194304 | tf_op jit(solution)/shard_map/adamw/pallas_call | solution.py:295
  91.8 25.6 %all_to_all.11.arrived = bf16[16,2,24,512]{3,2,1,0:T(8,128)(2,1)S(1)} all-to-all(bf16[16,2,24,512]{3,2,1,0:T(8,128)(2,1)S(1)} %get-tuple-element.54), channel_id=1, replica_groups=mesh['rep'=4,'z'=2,'core'=2,'y'=4,'x'=4] {'rep','z','core'}, dimensions={0} | all-to-all | bytes 1572864 | tf_op jit(solution)/shard_map/all_to_all | solution.py:388
  117.4 0.9 place.1
  (24 shorter events, 0.7 us)
Async XLA Ops:
  0.6 11.9 %copy-start.4 = (bf16[1,1,2,1536,384]{4,3,2,1,0:T(8,128)(2,1)S(1)}, bf16[1,1,2,1536,384]{4,3,2,1,0:T(8,128)(2,1)}, u32[]{:S(2)}) copy-start(bf16[1,1,2,1536,384]{4,3,2,1,0:T(8,128)(2,1)} %param.15) | copy-start | bytes 7077892
  12.6 77.4 %copy-start = (f32[6,1,24,512]{3,2,1,0:T(8,128)S(1)}, f32[6,1,24,512]{3,2,1,0:T(8,128)}, u32[]{:S(2)}) copy-start(f32[6,1,24,512]{3,2,1,0:T(8,128)} %master.1) | copy-start | bytes 884740
  12.6 77.4 %copy-start.1 = (f32[6,1,24,512]{3,2,1,0:T(8,128)S(1)}, f32[6,1,24,512]{3,2,1,0:T(8,128)}, u32[]{:S(2)}) copy-start(f32[6,1,24,512]{3,2,1,0:T(8,128)} %one.1) | copy-start | bytes 884740
  12.6 77.4 %copy-start.2 = (f32[6,1,24,512]{3,2,1,0:T(8,128)S(1)}, f32[6,1,24,512]{3,2,1,0:T(8,128)}, u32[]{:S(2)}) copy-start(f32[6,1,24,512]{3,2,1,0:T(8,128)} %two.1) | copy-start | bytes 884740
  12.6 77.4 %copy-start.3 = (s32[4,6]{1,0:T(4,128)S(1)}, s32[4,6]{1,0:T(4,128)}, u32[]{:S(2)}) copy-start(s32[4,6]{1,0:T(4,128)} %lmap.3) | copy-start | bytes 292
  12.8 6.6 %collective-permute-start.9 = (bf16[2,384,128]{2,1,0:T(8,128)(2,1)S(1)}, bf16[2,384,128]{2,1,0:T(8,128)(2,1)S(1)}, u32[]{:S(2)}, u32[]{:S(2)}) collective-permute-start(bf16[2,384,128]{2,1,0:T(8,128)(2,1)S(1)} %get-tuple-element.30), channel_id=1, source_target_pairs={{0,3},{1,0},{2,1},{3,2},{4,7},{5,4},{6,5},{7,6},{8,11},{9,8},{10,9... | collective-permute-start | bytes 589832 | tf_op jit(solution)/shard_map/cond/branch_1_fun/ppermute | solution.py:336
  16.2 7.8 %collective-permute-start.10 = (bf16[2,384,128]{2,1,0:T(8,128)(2,1)S(1)}, bf16[2,384,128]{2,1,0:T(8,128)(2,1)S(1)}, u32[]{:S(2)}, u32[]{:S(2)}) collective-permute-start(bf16[2,384,128]{2,1,0:T(8,128)(2,1)S(1)} %get-tuple-element.31), channel_id=1, source_target_pairs={{0,1},{1,2},{2,3},{3,0},{4,5},{5,6},{6,7},{7,4},{8,9},{9,10},{10,1... | collective-permute-start | bytes 589832 | tf_op jit(solution)/shard_map/cond/branch_1_fun/ppermute | solution.py:336
  16.2 7.8 %collective-permute-start.11 = (bf16[2,384,128]{2,1,0:T(8,128)(2,1)S(1)}, bf16[2,384,128]{2,1,0:T(8,128)(2,1)S(1)}, u32[]{:S(2)}, u32[]{:S(2)}) collective-permute-start(bf16[2,384,128]{2,1,0:T(8,128)(2,1)S(1)} %get-tuple-element.32), channel_id=1, source_target_pairs={{0,2},{1,3},{2,0},{3,1},{4,6},{5,7},{6,4},{7,5},{8,10},{9,11},{10,... | collective-permute-start | bytes 589832 | tf_op jit(solution)/shard_map/cond/branch_1_fun/ppermute | solution.py:336
  24.2 7.5 %collective-permute-start.14 = (bf16[2,384,128]{2,1,0:T(8,128)(2,1)S(1)}, bf16[2,384,128]{2,1,0:T(8,128)(2,1)S(1)}, u32[]{:S(2)}, u32[]{:S(2)}) collective-permute-start(bf16[2,384,128]{2,1,0:T(8,128)(2,1)S(1)} %add_convert_fusion), channel_id=1, source_target_pairs={{0,3},{1,0},{2,1},{3,2},{4,7},{5,4},{6,5},{7,6},{8,11},{9,8},{10,9... | collective-permute-start | bytes 589832 | tf_op jit(solution)/shard_map/cond/branch_1_fun/ppermute | solution.py:349
  27.0 6.1 %collective-permute-start.13 = (bf16[2,384,128]{2,1,0:T(8,128)(2,1)S(1)}, bf16[2,384,128]{2,1,0:T(8,128)(2,1)S(1)}, u32[]{:S(2)}, u32[]{:S(2)}) collective-permute-start(bf16[2,384,128]{2,1,0:T(8,128)(2,1)S(1)} %add_convert_fusion), channel_id=1, source_target_pairs={{0,2},{1,3},{2,0},{3,1},{4,6},{5,7},{6,4},{7,5},{8,10},{9,11},{10,... | collective-permute-start | bytes 589832 | tf_op jit(solution)/shard_map/cond/branch_1_fun/ppermute | solution.py:349
  27.3 9.8 %collective-permute-start.12 = (bf16[2,384,128]{2,1,0:T(8,128)(2,1)S(1)}, bf16[2,384,128]{2,1,0:T(8,128)(2,1)S(1)}, u32[]{:S(2)}, u32[]{:S(2)}) collective-permute-start(bf16[2,384,128]{2,1,0:T(8,128)(2,1)S(1)} %add_convert_fusion), channel_id=1, source_target_pairs={{0,1},{1,2},{2,3},{3,0},{4,5},{5,6},{6,7},{7,4},{8,9},{9,10},{10,1... | collective-permute-start | bytes 589832 | tf_op jit(solution)/shard_map/cond/branch_1_fun/ppermute | solution.py:349
  37.2 8.2 %collective-permute-start.15 = (bf16[4,384,128]{2,1,0:T(8,128)(2,1)S(1)}, bf16[4,384,128]{2,1,0:T(8,128)(2,1)S(1)}, u32[]{:S(2)}, u32[]{:S(2)}) collective-permute-start(bf16[4,384,128]{2,1,0:T(8,128)(2,1)S(1)} %pad_maximum_fusion.1.refs_0_), channel_id=1, source_target_pairs={{0,4},{1,5},{2,6},{3,7},{4,8},{5,9},{6,10},{7,11},{8,12},{9,13},{1... | collective-permute-start | bytes 1179656 | tf_op jit(solution)/shard_map/cond/branch_1_fun/ppermute | solution.py:349
  37.3 8.1 %collective-permute-start.19 = (bf16[4,384,128]{2,1,0:T(8,128)(2,1)S(1)}, bf16[4,384,128]{2,1,0:T(8,128)(2,1)S(1)}, u32[]{:S(2)}, u32[]{:S(2)}) collective-permute-start(bf16[4,384,128]{2,1,0:T(8,128)(2,1)S(1)} %pad_maximum_fusion.2.refs_4_), channel_id=1, source_target_pairs={{0,12},{1,13},{2,14},{3,15},{4,0},{5,1},{6,2},{7,3},{8,4},{9,5},{1... | collective-permute-start | bytes 1179656 | tf_op jit(solution)/shard_map/cond/branch_1_fun/ppermute | solution.py:349
  40.1 8.9 %collective-permute-start.17 = (bf16[4,384,128]{2,1,0:T(8,128)(2,1)S(1)}, bf16[4,384,128]{2,1,0:T(8,128)(2,1)S(1)}, u32[]{:S(2)}, u32[]{:S(2)}) collective-permute-start(bf16[4,384,128]{2,1,0:T(8,128)(2,1)S(1)} %pad_maximum_fusion.1.refs_0_), channel_id=1, source_target_pairs={{0,12},{1,13},{2,14},{3,15},{4,0},{5,1},{6,2},{7,3},{8,4},{9,5},{1... | collective-permute-start | bytes 1179656 | tf_op jit(solution)/shard_map/cond/branch_1_fun/ppermute | solution.py:349
  41.1 8.2 %collective-permute-start.18 = (bf16[4,384,128]{2,1,0:T(8,128)(2,1)S(1)}, bf16[4,384,128]{2,1,0:T(8,128)(2,1)S(1)}, u32[]{:S(2)}, u32[]{:S(2)}) collective-permute-start(bf16[4,384,128]{2,1,0:T(8,128)(2,1)S(1)} %pad_maximum_fusion.2.refs_4_), channel_id=1, source_target_pairs={{0,4},{1,5},{2,6},{3,7},{4,8},{5,9},{6,10},{7,11},{8,12},{9,13},{1... | collective-permute-start | bytes 1179656 | tf_op jit(solution)/shard_map/cond/branch_1_fun/ppermute | solution.py:349
  45.4 8.1 %collective-permute-start.16 = (bf16[4,384,128]{2,1,0:T(8,128)(2,1)S(1)}, bf16[4,384,128]{2,1,0:T(8,128)(2,1)S(1)}, u32[]{:S(2)}, u32[]{:S(2)}) collective-permute-start(bf16[4,384,128]{2,1,0:T(8,128)(2,1)S(1)} %collective-permute-done.15.refs_1_), channel_id=1, source_target_pairs={{0,4},{1,5},{2,6},{3,7},{4,8},{5,9},{6,10},{7,11},{8,12},{9,13},{1... | collective-permute-start | bytes 1179656 | tf_op jit(solution)/shard_map/cond/branch_1_fun/ppermute | solution.py:349
  45.4 8.1 %collective-permute-start.20 = (bf16[4,384,128]{2,1,0:T(8,128)(2,1)S(1)}, bf16[4,384,128]{2,1,0:T(8,128)(2,1)S(1)}, u32[]{:S(2)}, u32[]{:S(2)}) collective-permute-start(bf16[4,384,128]{2,1,0:T(8,128)(2,1)S(1)} %collective-permute-done.19.refs_7_), channel_id=1, source_target_pairs={{0,12},{1,13},{2,14},{3,15},{4,0},{5,1},{6,2},{7,3},{8,4},{9,5},{1... | collective-permute-start | bytes 1179656 | tf_op jit(solution)/shard_map/cond/branch_1_fun/ppermute | solution.py:349

commit v6 on v5

--- a/solution.py
+++ b/solution.py
@@ -197,8 +197,8 @@
 def grad_kernel(tokens, rows, x_ref, *refs):
     for slot in range(2):
         @pl.when(pl.program_id(0) == slot)
-        def _(pieces=refs[4 * slot:4 * slot + 4]):
-            grad_slot(tokens, rows, x_ref, pieces, *refs[8:])
+        def _(pieces=refs[4 * slot:4 * slot + 4], slot=slot):
+            grad_slot(tokens, rows, x_ref, pieces, refs[8].at[:, slot], *refs[9:])
 
 
 def first_kernel(tokens, rows, x_ref, *refs):
@@ -231,7 +231,7 @@
     slots, tokens, width = normed.shape[2:]
     group = width // rows
     part = tokens // 4
-    out_block = pl.BlockSpec((group, None, rows, KVH * HD), lambda j, *_: (0, j, 0, 0))
+    out_block = pl.BlockSpec(memory_space=pltpu.VMEM)
     return pl.pallas_call(
         functools.partial(grad_kernel, tokens, rows),
         grid_spec=pltpu.PrefetchScalarGridSpec(
@@ -261,13 +261,12 @@
         send[...] = jnp.zeros_like(send)
 
     for i in range(batch):
-        layer = step * batch + i
+        layer = i
         total = None
         places = []
         for r in range(reps):
             section = lmap[r, layer]
-            first, _ = first_and_count(lmap, r, section, layers)
-            slot = layer - first
+            slot = (lmap[r, layer - 1] == section).astype(jnp.int32) if layer else 0
             source = r * sections + section
             places.append((source, slot))
             term = arrived[source, slot].astype(F32)
@@ -288,17 +287,17 @@
 def adam(lmap, arrived, master, one, two):
     layers, _, rows, wide = master.shape
     reps = lmap.shape[0]
-    batch = layers // 2
+    batch = layers
     state = pl.BlockSpec((batch, None, rows, wide), lambda l, *_: (l, 0, 0, 0))
-    whole = pl.BlockSpec(arrived.shape, lambda l, *_: (0, 0, 0, 0))
+    resident = pl.BlockSpec(memory_space=pltpu.VMEM)
     f32 = jax.ShapeDtypeStruct(master.shape, F32)
     return pl.pallas_call(
         functools.partial(adam_kernel, reps, arrived.shape[0] // reps, layers, batch),
         grid_spec=pltpu.PrefetchScalarGridSpec(
             num_scalar_prefetch=1,
             grid=(layers // batch,),
-            in_specs=[whole, state, state, state],
-            out_specs=[state, state, state, whole],
+            in_specs=[resident, state, state, state],
+            out_specs=[state, state, state, resident],
         ),
         out_shape=[f32, f32, f32, jax.ShapeDtypeStruct(arrived.shape, BF)],
         compiler_params=pltpu.CompilerParams(vmem_limit_bytes=16 << 20),

time: 119 us -> 118 us (level)
  blocking collectives: 59.7 us -> 67.3 us
  Pallas kernels: 16.3 us -> 10.7 us
  starting transfers between devices: 16 us -> 13.4 us
    all_to_all x1, blocking collectives: 34.1 us -> 41.7 us  [body(): arrived = lax.all_to_all(grads, group_axes, 0, 0, tiled=True)]
    ppermute x9 -> x6, waiting for transfers between devices: 18.2 us -> 22.6 us  [turn(): return lax.ppermute(value, ('core', 'y', 'x'), pairs)]
    ppermute x3, waiting for transfers between devices: 6.11 us -> 1.74 us  [shift(): return lax.ppermute(value, axis, [(i, (i + by) % n) for i in range(n)])]
    pallas_call x1, Pallas kernels: 11.2 us -> 6.9 us  [attention(): pl.pallas_call(functools.partial(attention_kernel, layers, tokens, per_de...]
    ppermute x9 -> x6, starting transfers between devices: 10.9 us -> 6.76 us  [turn(): return lax.ppermute(value, ('core', 'y', 'x'), pairs)]
    ppermute x3, starting transfers between devices: 5.12 us -> 6.66 us  [shift(): return lax.ppermute(value, axis, [(i, (i + by) % n) for i in range(n)])]
    pallas_call x1, Pallas kernels: 2.3 us -> 1.08 us  [first_grad(): pl.pallas_call(functools.partial(first_kernel, tokens, rows), grid=(1,),...]
  transfers between devices with their start and end apart: 12 -> 9, of which waited for: 9 -> 6; matrix products, arithmetic and copies ran while one was open for 0% -> 0% of each run, Pallas kernels for 0% -> 0%
where the time goes in v6:
time: 118 us
  blocking collectives  67.3 us (57%)
  waiting for transfers between devices  24.4 us (21%)
  starting transfers between devices  13.4 us (11%)
  Pallas kernels  10.7 us (9%)
  between operations  1.54 us (1%)
    all_to_all x1, blocking collectives, body(): arrived = lax.all_to_all(grads, group_axes, 0, 0, tiled=True)  41.7 us
    all_to_all x1, blocking collectives, body(): weights = place(lax.all_to_all(send, group_axes, 0, 0, tiled=True))  25.6 us
    ppermute x6, waiting for transfers between devices, turn(): return lax.ppermute(value, ('core', 'y', 'x'), pairs)  22.6 us
    pallas_call x1, Pallas kernels, attention(): pl.pallas_call(functools.partial(attention_kernel, layers, tokens, per_de...  6.9 us
    ppermute x6, starting transfers between devices, turn(): return lax.ppermute(value, ('core', 'y', 'x'), pairs)  6.76 us
    ppermute x3, starting transfers between devices, shift(): return lax.ppermute(value, axis, [(i, (i + by) % n) for i in range(n)])  6.66 us
  transfers between devices with their start and end apart: 9, of which 6 were waited for; matrix products, arithmetic and copies ran while one was open for 0% of the time, Pallas kernels for 0%

profile of v6, /device:TPU:1, one launch (start us, length us, event | category | flops | bytes accessed | tf_op | source)
XLA Modules:
  0.0 117.7 jit_solution(11721399947959333490)
XLA Ops:
  0.6 6.9 %attention.1 = (bf16[2,384,128]{2,1,0:T(8,128)(2,1)S(1)}, bf16[2,384,128]{2,1,0:T(8,128)(2,1)S(1)}, bf16[2,384,128]{2,1,0:T(8,128)(2,1)S(1)}, bf16[2,384,128]{2,1,0:T(8,128)(2,1)S(1)}, s32[1]{0:T(128)}) custom-call(s32[4,6]{1,0:T(4,128)} %lmap.3, s32[4]{0:T(128)} %counts.1, s32[6]{0:T(128)} %windows.1, bf16[1,1,2,1536,256]{4,3,2,1,0:T(8,128)(2,1)} %q_ref.1, ...), custom_call_target="tpu_custom_call" | custom-call | flops 2415919104 | bytes 4194304 | tf_op jit(solution)/shard_map/attention/pallas_call | solution.py:158
  8.2 0.0 copy-start
  8.3 39.3 %conditional.1 = (bf16[16,2,24,512]{3,2,1,0:T(8,128)(2,1)S(1)}) conditional(s32[]{:T(128)} %bitcast.9, (bf16[2,384,128]{2,1,0:T(8,128)(2,1)S(1)}, bf16[2,384,128]{2,1,0:T(8,128)(2,1)S(1)}, bf16[2,384,128]{2,1,0:T(8,128)(2,1)S(1)}, bf16[2,384,128]{2,1,0:T(8,128)(2,1)S(1)}, bf16[1,1,2,1536,384]{4,3,2,1,0:T(8,128)(2,1)S(1)}) %tuple.22, ...), branch_computations={%region_0.0_spmd, %region_1.0_spmd} | conditional | flops 1209925632 | bytes 24576488 | solution.py:383
  8.3 3.7 %collective-permute-start.2 = (bf16[384,128]{1,0:T(8,128)(2,1)S(1)}, bf16[384,128]{1,0:T(8,128)(2,1)S(1)}, u32[]{:S(2)}, u32[]{:S(2)}) collective-permute-start(bf16[384,128]{1,0:T(8,128)(2,1)S(1)} %slice_bitcast_fusion), channel_id=1, source_target_pairs={{0,2},{1,3},{2,0},{3,1},{4,6},{5,7},{6,4},{7,5},{8,10},{9,11},{10,... | collective-permute-start | bytes 294920 | tf_op jit(solution)/shard_map/cond/branch_0_fun/ppermute | solution.py:335
  12.0 0.4 collective-permute-start.1
  12.3 2.6 %collective-permute-start = (bf16[384,128]{1,0:T(8,128)(2,1)S(1)}, bf16[384,128]{1,0:T(8,128)(2,1)S(1)}, u32[]{:S(2)}, u32[]{:S(2)}) collective-permute-start(bf16[384,128]{1,0:T(8,128)(2,1)S(1)} %slice_bitcast_fusion.2), channel_id=1, source_target_pairs={{0,3},{1,0},{2,1},{3,2},{4,7},{5,4},{6,5},{7,6},{8,11},{9,8},{10,9... | collective-permute-start | bytes 294920 | tf_op jit(solution)/shard_map/cond/branch_0_fun/ppermute | solution.py:335
  15.0 1.7 %collective-permute-done.1 = bf16[384,128]{1,0:T(8,128)(2,1)S(1)} collective-permute-done((bf16[384,128]{1,0:T(8,128)(2,1)S(1)}, bf16[384,128]{1,0:T(8,128)(2,1)S(1)}, u32[]{:S(2)}, u32[]{:S(2)}) %collective-permute-start.1) | collective-permute-done | bytes 98336 | tf_op jit(solution)/shard_map/cond/branch_0_fun/ppermute | solution.py:335
  16.7 0.1 fusion.2
  16.8 2.8 %collective-permute-start.5 = (bf16[384,128]{1,0:T(8,128)(2,1)S(1)}, bf16[384,128]{1,0:T(8,128)(2,1)S(1)}, u32[]{:S(2)}, u32[]{:S(2)}) collective-permute-start(bf16[384,128]{1,0:T(8,128)(2,1)S(1)} %fusion.2), channel_id=1, source_target_pairs={{0,3},{1,0},{2,1},{3,2},{4,7},{5,4},{6,5},{7,6},{8,11},{9,8},{10,9... | collective-permute-start | bytes 294920 | tf_op jit(solution)/shard_map/cond/branch_0_fun/ppermute | solution.py:348
  19.6 0.3 collective-permute-start.4
  19.9 0.7 collective-permute-start.3
  20.6 0.6 collective-permute-done.5
  21.2 3.6 %collective-permute-done.4 = bf16[384,128]{1,0:T(8,128)(2,1)S(1)} collective-permute-done((bf16[384,128]{1,0:T(8,128)(2,1)S(1)}, bf16[384,128]{1,0:T(8,128)(2,1)S(1)}, u32[]{:S(2)}, u32[]{:S(2)}) %collective-permute-start.4) | collective-permute-done | bytes 98336 | tf_op jit(solution)/shard_map/cond/branch_0_fun/ppermute | solution.py:348
  24.8 0.9 collective-permute-done.3
  25.8 0.1 pad_maximum_fusion.refs_0_
  25.8 0.1 collective-permute-start.6
  25.9 2.8 %collective-permute-start.8 = (bf16[4,384,128]{2,1,0:T(8,128)(2,1)S(1)}, bf16[4,384,128]{2,1,0:T(8,128)(2,1)S(1)}, u32[]{:S(2)}, u32[]{:S(2)}) collective-permute-start(bf16[4,384,128]{2,1,0:T(8,128)(2,1)S(1)} %pad_maximum_fusion.refs_0_), channel_id=1, source_target_pairs={{0,12},{1,13},{2,14},{3,15},{4,0},{5,1},{6,2},{7,3},{8,4},{9,5},{1... | collective-permute-start | bytes 1179656 | tf_op jit(solution)/shard_map/cond/branch_0_fun/ppermute | solution.py:348
  28.8 9.3 %collective-permute-done.6.refs_1_ = bf16[4,384,128]{2,1,0:T(8,128)(2,1)S(1)} collective-permute-done((bf16[4,384,128]{2,1,0:T(8,128)(2,1)S(1)}, bf16[4,384,128]{2,1,0:T(8,128)(2,1)S(1)}, u32[]{:S(2)}, u32[]{:S(2)}) %collective-permute-start.6) | collective-permute-done | bytes 393248 | tf_op jit(solution)/shard_map/cond/branch_0_fun/ppermute | solution.py:348
  38.1 8.1 %collective-permute-done.7.refs_2_ = bf16[4,384,128]{2,1,0:T(8,128)(2,1)S(1)} collective-permute-done((bf16[4,384,128]{2,1,0:T(8,128)(2,1)S(1)}, bf16[4,384,128]{2,1,0:T(8,128)(2,1)S(1)}, u32[]{:S(2)}, u32[]{:S(2)}) %collective-permute-start.7) | collective-permute-done | bytes 393248 | tf_op jit(solution)/shard_map/cond/branch_0_fun/ppermute | solution.py:348
  46.2 1.1 first_grad.1
  47.5 41.7 %all_to_all.10.arrived = bf16[16,2,24,512]{3,2,1,0:T(8,128)(2,1)S(1)} all-to-all(bf16[16,2,24,512]{3,2,1,0:T(8,128)(2,1)S(1)} %get-tuple-element.63), channel_id=1, replica_groups=mesh['rep'=4,'z'=2,'core'=2,'y'=4,'x'=4] {'rep','z','core'}, dimensions={0} | all-to-all | bytes 1572864 | tf_op jit(solution)/shard_map/all_to_all | solution.py:384
  89.2 1.8 %adamw.1 = (f32[6,1,24,512]{3,2,1,0:T(8,128)}, f32[6,1,24,512]{3,2,1,0:T(8,128)}, f32[6,1,24,512]{3,2,1,0:T(8,128)}, bf16[16,2,24,512]{3,2,1,0:T(8,128)(2,1)S(1)}) custom-call(s32[4,6]{1,0:T(4,128)S(1)} %copy-done.3, bf16[16,2,24,512]{3,2,1,0:T(8,128)(2,1)S(1)} %all_to_all.10.arrived, f32[6,1,24,512]{3,2,1,0:T(8,128)S(1)} %copy-done, ...), custom_call_target="tpu_custom_call" | custom-call | flops 1474560 | bytes 4194304 | tf_op jit(solution)/shard_map/adamw/pallas_call | solution.py:294
  91.1 25.6 %all_to_all.11.arrived = bf16[16,2,24,512]{3,2,1,0:T(8,128)(2,1)S(1)} all-to-all(bf16[16,2,24,512]{3,2,1,0:T(8,128)(2,1)S(1)} %get-tuple-element.54), channel_id=1, replica_groups=mesh['rep'=4,'z'=2,'core'=2,'y'=4,'x'=4] {'rep','z','core'}, dimensions={0} | all-to-all | bytes 1572864 | tf_op jit(solution)/shard_map/all_to_all | solution.py:387
  116.7 0.9 place.1
  (16 shorter events, 0.1 us)
Async XLA Ops:
  0.6 7.6 %copy-start.4 = (bf16[1,1,2,1536,384]{4,3,2,1,0:T(8,128)(2,1)S(1)}, bf16[1,1,2,1536,384]{4,3,2,1,0:T(8,128)(2,1)}, u32[]{:S(2)}) copy-start(bf16[1,1,2,1536,384]{4,3,2,1,0:T(8,128)(2,1)} %param.15) | copy-start | bytes 7077892
  8.2 81.0 %copy-start = (f32[6,1,24,512]{3,2,1,0:T(8,128)S(1)}, f32[6,1,24,512]{3,2,1,0:T(8,128)}, u32[]{:S(2)}) copy-start(f32[6,1,24,512]{3,2,1,0:T(8,128)} %master.1) | copy-start | bytes 884740
  8.2 81.0 %copy-start.1 = (f32[6,1,24,512]{3,2,1,0:T(8,128)S(1)}, f32[6,1,24,512]{3,2,1,0:T(8,128)}, u32[]{:S(2)}) copy-start(f32[6,1,24,512]{3,2,1,0:T(8,128)} %one.1) | copy-start | bytes 884740
  8.2 81.0 %copy-start.2 = (f32[6,1,24,512]{3,2,1,0:T(8,128)S(1)}, f32[6,1,24,512]{3,2,1,0:T(8,128)}, u32[]{:S(2)}) copy-start(f32[6,1,24,512]{3,2,1,0:T(8,128)} %two.1) | copy-start | bytes 884740
  8.2 81.0 %copy-start.3 = (s32[4,6]{1,0:T(4,128)S(1)}, s32[4,6]{1,0:T(4,128)}, u32[]{:S(2)}) copy-start(s32[4,6]{1,0:T(4,128)} %lmap.3) | copy-start | bytes 292
  8.3 6.7 %collective-permute-start.2 = (bf16[384,128]{1,0:T(8,128)(2,1)S(1)}, bf16[384,128]{1,0:T(8,128)(2,1)S(1)}, u32[]{:S(2)}, u32[]{:S(2)}) collective-permute-start(bf16[384,128]{1,0:T(8,128)(2,1)S(1)} %slice_bitcast_fusion), channel_id=1, source_target_pairs={{0,2},{1,3},{2,0},{3,1},{4,6},{5,7},{6,4},{7,5},{8,10},{9,11},{10,... | collective-permute-start | bytes 294920 | tf_op jit(solution)/shard_map/cond/branch_0_fun/ppermute | solution.py:335
  12.0 4.8 %collective-permute-start.1 = (bf16[384,128]{1,0:T(8,128)(2,1)S(1)}, bf16[384,128]{1,0:T(8,128)(2,1)S(1)}, u32[]{:S(2)}, u32[]{:S(2)}) collective-permute-start(bf16[384,128]{1,0:T(8,128)(2,1)S(1)} %slice_bitcast_fusion.1), channel_id=1, source_target_pairs={{0,1},{1,2},{2,3},{3,0},{4,5},{5,6},{6,7},{7,4},{8,9},{9,10},{10,1... | collective-permute-start | bytes 294920 | tf_op jit(solution)/shard_map/cond/branch_0_fun/ppermute | solution.py:335
  12.3 4.4 %collective-permute-start = (bf16[384,128]{1,0:T(8,128)(2,1)S(1)}, bf16[384,128]{1,0:T(8,128)(2,1)S(1)}, u32[]{:S(2)}, u32[]{:S(2)}) collective-permute-start(bf16[384,128]{1,0:T(8,128)(2,1)S(1)} %slice_bitcast_fusion.2), channel_id=1, source_target_pairs={{0,3},{1,0},{2,1},{3,2},{4,7},{5,4},{6,5},{7,6},{8,11},{9,8},{10,9... | collective-permute-start | bytes 294920 | tf_op jit(solution)/shard_map/cond/branch_0_fun/ppermute | solution.py:335
  16.8 4.4 %collective-permute-start.5 = (bf16[384,128]{1,0:T(8,128)(2,1)S(1)}, bf16[384,128]{1,0:T(8,128)(2,1)S(1)}, u32[]{:S(2)}, u32[]{:S(2)}) collective-permute-start(bf16[384,128]{1,0:T(8,128)(2,1)S(1)} %fusion.2), channel_id=1, source_target_pairs={{0,3},{1,0},{2,1},{3,2},{4,7},{5,4},{6,5},{7,6},{8,11},{9,8},{10,9... | collective-permute-start | bytes 294920 | tf_op jit(solution)/shard_map/cond/branch_0_fun/ppermute | solution.py:348
  19.6 5.3 %collective-permute-start.4 = (bf16[384,128]{1,0:T(8,128)(2,1)S(1)}, bf16[384,128]{1,0:T(8,128)(2,1)S(1)}, u32[]{:S(2)}, u32[]{:S(2)}) collective-permute-start(bf16[384,128]{1,0:T(8,128)(2,1)S(1)} %fusion.2), channel_id=1, source_target_pairs={{0,2},{1,3},{2,0},{3,1},{4,6},{5,7},{6,4},{7,5},{8,10},{9,11},{10,... | collective-permute-start | bytes 294920 | tf_op jit(solution)/shard_map/cond/branch_0_fun/ppermute | solution.py:348
  19.9 5.9 %collective-permute-start.3 = (bf16[384,128]{1,0:T(8,128)(2,1)S(1)}, bf16[384,128]{1,0:T(8,128)(2,1)S(1)}, u32[]{:S(2)}, u32[]{:S(2)}) collective-permute-start(bf16[384,128]{1,0:T(8,128)(2,1)S(1)} %fusion.2), channel_id=1, source_target_pairs={{0,1},{1,2},{2,3},{3,0},{4,5},{5,6},{6,7},{7,4},{8,9},{9,10},{10,1... | collective-permute-start | bytes 294920 | tf_op jit(solution)/shard_map/cond/branch_0_fun/ppermute | solution.py:348
  25.8 12.2 %collective-permute-start.6 = (bf16[4,384,128]{2,1,0:T(8,128)(2,1)S(1)}, bf16[4,384,128]{2,1,0:T(8,128)(2,1)S(1)}, u32[]{:S(2)}, u32[]{:S(2)}) collective-permute-start(bf16[4,384,128]{2,1,0:T(8,128)(2,1)S(1)} %pad_maximum_fusion.refs_0_), channel_id=1, source_target_pairs={{0,4},{1,5},{2,6},{3,7},{4,8},{5,9},{6,10},{7,11},{8,12},{9,13},{1... | collective-permute-start | bytes 1179656 | tf_op jit(solution)/shard_map/cond/branch_0_fun/ppermute | solution.py:348
  25.9 12.2 %collective-permute-start.8 = (bf16[4,384,128]{2,1,0:T(8,128)(2,1)S(1)}, bf16[4,384,128]{2,1,0:T(8,128)(2,1)S(1)}, u32[]{:S(2)}, u32[]{:S(2)}) collective-permute-start(bf16[4,384,128]{2,1,0:T(8,128)(2,1)S(1)} %pad_maximum_fusion.refs_0_), channel_id=1, source_target_pairs={{0,12},{1,13},{2,14},{3,15},{4,0},{5,1},{6,2},{7,3},{8,4},{9,5},{1... | collective-permute-start | bytes 1179656 | tf_op jit(solution)/shard_map/cond/branch_0_fun/ppermute | solution.py:348
  38.1 8.1 %collective-permute-start.7 = (bf16[4,384,128]{2,1,0:T(8,128)(2,1)S(1)}, bf16[4,384,128]{2,1,0:T(8,128)(2,1)S(1)}, u32[]{:S(2)}, u32[]{:S(2)}) collective-permute-start(bf16[4,384,128]{2,1,0:T(8,128)(2,1)S(1)} %collective-permute-done.6.refs_1_), channel_id=1, source_target_pairs={{0,4},{1,5},{2,6},{3,7},{4,8},{5,9},{6,10},{7,11},{8,12},{9,13},{1... | collective-permute-start | bytes 1179656 | tf_op jit(solution)/shard_map/cond/branch_0_fun/ppermute | solution.py:348
